TPU v7x, 32 devices: a whole 2x2x4 slice. The times are simulated.
32 devices in a mesh: space: 4 (over y, core), terms: 8 (over z, x).
Axes of the slice: x: 2, y: 2, z: 4, core: 2. Of those that a mesh axis runs over, the one named last changes fastest.
Arguments:
- forcing: float32 [144, 3, 8, 32, 128], P('terms', None, 'space'), may hold values from -6 to 6
- stencil: float32 [27, 3, 3], replicated, may hold values from -0.12 to 3, as said below
- fields: float32 [5, 8, 32, 128], P(None, 'space'), may hold values from -3 to 3
- coupling: float32 [126, 5], replicated, may hold values from 0.25 to 1
- slot_term: int32 [144], replicated, may hold values from -1 to 125, as said below
Outputs:
- solution: float32 [144, 3, 8, 32, 128], P('terms', None, 'space')
Inputs may be any that keep to these rules, and one draw needn't show every extreme that they name: `slot_term`: device k of terms holds the slots k * 18 to (k + 1) * 18 - 1; of these, the first 1 hold level-0 terms or -1, the next 1 level 1, then 2 level 2, 5 level 3 and 9 level 4. Every term stands in exactly one slot. The central diagonal entries stencil[13, a, a] lie in 2 to 3; every other entry lies in -0.12 to 0.05.
All inputs are finite; a program needn't handle non-finite values.
Results may differ from a plain program's by a relative error of at most 0.00014.
Values sent between devices are 32-bit elements; how exact they have to be, the bound alone decides.
No kernel may reach another device: no remote copies, remote signals or barrier semaphores. Data moves between devices by JAX's collectives and lax.ppermute only.
A program may use at most 128 MiB of HBM per device.

v0:
```python
import math

import jax
import jax.numpy as jnp
import numpy as np
from jax import lax
from jax.sharding import PartitionSpec as P

DIMS = 5
DEGREE = 4
TERMS = 126


def with_halo(cells, sides, width):
    for axis, dim in sides:
        count = lax.axis_size(axis)
        ends = count - 1
        head = lax.slice_in_dim(cells, 0, width, axis=dim)
        tail = lax.slice_in_dim(cells, cells.shape[dim] - width, cells.shape[dim], axis=dim)
        cells = jnp.concatenate(
            [
                lax.ppermute(tail, axis, [(i, (i + 1) % count) for i in range(ends)]),
                cells,
                lax.ppermute(head, axis, [((i + 1) % count, i) for i in range(ends)]),
            ],
            axis=dim,
        )
    return cells


def compositions(total, pieces_left):
    if pieces_left == 1:
        return [[total]]
    result = []
    for leading in range(total, -1, -1):
        for remainder in compositions(total - leading, pieces_left - 1):
            result.append([leading] + remainder)
    return result


def chaos_parents(dimensions, top_degree):
    indices = []
    for level_now in range(top_degree + 1):
        indices.extend(compositions(level_now, dimensions))
    lookup = {}
    for number, vector in enumerate(indices):
        lookup[tuple(vector)] = number
    parents = np.full((len(indices), dimensions), -1, dtype=np.int32)
    for number, vector in enumerate(indices):
        for dimension in range(dimensions):
            if vector[dimension] > 0:
                lowered = list(vector)
                lowered[dimension] -= 1
                parents[number, dimension] = lookup[tuple(lowered)]
    return parents


def shifted(array, offset, axis_dim):
    if offset == 0:
        return array
    length = array.shape[axis_dim]
    zeros_edge = jnp.zeros_like(lax.slice_in_dim(array, 0, 1, axis=axis_dim))
    if offset > 0:
        return jnp.concatenate(
            [lax.slice_in_dim(array, 1, length, axis=axis_dim), zeros_edge], axis=axis_dim
        )
    return jnp.concatenate(
        [zeros_edge, lax.slice_in_dim(array, 0, length - 1, axis=axis_dim)], axis=axis_dim
    )


def apply_stencil(extended, stencil):
    inner_x = extended.shape[2] - 2
    summed = jnp.zeros(extended.shape[:2] + (inner_x,) + extended.shape[3:], jnp.float32)
    for step_y in range(3):
        for step_z in range(3):
            moved_yz = shifted(shifted(extended, step_y - 1, 3), step_z - 1, 4)
            for step_x in range(3):
                window = lax.slice_in_dim(moved_yz, step_x, step_x + inner_x, axis=2)
                block_coef = stencil[9 * step_x + 3 * step_y + step_z]
                summed = summed + jnp.einsum(
                    "ab,sbxyz->saxyz", block_coef, window, precision=lax.Precision.HIGHEST
                )
    return summed


def on_device(forcing, stencil, fields, coupling, slot_term):
    groups = lax.axis_size("terms")
    slot_dev = forcing.shape[0]
    my_group = lax.axis_index("terms")
    parents = chaos_parents(DIMS, DEGREE)
    level_counts = [math.comb(level_now + DIMS - 1, DIMS - 1) for level_now in range(DEGREE + 1)]
    level_caps = [(level_count + groups - 1) // groups for level_count in level_counts]
    level_starts = [sum(level_caps[:level_now]) for level_now in range(DEGREE + 1)]
    all_terms = slot_term.reshape(groups, slot_dev)
    my_terms = lax.dynamic_slice_in_dim(slot_term, my_group * slot_dev, slot_dev)
    pivots = jnp.diagonal(stencil[13])[None, :, None, None, None]
    link_mask = parents[:, :, None] == np.arange(TERMS)[None, None, :]
    link_table = jnp.where(jnp.asarray(link_mask), coupling[:, :, None], 0.0)
    term_range = jnp.arange(TERMS, dtype=jnp.int32)

    def rim_one(field):
        return with_halo(field, (("space", 2),), 1)

    def relax(level_load, need_image):
        first_pass = level_load / pivots
        settled = first_pass + (level_load - apply_stencil(rim_one(first_pass), stencil)) / pivots
        if need_image:
            return (settled, apply_stencil(rim_one(settled), stencil))
        return (settled, None)

    blocks = []
    begin_level = 0
    prev_image = None
    for level_now in range(begin_level, DEGREE + 1):
        level_start = level_starts[level_now]
        level_cap = level_caps[level_now]
        child_ids = my_terms[level_start : level_start + level_cap]
        filled = (child_ids >= 0).astype(jnp.float32)[:, None, None, None, None]
        level_load = forcing[level_start : level_start + level_cap]
        if level_now == 0:
            level_load = level_load * filled
        else:
            prev_start = level_starts[level_now - 1]
            prev_cap = level_caps[level_now - 1]
            parent_ids = all_terms[:, prev_start : prev_start + prev_cap].reshape(-1)
            empty_sum = jnp.zeros((level_cap,) + forcing.shape[1:], jnp.float32)
            piece = lax.all_gather(prev_image, "terms", axis=0, tiled=True)
            fold_row_ids = lax.slice_in_dim(parent_ids, 0, piece.shape[0], axis=0)
            child_hot = (child_ids[:, None] == term_range[None, :]).astype(jnp.float32)
            row_hot = (fold_row_ids[:, None] == term_range[None, :]).astype(jnp.float32)
            mixture = jnp.einsum(
                "cdr,raxyz->cdaxyz",
                jnp.einsum(
                    "ct,tdq,rq->cdr",
                    child_hot,
                    link_table,
                    row_hot,
                    precision=lax.Precision.HIGHEST,
                ),
                piece,
                precision=lax.Precision.HIGHEST,
            )
            contribution = empty_sum + jnp.sum(mixture * fields[None, :, None], axis=1)
            level_load = (level_load - contribution) * filled
        settled, level_image = relax(level_load, level_now < DEGREE)
        blocks.append(settled)
        prev_image = level_image
    return jnp.concatenate(blocks, axis=0)


def solution(mesh):
    return jax.shard_map(
        on_device,
        mesh=mesh,
        in_specs=(
            P("terms", None, "space", None, None),
            P(),
            P(None, "space", None, None),
            P(),
            P(),
        ),
        out_specs=P("terms", None, "space", None, None),
        check_vma=False,
    )
```

profile of v0, /device:TPU:1, one launch (start us, length us, event | category | flops | bytes accessed | tf_op | source)
XLA Modules:
  0.0 547.4 jit_solution(2989498984466199561)
XLA Ops:
  11.6 4.5 collective-permute-start
  33.6 3.6 collective-permute-start.2
  39.7 3.1 collective-permute-done.3
  53.8 27.3 %all_gather.12 = f32[8,3,2,32,128]{4,3,2,1,0:T(8,128)S(1)} all-gather(f32[1,3,2,32,128]{4,3,2,1,0:T(8,128)S(1)} %copy.35), channel_id=1, replica_groups=mesh['space'=4,'terms'=8] {'terms'}, dimensions={0}, use_global_device_ids=true | all-gather | bytes 884736 | tf_op jit(solution)/shard_map/all_gather | solution.py:128
  82.6 7.4 %collective-permute-start.4 = (f32[1,3,1,32,128]{4,1,3,2,0:T(4,128)S(1)}, f32[1,3,1,32,128]{4,1,3,2,0:T(4,128)S(1)}, u32[]{:S(2)}, u32[]{:S(2)}) collective-permute-start(f32[1,3,1,32,128]{4,1,3,2,0:T(4,128)S(1)} %get-tuple-element.120), channel_id=1, source_target_pairs={{0,8},{8,16},{16,24},{1,9},{9,17},{17,25},{2,10},{10,18},{18,26},{... | collective-permute-start | bytes 147464 | tf_op jit(solution)/shard_map/ppermute | solution.py:22
  92.5 3.1 collective-permute-done.5
  125.2 26.6 %all_gather.13 = f32[8,3,2,32,128]{4,3,2,1,0:T(8,128)S(1)} all-gather(f32[1,3,2,32,128]{4,3,2,1,0:T(8,128)S(1)} %copy.41), channel_id=1, replica_groups=mesh['space'=4,'terms'=8] {'terms'}, dimensions={0}, use_global_device_ids=true | all-gather | bytes 884736 | tf_op jit(solution)/shard_map/all_gather | solution.py:128
  154.5 7.5 %collective-permute-start.8 = (f32[2,3,1,32,128]{4,1,3,2,0:T(4,128)S(1)}, f32[2,3,1,32,128]{4,1,3,2,0:T(4,128)S(1)}, u32[]{:S(2)}, u32[]{:S(2)}) collective-permute-start(f32[2,3,1,32,128]{4,1,3,2,0:T(4,128)S(1)} %get-tuple-element.84), channel_id=1, source_target_pairs={{0,8},{8,16},{16,24},{1,9},{9,17},{17,25},{2,10},{10,18},{18,26},{... | collective-permute-start | bytes 294920 | tf_op jit(solution)/shard_map/ppermute | solution.py:22
  164.7 3.6 collective-permute-done.9
  188.7 2.8 collective-permute-start.11
  192.1 2.9 collective-permute-done.11
  215.8 41.2 %all-gather.3.cloned.1.call-done = f32[16,3,2,32,128]{4,3,2,1,0:T(8,128)} async-done(((f32[2,3,2,32,128]{4,3,2,1,0:T(8,128)}), f32[16,3,2,32,128]{4,3,2,1,0:T(8,128)}) %all-gather.3.cloned.1.call-update) | async-done | bytes 1572880 | tf_op jit(solution)/shard_map/all_gather | solution.py:128
  257.0 6.9 %multiply_reduce_fusion.1 = f32[5,3,2,32,128]{4,3,2,1,0:T(8,128)S(1)} fusion(f32[5,2,32,128]{3,0,2,1:T(8,128)S(1)} %copy.37, f32[16,3,2,32,128]{4,3,2,1,0:T(8,128)} %all-gather.3.cloned.1.call-done, f32[5,5,16,1,1,1]{2,0,1,5,4,3:T(8,128)S(1)} %convolution_bitcast_fusion.88), kind=kOutput, calls=%fused_computation.5 | convolution fusion | flops 119070720 | bytes 2229824 | tf_op jit(solution)/shard_map/cdr,raxyz->cdaxyz/dot_general | solution.py:132
  264.7 4.3 collective-permute-start.12
  272.9 4.4 collective-permute-done.13
  325.2 4.4 collective-permute-done.15
  373.0 64.4 %all-gather.5.cloned.1.call-done = f32[40,3,2,32,128]{4,3,2,1,0:T(8,128)} async-done(((f32[5,3,2,32,128]{4,3,2,1,0:T(8,128)}), f32[40,3,2,32,128]{4,3,2,1,0:T(8,128)}) %all-gather.5.cloned.1.call-update) | async-done | bytes 3932176 | tf_op jit(solution)/shard_map/all_gather | solution.py:128
  437.4 13.0 %multiply_reduce_fusion = f32[9,3,2,32,128]{4,3,2,1,0:T(8,128)S(1)} fusion(f32[5,2,32,128]{3,0,2,1:T(8,128)S(1)} %copy.37, f32[40,3,2,32,128]{4,3,2,1,0:T(8,128)} %all-gather.5.cloned.1.call-done, f32[9,5,40,1,1,1]{2,0,1,5,4,3:T(8,128)S(1)} %convolution_bitcast_fusion.87), kind=kOutput, calls=%fused_computation.1 | convolution fusion | flops 532832256 | bytes 4987936 | tf_op jit(solution)/shard_map/cdr,raxyz->cdaxyz/dot_general | solution.py:132
  452.2 4.8 collective-permute-start.16
  462.5 4.1 collective-permute-done.17
  520.5 2.9 fusion.98
  523.5 3.3 fusion.166
  526.8 3.2 fusion.169
  534.6 4.3 fusion.173
  (379 shorter events, 276.2 us)
Async XLA Ops:
  6.5 12.6 %copy-start.6 = (pred[126,5,126]{2,0,1:T(8,128)(4,1)S(1)}, pred[126,5,126]{2,0,1:T(8,128)(4,1)}, u32[]{:S(2)}) copy-start(pred[126,5,126]{2,0,1:T(8,128)(4,1)} %constant.13.clone) | copy-start | bytes 238144
  6.5 12.1 %copy-start.4 = (s32[144]{0:T(256)S(1)}, s32[144]{0:T(256)}, u32[]{:S(2)}) copy-start(s32[144]{0:T(256)} %param.10) | copy-start | bytes 1732
  6.5 12.6 %copy-start.5 = (f32[126,5]{0,1:T(8,128)S(1)}, f32[126,5]{0,1:T(8,128)}, u32[]{:S(2)}) copy-start(f32[126,5]{0,1:T(8,128)} %param.9) | copy-start | bytes 7564
  6.5 250.4 %all-gather.3.cloned.1.call-start = ((), (), s32[]{:S(2)}) async-start(), calls=%async_computation | async-start | bytes 1769472 | tf_op jit(solution)/shard_map/all_gather | solution.py:128
  10.8 11.7 %copy-start.3 = (f32[5,2,32,128]{3,2,1,0:T(8,128)S(1)}, f32[5,2,32,128]{3,2,1,0:T(8,128)}, u32[]{:S(2)}) copy-start(f32[5,2,32,128]{3,2,1,0:T(8,128)} %param.8) | copy-start | bytes 491524
  11.6 11.0 %collective-permute-start = (f32[1,3,1,32,128]{4,1,3,2,0:T(4,128)S(1)}, f32[1,3,1,32,128]{4,1,3,2,0:T(4,128)S(1)}, u32[]{:S(2)}, u32[]{:S(2)}) collective-permute-start(f32[1,3,1,32,128]{4,1,3,2,0:T(4,128)S(1)} %get-tuple-element.124), channel_id=1, source_target_pairs={{0,8},{8,16},{16,24},{1,9},{9,17},{17,25},{2,10},{10,18},{18,26},{... | collective-permute-start | bytes 147464 | tf_op jit(solution)/shard_map/ppermute | solution.py:22
  16.1 6.5 %collective-permute-start.1 = (f32[1,3,1,32,128]{4,1,3,2,0:T(4,128)S(1)}, f32[1,3,1,32,128]{4,1,3,2,0:T(4,128)S(1)}, u32[]{:S(2)}, u32[]{:S(2)}) collective-permute-start(f32[1,3,1,32,128]{4,1,3,2,0:T(4,128)S(1)} %get-tuple-element.125), channel_id=1, source_target_pairs={{8,0},{16,8},{24,16},{9,1},{17,9},{25,17},{10,2},{18,10},{26,18},{... | collective-permute-start | bytes 147464 | tf_op jit(solution)/shard_map/ppermute | solution.py:24
  33.6 6.1 %collective-permute-start.2 = (f32[1,3,1,32,128]{4,1,3,2,0:T(4,128)S(1)}, f32[1,3,1,32,128]{4,1,3,2,0:T(4,128)S(1)}, u32[]{:S(2)}, u32[]{:S(2)}) collective-permute-start(f32[1,3,1,32,128]{4,1,3,2,0:T(4,128)S(1)} %get-tuple-element.122), channel_id=1, source_target_pairs={{0,8},{8,16},{16,24},{1,9},{9,17},{17,25},{2,10},{10,18},{18,26},{... | collective-permute-start | bytes 147464 | tf_op jit(solution)/shard_map/ppermute | solution.py:22
  37.3 5.6 %collective-permute-start.3 = (f32[1,3,1,32,128]{4,1,3,2,0:T(4,128)S(1)}, f32[1,3,1,32,128]{4,1,3,2,0:T(4,128)S(1)}, u32[]{:S(2)}, u32[]{:S(2)}) collective-permute-start(f32[1,3,1,32,128]{4,1,3,2,0:T(4,128)S(1)} %get-tuple-element.123), channel_id=1, source_target_pairs={{8,0},{16,8},{24,16},{9,1},{17,9},{25,17},{10,2},{18,10},{26,18},{... | collective-permute-start | bytes 147464 | tf_op jit(solution)/shard_map/ppermute | solution.py:24
  82.6 9.9 %collective-permute-start.4 = (f32[1,3,1,32,128]{4,1,3,2,0:T(4,128)S(1)}, f32[1,3,1,32,128]{4,1,3,2,0:T(4,128)S(1)}, u32[]{:S(2)}, u32[]{:S(2)}) collective-permute-start(f32[1,3,1,32,128]{4,1,3,2,0:T(4,128)S(1)} %get-tuple-element.120), channel_id=1, source_target_pairs={{0,8},{8,16},{16,24},{1,9},{9,17},{17,25},{2,10},{10,18},{18,26},{... | collective-permute-start | bytes 147464 | tf_op jit(solution)/shard_map/ppermute | solution.py:22
  90.0 5.6 %collective-permute-start.5 = (f32[1,3,1,32,128]{4,1,3,2,0:T(4,128)S(1)}, f32[1,3,1,32,128]{4,1,3,2,0:T(4,128)S(1)}, u32[]{:S(2)}, u32[]{:S(2)}) collective-permute-start(f32[1,3,1,32,128]{4,1,3,2,0:T(4,128)S(1)} %get-tuple-element.121), channel_id=1, source_target_pairs={{8,0},{16,8},{24,16},{9,1},{17,9},{25,17},{10,2},{18,10},{26,18},{... | collective-permute-start | bytes 147464 | tf_op jit(solution)/shard_map/ppermute | solution.py:24
  106.8 5.1 collective-permute-start.6
  108.7 5.6 %collective-permute-start.7 = (f32[1,3,1,32,128]{4,1,3,2,0:T(4,128)S(1)}, f32[1,3,1,32,128]{4,1,3,2,0:T(4,128)S(1)}, u32[]{:S(2)}, u32[]{:S(2)}) collective-permute-start(f32[1,3,1,32,128]{4,1,3,2,0:T(4,128)S(1)} %get-tuple-element.119), channel_id=1, source_target_pairs={{8,0},{16,8},{24,16},{9,1},{17,9},{25,17},{10,2},{18,10},{26,18},{... | collective-permute-start | bytes 147464 | tf_op jit(solution)/shard_map/ppermute | solution.py:24
  154.5 10.1 %collective-permute-start.8 = (f32[2,3,1,32,128]{4,1,3,2,0:T(4,128)S(1)}, f32[2,3,1,32,128]{4,1,3,2,0:T(4,128)S(1)}, u32[]{:S(2)}, u32[]{:S(2)}) collective-permute-start(f32[2,3,1,32,128]{4,1,3,2,0:T(4,128)S(1)} %get-tuple-element.84), channel_id=1, source_target_pairs={{0,8},{8,16},{16,24},{1,9},{9,17},{17,25},{2,10},{10,18},{18,26},{... | collective-permute-start | bytes 294920 | tf_op jit(solution)/shard_map/ppermute | solution.py:22
  162.0 6.3 %collective-permute-start.9 = (f32[2,3,1,32,128]{4,1,3,2,0:T(4,128)S(1)}, f32[2,3,1,32,128]{4,1,3,2,0:T(4,128)S(1)}, u32[]{:S(2)}, u32[]{:S(2)}) collective-permute-start(f32[2,3,1,32,128]{4,1,3,2,0:T(4,128)S(1)} %get-tuple-element.85), channel_id=1, source_target_pairs={{8,0},{16,8},{24,16},{9,1},{17,9},{25,17},{10,2},{18,10},{26,18},{... | collective-permute-start | bytes 294920 | tf_op jit(solution)/shard_map/ppermute | solution.py:24
  186.8 5.3 collective-permute-start.10
  188.7 6.3 %collective-permute-start.11 = (f32[2,3,1,32,128]{4,1,3,2,0:T(4,128)S(1)}, f32[2,3,1,32,128]{4,1,3,2,0:T(4,128)S(1)}, u32[]{:S(2)}, u32[]{:S(2)}) collective-permute-start(f32[2,3,1,32,128]{4,1,3,2,0:T(4,128)S(1)} %get-tuple-element.83), channel_id=1, source_target_pairs={{8,0},{16,8},{24,16},{9,1},{17,9},{25,17},{10,2},{18,10},{26,18},{... | collective-permute-start | bytes 294920 | tf_op jit(solution)/shard_map/ppermute | solution.py:24
  213.8 223.6 %all-gather.5.cloned.1.call-start = ((), (), s32[]{:S(2)}) async-start(), calls=%async_computation.1 | async-start | bytes 4423680 | tf_op jit(solution)/shard_map/all_gather | solution.py:128
  264.7 8.3 %collective-permute-start.12 = (f32[5,3,1,32,128]{4,1,3,2,0:T(4,128)S(1)}, f32[5,3,1,32,128]{4,1,3,2,0:T(4,128)S(1)}, u32[]{:S(2)}, u32[]{:S(2)}) collective-permute-start(f32[5,3,1,32,128]{4,1,3,2,0:T(4,128)S(1)} %get-tuple-element.64), channel_id=1, source_target_pairs={{0,8},{8,16},{16,24},{1,9},{9,17},{17,25},{2,10},{10,18},{18,26},{... | collective-permute-start | bytes 737288 | tf_op jit(solution)/shard_map/ppermute | solution.py:22
  269.0 8.4 %collective-permute-start.13 = (f32[5,3,1,32,128]{4,1,3,2,0:T(4,128)S(1)}, f32[5,3,1,32,128]{4,1,3,2,0:T(4,128)S(1)}, u32[]{:S(2)}, u32[]{:S(2)}) collective-permute-start(f32[5,3,1,32,128]{4,1,3,2,0:T(4,128)S(1)} %get-tuple-element.65), channel_id=1, source_target_pairs={{8,0},{16,8},{24,16},{9,1},{17,9},{25,17},{10,2},{18,10},{26,18},{... | collective-permute-start | bytes 737288 | tf_op jit(solution)/shard_map/ppermute | solution.py:24
  319.3 5.9 %collective-permute-start.14 = (f32[5,3,1,32,128]{4,1,3,2,0:T(4,128)S(1)}, f32[5,3,1,32,128]{4,1,3,2,0:T(4,128)S(1)}, u32[]{:S(2)}, u32[]{:S(2)}) collective-permute-start(f32[5,3,1,32,128]{4,1,3,2,0:T(4,128)S(1)} %get-tuple-element.62), channel_id=1, source_target_pairs={{0,8},{8,16},{16,24},{1,9},{9,17},{17,25},{2,10},{10,18},{18,26},{... | collective-permute-start | bytes 737288 | tf_op jit(solution)/shard_map/ppermute | solution.py:22
  321.2 8.4 %collective-permute-start.15 = (f32[5,3,1,32,128]{4,1,3,2,0:T(4,128)S(1)}, f32[5,3,1,32,128]{4,1,3,2,0:T(4,128)S(1)}, u32[]{:S(2)}, u32[]{:S(2)}) collective-permute-start(f32[5,3,1,32,128]{4,1,3,2,0:T(4,128)S(1)} %get-tuple-element.63), channel_id=1, source_target_pairs={{8,0},{16,8},{24,16},{9,1},{17,9},{25,17},{10,2},{18,10},{26,18},{... | collective-permute-start | bytes 737288 | tf_op jit(solution)/shard_map/ppermute | solution.py:24
  452.2 10.0 %collective-permute-start.16 = (f32[9,3,1,32,128]{4,3,2,1,0:T(8,128)S(1)}, f32[9,3,1,32,128]{4,3,2,1,0:T(8,128)S(1)}, u32[]{:S(2)}, u32[]{:S(2)}) collective-permute-start(f32[9,3,1,32,128]{4,3,2,1,0:T(8,128)S(1)} %copy.57), channel_id=1, source_target_pairs={{0,8},{8,16},{16,24},{1,9},{9,17},{17,25},{2,10},{10,18},{18,26},{... | collective-permute-start | bytes 1327112 | tf_op jit(solution)/shard_map/ppermute | solution.py:22
  457.0 9.6 %collective-permute-start.17 = (f32[9,3,1,32,128]{4,3,2,1,0:T(8,128)S(1)}, f32[9,3,1,32,128]{4,3,2,1,0:T(8,128)S(1)}, u32[]{:S(2)}, u32[]{:S(2)}) collective-permute-start(f32[9,3,1,32,128]{4,3,2,1,0:T(8,128)S(1)} %copy.58), channel_id=1, source_target_pairs={{8,0},{16,8},{24,16},{9,1},{17,9},{25,17},{10,2},{18,10},{26,18},{... | collective-permute-start | bytes 1327112 | tf_op jit(solution)/shard_map/ppermute | solution.py:24
  (3 other events, 19.5 us)
Sparse Core Ops, SparseCore 0:
  213.9 42.9 all-gather.2
  371.0 66.3 all-gather.4
where the time goes:
time: 556 us; the launch traced here: 547 us
  matrix products  247 us (44%)
  waiting for transfers between devices  136 us (24%)
  starting transfers between devices  58.4 us (11%)
  blocking collectives  53.9 us (10%)
  local copies, waits for them, and re-layouts  30.1 us (5%)
  between operations  17.5 us (3%)
    dot_general x243, matrix products, apply_stencil(): jnp.einsum('ab,sbxyz->saxyz', block_coef, window, precision=lax.Precision...  221 us
    all_gather x2, waiting for transfers between devices, on_device(): piece = lax.all_gather(prev_image, 'terms', axis=0, tiled=True)  106 us
    all_gather x2, blocking collectives, on_device(): piece = lax.all_gather(prev_image, 'terms', axis=0, tiled=True)  53.9 us
    ppermute x9, starting transfers between devices, with_halo(): lax.ppermute(tail, axis, [(i, (i + 1) % count) for i in range(ends)])  37.8 us
    ppermute x9, waiting for transfers between devices, with_halo(): lax.ppermute(head, axis, [((i + 1) % count, i) for i in range(ends)])  28 us
    dot_general x4, matrix products, on_device(): jnp.einsum('cdr,raxyz->cdaxyz', jnp.einsum('ct,tdq,rq->cdr', child_hot, l...  23.5 us
    ppermute x9, starting transfers between devices, with_halo(): lax.ppermute(head, axis, [((i + 1) % count, i) for i in range(ends)])  20.5 us
    slice x32, local copies, waits for them, and re-layouts, shifted(): lax.slice_in_dim(array, 0, length - 1, axis=axis_dim)  16.6 us
  transfers between devices with their start and end apart: 20, of which 13 were waited for; matrix products, arithmetic and copies ran while one was open for 3% of the time, Pallas kernels for 0%

commit v1 on v0

v1 whole, which is shorter than its diff:
```python
import functools
import math

import jax
import jax.numpy as jnp
import numpy as np
from jax import lax
from jax.experimental import pallas as pl
from jax.experimental.pallas import tpu as pltpu
from jax.sharding import PartitionSpec as P

DIMS = 5
DEGREE = 4
F32 = jnp.float32
BF16 = jnp.bfloat16
VMEM = pl.BlockSpec(memory_space=pltpu.VMEM)
SMEM = pl.BlockSpec(memory_space=pltpu.SMEM)
PARAMS = pltpu.CompilerParams(vmem_limit_bytes=56 * 2**20)


def compositions(total, pieces_left):
    if pieces_left == 1:
        return [[total]]
    result = []
    for leading in range(total, -1, -1):
        for remainder in compositions(total - leading, pieces_left - 1):
            result.append([leading] + remainder)
    return result


def chaos_links():
    indices = []
    for level in range(DEGREE + 1):
        indices.extend(compositions(level, DIMS))
    lookup = {tuple(vector): number for number, vector in enumerate(indices)}
    dims = np.zeros((len(indices), DEGREE), np.int32)
    parents = np.full((len(indices), DEGREE), -1, np.int32)
    for number, vector in enumerate(indices):
        place = 0
        for dim in range(DIMS):
            if vector[dim] > 0:
                lowered = list(vector)
                lowered[dim] -= 1
                dims[number, place] = dim
                parents[number, place] = lookup[tuple(lowered)]
                place += 1
    return dims, parents


LINK_DIMS, LINK_PARENTS = chaos_links()
COUNTS = [math.comb(level + DIMS - 1, DIMS - 1) for level in range(DEGREE + 1)]
FIRSTS = [sum(COUNTS[:level]) for level in range(DEGREE + 1)]


def stencil_matrix(stencil, rows):
    taps = stencil.reshape(3, 3, 3, 3, 3)
    place = np.arange(rows)
    total = 0.0
    for step in range(3):
        band = jnp.asarray((place[None, :] == place[:, None] + step - 1).astype(np.float32))
        part = jnp.transpose(taps[:, step], (1, 2, 0, 3))
        total = total + part[:, :, None, :, :, None] * band[None, None, :, None, None, :]
    return total.reshape(9 * rows, 9 * rows)


def split_matrix(matrix_ref, packed_ref):
    size = matrix_ref.shape[1]
    high = matrix_ref[...].astype(BF16)
    packed_ref[:, :size] = high
    packed_ref[:, size : 2 * size] = high
    packed_ref[:, 2 * size :] = (matrix_ref[...] - high.astype(F32)).astype(BF16)


def put_split(value, high_ref, low_ref, place):
    high = value.astype(BF16)
    high_ref[place] = high
    low_ref[place] = (value - high.astype(F32)).astype(BF16)


def apply_pair(high_ref, low_ref, packed_ref, place):
    def window(ref):
        return [jnp.concatenate([ref[place + k], ref[place + k + 1]], axis=1) for k in range(3)]

    high = window(high_ref)
    operand = jnp.concatenate(high + window(low_ref) + high, axis=0)
    product = jnp.dot(packed_ref[...], operand, preferred_element_type=F32)
    lanes = high_ref.shape[2]
    size = high_ref.shape[1]
    lane = lax.broadcasted_iota(jnp.int32, (size, lanes), 1)
    results = []
    for half in range(2):
        block = product[:, half * lanes : (half + 1) * lanes]
        before = pltpu.roll(block[:size], 1, 1)
        after = pltpu.roll(block[2 * size :], lanes - 1, 1)
        results.append(block[size : 2 * size] + jnp.where(lane > 0, before, 0.0) + jnp.where(lane < lanes - 1, after, 0.0))
    return results


def inverse_pivots(inverse_ref, rows, lanes):
    return jnp.concatenate([jnp.full((rows, lanes), inverse_ref[a], F32) for a in range(3)], axis=0)


def sweep_kernel(terms, edge_ref, inverse_ref, matrix_ref, load_ref, even_ref, odd_ref, settled_ref, image_ref, packed, high, low, high2, low2):
    rows, lanes = load_ref.shape[3:]
    size = 3 * rows
    split_matrix(matrix_ref, packed)
    inverse = inverse_pivots(inverse_ref, rows, lanes)
    is_even = edge_ref[0] > 0.5
    has_lower = edge_ref[1]
    has_upper = edge_ref[2]

    def layer(ref, term, x):
        return ref[term, :, x].reshape(size, lanes)

    def one(term, carry):
        def load(x):
            if 2 <= x < 4:
                return layer(load_ref, term, x - 2)
            if x < 2:
                return jnp.where(is_even, layer(odd_ref, term, x), layer(even_ref, term, x))
            return jnp.where(is_even, layer(even_ref, term, x - 4), layer(odd_ref, term, x - 4))

        for x in range(6):
            put_split(load(x) * inverse, high, low, x)
        for pair in range(2):
            applied = apply_pair(high, low, packed, 2 * pair)
            for half in range(2):
                x = 2 * pair + half + 1
                load_x = load(x)
                settled = load_x * inverse + (load_x - applied[half]) * inverse
                if x == 1:
                    settled = settled * has_lower
                if x == 4:
                    settled = settled * has_upper
                if 2 <= x < 4:
                    settled_ref[term, :, x - 2] = settled.reshape(3, rows, lanes)
                put_split(settled, high2, low2, x - 1)
        applied = apply_pair(high2, low2, packed, 0)
        for half in range(2):
            image_ref[term, :, half] = applied[half].reshape(3, rows, lanes)
        return carry

    lax.fori_loop(0, terms, one, 0)


def last_kernel(terms, edge_ref, inverse_ref, matrix_ref, load_ref, even_ref, odd_ref, settled_ref, packed, high, low):
    rows, lanes = load_ref.shape[3:]
    size = 3 * rows
    split_matrix(matrix_ref, packed)
    inverse = inverse_pivots(inverse_ref, rows, lanes)
    is_even = edge_ref[0] > 0.5

    def one(term, carry):
        even = even_ref[term, :, 0].reshape(size, lanes)
        odd = odd_ref[term, :, 0].reshape(size, lanes)
        put_split(jnp.where(is_even, odd, even) * inverse, high, low, 0)
        put_split(jnp.where(is_even, even, odd) * inverse, high, low, 3)
        for x in range(2):
            put_split(load_ref[term, :, x].reshape(size, lanes) * inverse, high, low, x + 1)
        applied = apply_pair(high, low, packed, 0)
        for x in range(2):
            load = load_ref[term, :, x].reshape(size, lanes)
            settled = load * inverse + (load - applied[x]) * inverse
            settled_ref[term, :, x] = settled.reshape(3, rows, lanes)
        return carry

    lax.fori_loop(0, terms, one, 0)


def load_kernel(terms, cap, blocks, slot_ref, dim_ref, block_ref, row_ref, weight_ref, forcing_ref, fields_ref, *refs):
    image_refs = refs[:blocks]
    load_ref, images = refs[blocks:]
    for block in range(blocks):
        images[block * cap : (block + 1) * cap] = image_refs[block][...]

    def one(term, carry):
        total = forcing_ref[slot_ref[term]] * weight_ref[term, DEGREE]
        for link in range(DEGREE):
            place = block_ref[term, link] * cap + row_ref[term, link]
            field = fields_ref[dim_ref[term, link]] * weight_ref[term, link]
            total = total - field[None] * images[place]
        load_ref[term] = total
        return carry

    lax.fori_loop(0, terms, one, 0)


def run_sweep(load, even, odd, edge, inverse, matrix):
    terms, _, _, rows, lanes = load.shape
    size = 3 * rows
    out = jax.ShapeDtypeStruct(load.shape, F32)
    return pl.pallas_call(
        functools.partial(sweep_kernel, terms),
        out_shape=[out, out],
        in_specs=[SMEM, SMEM] + [VMEM] * 4,
        out_specs=[VMEM, VMEM],
        scratch_shapes=[pltpu.VMEM((3 * size, 9 * size), BF16)]
        + [pltpu.VMEM((6, size, lanes), BF16)] * 2
        + [pltpu.VMEM((4, size, lanes), BF16)] * 2,
        compiler_params=PARAMS,
        cost_estimate=pl.CostEstimate(flops=2 * 3 * terms * 27 * size * size * 256, bytes_accessed=20 * load.size, transcendentals=0),
        name="sweep",
    )(edge, inverse, matrix, load, even, odd)


def run_last(load, even, odd, edge, inverse, matrix):
    terms, _, _, rows, lanes = load.shape
    size = 3 * rows
    return pl.pallas_call(
        functools.partial(last_kernel, terms),
        out_shape=jax.ShapeDtypeStruct(load.shape, F32),
        in_specs=[SMEM, SMEM] + [VMEM] * 4,
        out_specs=VMEM,
        scratch_shapes=[pltpu.VMEM((3 * size, 9 * size), BF16)] + [pltpu.VMEM((4, size, lanes), BF16)] * 2,
        compiler_params=PARAMS,
        cost_estimate=pl.CostEstimate(flops=2 * terms * 27 * size * size * 256, bytes_accessed=12 * load.size, transcendentals=0),
        name="last_sweep",
    )(edge, inverse, matrix, load, even, odd)


def run_load(terms, slots, links, weights, forcing, fields, images):
    cap = images[0].shape[0]
    blocks = len(images)
    return pl.pallas_call(
        functools.partial(load_kernel, terms, cap, blocks),
        out_shape=jax.ShapeDtypeStruct((terms,) + forcing.shape[1:], F32),
        in_specs=[SMEM] * 5 + [VMEM] * (2 + blocks),
        out_specs=VMEM,
        scratch_shapes=[pltpu.VMEM((cap * blocks,) + forcing.shape[1:], F32)],
        compiler_params=PARAMS,
        cost_estimate=pl.CostEstimate(flops=12 * terms * forcing[0].size, bytes_accessed=4 * cap * blocks * forcing[0].size, transcendentals=0),
        name="loads",
    )(slots, *links, weights, forcing, fields, *images)


def beside(array, axis, stride):
    count = lax.axis_size(axis)
    even = [(i, i ^ 1) for i in range(count)]
    odd = [(i, ((i + 1) ^ 1) - 1) for i in range(1, count - 1)]
    return lax.ppermute(array[0], axis, even), lax.ppermute(array[1], axis, odd)


def gather_blocks(block, index):
    count = lax.axis_size("terms")
    if count != 8:
        whole = lax.all_gather(block, "terms", axis=0, tiled=False)
        return [whole[i] for i in range(count)], jnp.arange(count, dtype=jnp.int32)

    def columns(pairs):
        return [(2 * i + x, 2 * j + x) for i, j in pairs for x in range(2)]

    ends = columns([(0, 1), (1, 0), (2, 3), (3, 2)])
    middle = columns([(1, 2), (2, 1)])
    outward = columns([(1, 0), (2, 3)])
    across = [(i, i ^ 1) for i in range(8)]

    def send(array, pairs):
        return lax.ppermute(array, "terms", pairs)

    near = send(block, ends)
    middle_one = send(block, middle)
    second = middle_one + send(middle_one, outward)
    middle_two = send(near, middle)
    third = middle_two + send(middle_two, outward)
    own = [block, near, second, third]
    order = np.array([[0, 1, 2, 3], [1, 0, 2, 3], [3, 2, 0, 1], [3, 2, 1, 0]], np.int32)
    place = jnp.asarray(order)[index // 2]
    places = [place[source // 2] + 4 * ((index ^ source) & 1) for source in range(8)]
    return own + [send(array, across) for array in own], jnp.stack(places).astype(jnp.int32)


def on_device(forcing, stencil, fields, coupling, slot_term):
    groups = lax.axis_size("terms")
    slabs = lax.axis_size("space")
    slot_dev = forcing.shape[0]
    group = lax.axis_index("terms")
    slab = lax.axis_index("space")
    caps = [(count + groups - 1) // groups for count in COUNTS]
    starts = [sum(caps[:level]) for level in range(DEGREE + 1)]
    rows = forcing.shape[3]

    matrix = stencil_matrix(stencil, rows)
    inverse = 1.0 / jnp.diagonal(stencil[13])
    is_even = slab % 2 == 0
    edge = jnp.stack([is_even, slab > 0, slab < slabs - 1]).astype(F32)
    table = slot_term.reshape(groups, slot_dev)
    mine = lax.dynamic_index_in_dim(table, group, 0, keepdims=False)
    slot_of = jnp.sum(
        jnp.where(slot_term[None, :] == jnp.arange(126, dtype=jnp.int32)[:, None], jnp.arange(slot_term.shape[0], dtype=jnp.int32)[None, :], 0),
        axis=1,
    ).astype(jnp.int32)
    dims = jnp.asarray(LINK_DIMS)
    parents = jnp.asarray(np.maximum(LINK_PARENTS, 0))
    weights = jnp.where(jnp.asarray(LINK_PARENTS >= 0), jnp.take_along_axis(coupling, dims, axis=1), 0.0)
    weights = jnp.concatenate([weights, jnp.ones((126, 1), F32)], axis=1)

    def level_slots(level):
        return forcing[starts[level] : starts[level] + caps[level]]

    def slot_tables(level):
        ids = mine[starts[level] : starts[level] + caps[level]]
        filled = ids >= 0
        safe = jnp.maximum(ids, 0)
        weight = weights[safe] * filled.astype(F32)[:, None]
        return safe, weight, filled

    filled0 = (mine[:1] >= 0).astype(F32)[:, None, None, None, None]
    load0 = level_slots(0) * filled0
    strides = [1 << bit for bit in range(groups.bit_length() - 1)]
    strides = strides[1:] + strides[:1]
    for stride in strides:
        load0 = load0 + lax.ppermute(load0, "terms", [(i, i ^ stride) for i in range(groups)])
    gathered, offsets = level_slots(1), [0]
    for stride in strides:
        gathered = jnp.concatenate([gathered, lax.ppermute(gathered, "terms", [(i, i ^ stride) for i in range(groups)])], axis=0)
        offsets = offsets + [offset ^ stride for offset in offsets]
    offset_place = np.zeros((groups,), np.int32)
    offset_place[offsets] = np.arange(groups)

    settled0, image0 = run_sweep(load0, *beside((load0, load0), "space", 1), edge, inverse, matrix)
    source1 = slot_of[FIRSTS[1] : FIRSTS[1] + DIMS] // slot_dev
    slots1 = jnp.asarray(offset_place)[source1 ^ group]
    zeros = jnp.zeros((DIMS, DEGREE), jnp.int32)
    load1 = run_load(DIMS, slots1, (dims[1:6], zeros, zeros), weights[1:6], gathered, fields, [image0])
    settled1, image1 = run_sweep(load1, *beside((load1, load1), "space", 1), edge, inverse, matrix)

    settled = [settled0 * filled0]
    safe1, _, filled1 = slot_tables(1)
    own1 = lax.dynamic_slice_in_dim(settled1, jnp.clip(safe1[0] - 1, 0, DIMS - 1), 1, axis=0)
    settled.append(jnp.where(filled1[0], own1, 0.0))

    images, places, held = [image1], None, None
    for level in range(2, DEGREE + 1):
        safe, weight, _ = slot_tables(level)
        parent = parents[safe]
        if level == 2:
            block = jnp.zeros_like(parent)
            row = jnp.maximum(parent - FIRSTS[1], 0)
        else:
            slot = slot_of[parent]
            block = places[slot // slot_dev]
            row = jnp.clip(slot % slot_dev - starts[level - 1], 0, caps[level - 1] - 1)
        load = run_load(caps[level], jnp.arange(caps[level], dtype=jnp.int32), (dims[safe], block, row), weight, level_slots(level), fields, images)
        if level < DEGREE:
            result, image = run_sweep(load, *beside((load, load), "space", 1), edge, inverse, matrix)
            images, places = gather_blocks(image, group)
        else:
            head, tail = load[:, :, :1], load[:, :, 1:]
            pieces = (jnp.where(is_even, tail, head), jnp.where(is_even, head, tail))
            result = run_last(load, *beside(pieces, "space", 1), edge, inverse, matrix)
        settled.append(result)
    return jnp.concatenate(settled, axis=0)


def solution(mesh):
    return jax.shard_map(
        on_device,
        mesh=mesh,
        in_specs=(
            P("terms", None, "space", None, None),
            P(),
            P(None, "space", None, None),
            P(),
            P(),
        ),
        out_specs=P("terms", None, "space", None, None),
        check_vma=False,
    )
```

time: 556 us -> 247 us (0.44)
  the two profiles are of different devices: /device:TPU:1 before, /device:TPU:9 now
where the time goes in v1:
time: 247 us; the launch traced here: 246 us
  waiting for transfers between devices  94.2 us (38%)
  starting transfers between devices  50.7 us (21%)
  Pallas kernels  42.8 us (17%)
  local copies, waits for them, and re-layouts  37.4 us (15%)
  other arithmetic  13.4 us (5%)
  between operations  7.65 us (3%)
    ppermute x18, waiting for transfers between devices, send(): return lax.ppermute(array, 'terms', pairs)  59.6 us
    ppermute x18, starting transfers between devices, send(): return lax.ppermute(array, 'terms', pairs)  26.5 us
    pallas_call x4, Pallas kernels, run_sweep(): pl.pallas_call(functools.partial(sweep_kernel, terms), out_shape=[out, ou...  25.2 us
    ppermute x5, waiting for transfers between devices, beside(): lax.ppermute(array[1], axis, odd)  22 us
    ppermute x5, starting transfers between devices, beside(): lax.ppermute(array[1], axis, odd)  12.8 us
    pallas_call x4, Pallas kernels, run_load(): pl.pallas_call(functools.partial(load_kernel, terms, cap, blocks), out_sh...  11.1 us
    ppermute x3, waiting for transfers between devices, on_device(): lax.ppermute(gathered, 'terms', [(i, i ^ stride) for i in range(groups)])  8.64 us
    pallas_call x1, Pallas kernels, run_last(): pl.pallas_call(functools.partial(last_kernel, terms), out_shape=jax.Shape...  6.51 us
  transfers between devices with their start and end apart: 34, of which 24 were waited for; matrix products, arithmetic and copies ran while one was open for 15% of the time, Pallas kernels for 1%

profile of v1, /device:TPU:9, one launch (start us, length us, event | category | flops | bytes accessed | tf_op | source)
XLA Modules:
  0.0 246.1 jit_solution(16795689351791762370)
XLA Ops:
  11.9 3.8 %gather_fusion.15 = f32[504]{0:T(512)S(1)} fusion(f32[126,5]{0,1:T(8,128)S(1)} %copy-done, s32[504]{0:T(512)S(1)} %copy-done.2), kind=kCustom, calls=%fused_computation.15 | custom fusion | bytes 8064 | tf_op jit(solution)/shard_map/jit(take_along_axis)/gather | solution.py:294
  21.3 8.6 %collective-permute-done.6 = f32[2,3,2,32,128]{4,3,2,1,0:T(8,128)S(1)} collective-permute-done((f32[2,3,2,32,128]{4,3,2,1,0:T(8,128)S(1)}, f32[2,3,2,32,128]{4,3,2,1,0:T(8,128)S(1)}, u32[]{:S(2)}, u32[]{:S(2)}) %collective-permute-start.6) | collective-permute-done | bytes 196640 | tf_op jit(solution)/shard_map/ppermute | solution.py:315
  34.0 3.2 %collective-permute-start.1 = (f32[1,3,2,32,128]{4,3,2,1,0:T(8,128)S(1)}, f32[1,3,2,32,128]{4,3,2,1,0:T(8,128)S(1)}, u32[]{:S(2)}, u32[]{:S(2)}) collective-permute-start(f32[1,3,2,32,128]{4,3,2,1,0:T(8,128)S(1)} %add.213), channel_id=1, source_target_pairs={{0,4},{1,5},{2,6},{3,7},{4,0},{5,1},{6,2},{7,3},{8,12},{9,13},{10,... | collective-permute-start | bytes 294920 | tf_op jit(solution)/shard_map/ppermute | solution.py:312
  45.9 3.0 %collective-permute-start.4 = (f32[1,3,2,32,128]{4,3,2,1,0:T(8,128)S(1)}, f32[1,3,2,32,128]{4,3,2,1,0:T(8,128)S(1)}, u32[]{:S(2)}, u32[]{:S(2)}) collective-permute-start(f32[1,3,2,32,128]{4,3,2,1,0:T(8,128)S(1)} %add.215.load_ref), channel_id=1, source_target_pairs={{8,16},{16,8},{9,17},{17,9},{10,18},{18,10},{11,19},{19,11},{12,20... | collective-permute-start | bytes 294920 | tf_op jit(solution)/shard_map/ppermute | solution.py:240
  52.4 3.0 %sweep.4 = (f32[1,3,2,32,128]{4,3,2,1,0:T(8,128)}, f32[1,3,2,32,128]{4,3,2,1,0:T(8,128)}) custom-call(f32[3]{0:T(128)} %add_convert_fusion.edge_ref, f32[3]{0:T(128)} %broadcast_divide_fusion.2.inverse_ref, f32[288,288]{1,0:T(8,128)} %add.211.matrix_ref, f32[1,3,2,32,128]{4,3,2,1,0:T(8,128)} %copy-done.21, f32[1,3,2,32,128]{4,3,2,1,0:T(8,128)} %copy-done.34, ...), custom_call_target="tpu_custom_call" | custom-call | flops 382205952 | bytes 491520 | tf_op jit(solution)/shard_map/sweep/pallas_call | solution.py:192
  60.5 3.0 %collective-permute-start.9 = (f32[5,3,2,32,128]{4,3,2,1,0:T(8,128)}, f32[5,3,2,32,128]{4,3,2,1,0:T(8,128)}, u32[]{:S(2)}, u32[]{:S(2)}) collective-permute-start(f32[5,3,2,32,128]{4,3,2,1,0:T(8,128)} %loads.4.load_ref), channel_id=1, source_target_pairs={{8,16},{16,8},{9,17},{17,9},{10,18},{18,10},{11,19},{19,11},{12,20... | collective-permute-start | bytes 1474568 | tf_op jit(solution)/shard_map/ppermute | solution.py:240
  71.1 8.8 %sweep.5 = (f32[5,3,2,32,128]{4,3,2,1,0:T(8,128)}, f32[5,3,2,32,128]{4,3,2,1,0:T(8,128)}) custom-call(f32[3]{0:T(128)} %add_convert_fusion.edge_ref, f32[3]{0:T(128)} %broadcast_divide_fusion.2.inverse_ref, f32[288,288]{1,0:T(8,128)} %add.211.matrix_ref, f32[5,3,2,32,128]{4,3,2,1,0:T(8,128)} %loads.4.load_ref, f32[5,3,2,32,128]{4,3,2,1,0:T(8,128)} %copy-done.27, ...), custom_call_target="tpu_custom_call" | custom-call | flops 1911029760 | bytes 2457600 | tf_op jit(solution)/shard_map/sweep/pallas_call | solution.py:192
  85.9 4.3 %collective-permute-done.11.odd_ref = f32[2,3,2,32,128]{4,3,2,1,0:T(8,128)S(1)} collective-permute-done((f32[2,3,2,32,128]{4,3,2,1,0:T(8,128)}, f32[2,3,2,32,128]{4,3,2,1,0:T(8,128)S(1)}, u32[]{:S(2)}, u32[]{:S(2)}) %collective-permute-start.11) | collective-permute-done | bytes 196640 | tf_op jit(solution)/shard_map/ppermute | solution.py:240
  90.9 4.6 %sweep.6 = (f32[2,3,2,32,128]{4,3,2,1,0:T(8,128)}, f32[2,3,2,32,128]{4,3,2,1,0:T(8,128)}) custom-call(f32[3]{0:T(128)} %add_convert_fusion.edge_ref, f32[3]{0:T(128)} %broadcast_divide_fusion.2.inverse_ref, f32[288,288]{1,0:T(8,128)} %add.211.matrix_ref, f32[2,3,2,32,128]{4,3,2,1,0:T(8,128)} %loads.5.load_ref, f32[2,3,2,32,128]{4,3,2,1,0:T(8,128)} %copy-done.32, ...), custom_call_target="tpu_custom_call" | custom-call | flops 764411904 | bytes 983040 | tf_op jit(solution)/shard_map/sweep/pallas_call | solution.py:192
  123.1 4.2 %collective-permute-done.18.refs_5_ = f32[2,3,2,32,128]{4,3,2,1,0:T(8,128)S(1)} collective-permute-done((f32[2,3,2,32,128]{4,3,2,1,0:T(8,128)S(1)}, f32[2,3,2,32,128]{4,3,2,1,0:T(8,128)S(1)}, u32[]{:S(2)}, u32[]{:S(2)}) %collective-permute-start.18) | collective-permute-done | bytes 196640 | tf_op jit(solution)/shard_map/ppermute | solution.py:258
  127.3 3.9 %collective-permute-done.19.refs_6_ = f32[2,3,2,32,128]{4,3,2,1,0:T(8,128)S(1)} collective-permute-done((f32[2,3,2,32,128]{4,3,2,1,0:T(8,128)S(1)}, f32[2,3,2,32,128]{4,3,2,1,0:T(8,128)S(1)}, u32[]{:S(2)}, u32[]{:S(2)}) %collective-permute-start.19) | collective-permute-done | bytes 196640 | tf_op jit(solution)/shard_map/ppermute | solution.py:258
  138.7 8.3 %collective-permute-done.22.odd_ref = f32[5,3,2,32,128]{4,3,2,1,0:T(8,128)S(1)} collective-permute-done((f32[5,3,2,32,128]{4,3,2,1,0:T(8,128)}, f32[5,3,2,32,128]{4,3,2,1,0:T(8,128)S(1)}, u32[]{:S(2)}, u32[]{:S(2)}) %collective-permute-start.22) | collective-permute-done | bytes 491552 | tf_op jit(solution)/shard_map/ppermute | solution.py:240
  147.8 8.8 %sweep.7 = (f32[5,3,2,32,128]{4,3,2,1,0:T(8,128)}, f32[5,3,2,32,128]{4,3,2,1,0:T(8,128)}) custom-call(f32[3]{0:T(128)} %add_convert_fusion.edge_ref, f32[3]{0:T(128)} %broadcast_divide_fusion.2.inverse_ref, f32[288,288]{1,0:T(8,128)} %add.211.matrix_ref, f32[5,3,2,32,128]{4,3,2,1,0:T(8,128)} %loads.6.load_ref, f32[5,3,2,32,128]{4,3,2,1,0:T(8,128)} %copy-done.28, ...), custom_call_target="tpu_custom_call" | custom-call | flops 1911029760 | bytes 2457600 | tf_op jit(solution)/shard_map/sweep/pallas_call | solution.py:192
  156.6 3.3 %collective-permute-start.24 = (f32[5,3,2,32,128]{4,3,2,1,0:T(8,128)}, f32[5,3,2,32,128]{4,3,2,1,0:T(8,128)S(1)}, u32[]{:S(2)}, u32[]{:S(2)}) collective-permute-start(f32[5,3,2,32,128]{4,3,2,1,0:T(8,128)} %get-tuple-element.20.refs_0_), channel_id=1, source_target_pairs={{2,4},{3,5},{4,2},{5,3},{10,12},{11,13},{12,10},{13,11},{18,20},{1... | collective-permute-start | bytes 1474568 | tf_op jit(solution)/shard_map/ppermute | solution.py:258
  159.8 4.9 %collective-permute-done.23.refs_1_ = f32[5,3,2,32,128]{4,3,2,1,0:T(8,128)S(1)} collective-permute-done((f32[5,3,2,32,128]{4,3,2,1,0:T(8,128)}, f32[5,3,2,32,128]{4,3,2,1,0:T(8,128)S(1)}, u32[]{:S(2)}, u32[]{:S(2)}) %collective-permute-start.23) | collective-permute-done | bytes 491552 | tf_op jit(solution)/shard_map/ppermute | solution.py:258
  164.7 3.1 %collective-permute-start.26 = (f32[5,3,2,32,128]{4,3,2,1,0:T(8,128)S(1)}, f32[5,3,2,32,128]{4,3,2,1,0:T(8,128)S(1)}, u32[]{:S(2)}, u32[]{:S(2)}) collective-permute-start(f32[5,3,2,32,128]{4,3,2,1,0:T(8,128)S(1)} %collective-permute-done.23.refs_1_), channel_id=1, source_target_pairs={{2,4},{3,5},{4,2},{5,3},{10,12},{11,13},{12,10},{13,11},{18,20},{1... | collective-permute-start | bytes 1474568 | tf_op jit(solution)/shard_map/ppermute | solution.py:258
  171.5 5.5 %collective-permute-done.26 = f32[5,3,2,32,128]{4,3,2,1,0:T(8,128)S(1)} collective-permute-done((f32[5,3,2,32,128]{4,3,2,1,0:T(8,128)S(1)}, f32[5,3,2,32,128]{4,3,2,1,0:T(8,128)S(1)}, u32[]{:S(2)}, u32[]{:S(2)}) %collective-permute-start.26) | collective-permute-done | bytes 491552 | tf_op jit(solution)/shard_map/ppermute | solution.py:258
  181.2 6.6 %collective-permute-done.27 = f32[5,3,2,32,128]{4,3,2,1,0:T(8,128)S(1)} collective-permute-done((f32[5,3,2,32,128]{4,3,2,1,0:T(8,128)S(1)}, f32[5,3,2,32,128]{4,3,2,1,0:T(8,128)S(1)}, u32[]{:S(2)}, u32[]{:S(2)}) %collective-permute-start.27) | collective-permute-done | bytes 491552 | tf_op jit(solution)/shard_map/ppermute | solution.py:258
  195.7 6.8 %collective-permute-done.29.refs_5_ = f32[5,3,2,32,128]{4,3,2,1,0:T(8,128)} collective-permute-done((f32[5,3,2,32,128]{4,3,2,1,0:T(8,128)S(1)}, f32[5,3,2,32,128]{4,3,2,1,0:T(8,128)}, u32[]{:S(2)}, u32[]{:S(2)}) %collective-permute-start.29) | collective-permute-done | bytes 491552 | tf_op jit(solution)/shard_map/ppermute | solution.py:258
  202.5 10.5 %collective-permute-done.30.refs_6_ = f32[5,3,2,32,128]{4,3,2,1,0:T(8,128)} collective-permute-done((f32[5,3,2,32,128]{4,3,2,1,0:T(8,128)S(1)}, f32[5,3,2,32,128]{4,3,2,1,0:T(8,128)}, u32[]{:S(2)}, u32[]{:S(2)}) %collective-permute-start.30) | collective-permute-done | bytes 491552 | tf_op jit(solution)/shard_map/ppermute | solution.py:258
  213.1 7.9 %collective-permute-done.31.refs_7_ = f32[5,3,2,32,128]{4,3,2,1,0:T(8,128)} collective-permute-done((f32[5,3,2,32,128]{4,3,2,1,0:T(8,128)S(1)}, f32[5,3,2,32,128]{4,3,2,1,0:T(8,128)}, u32[]{:S(2)}, u32[]{:S(2)}) %collective-permute-start.31) | collective-permute-done | bytes 491552 | tf_op jit(solution)/shard_map/ppermute | solution.py:258
  221.6 4.0 %loads.7.load_ref = f32[9,3,2,32,128]{4,3,2,1,0:T(8,128)} custom-call(s32[9]{0:T(128)} %iota.29.slot_ref, s32[9,4]{1,0:T(8,128)} %gather_fusion.10, s32[9,4]{1,0:T(8,128)} %reshape.377.block_ref, s32[9,4]{1,0:T(8,128)} %fusion.1.row_ref, f32[9,5]{1,0:T(8,128)} %pad_multiply_fusion.weight_ref, f32[9,3,2,32,128]{4,3,2,1,0:T(8,128)} %slice.126.forcing_ref, ...), custom_call_target="tpu_custom_call" | custom-call | flops 2654208 | bytes 3932160 | tf_op jit(solution)/shard_map/loads/pallas_call | solution.py:224
  230.0 6.6 %collective-permute-done.33.odd_ref = f32[9,3,1,32,128]{4,3,2,1,0:T(8,128)S(1)} collective-permute-done((f32[9,3,1,32,128]{4,3,2,1,0:T(8,128)S(1)}, f32[9,3,1,32,128]{4,3,2,1,0:T(8,128)S(1)}, u32[]{:S(2)}, u32[]{:S(2)}) %collective-permute-start.33) | collective-permute-done | bytes 442400 | tf_op jit(solution)/shard_map/ppermute | solution.py:240
  237.4 6.5 %last_sweep.1 = f32[9,3,2,32,128]{4,3,2,1,0:T(8,128)} custom-call(f32[3]{0:T(128)} %add_convert_fusion.edge_ref, f32[3]{0:T(128)} %broadcast_divide_fusion.2.inverse_ref, f32[288,288]{1,0:T(8,128)} %add.211.matrix_ref, f32[9,3,2,32,128]{4,3,2,1,0:T(8,128)} %loads.7.load_ref, f32[9,3,1,32,128]{4,3,2,1,0:T(8,128)} %copy-done.30, f32[9,3,1,32,128]{4,3,2,1,0:T(8,128)} %copy-done.31), custom_call_target="tpu_custom_call" | custom-call | flops 1146617856 | bytes 2654208 | tf_op jit(solution)/shard_map/last_sweep/pallas_call | solution.py:209
  (239 shorter events, 105.0 us)
Async XLA Ops:
  3.0 15.8 %collective-permute-start.5 = (f32[1,3,2,32,128]{4,3,2,1,0:T(8,128)S(1)}, f32[1,3,2,32,128]{4,3,2,1,0:T(8,128)S(1)}, u32[]{:S(2)}, u32[]{:S(2)}) collective-permute-start(f32[1,3,2,32,128]{4,3,2,1,0:T(8,128)S(1)} %get-tuple-element.21), channel_id=1, source_target_pairs={{0,2},{1,3},{2,0},{3,1},{4,6},{5,7},{6,4},{7,5},{8,10},{9,11},{10,... | collective-permute-start | bytes 294920 | tf_op jit(solution)/shard_map/ppermute | solution.py:315
  3.1 31.0 %collective-permute-start = (f32[1,3,2,32,128]{4,3,2,1,0:T(8,128)S(1)}, f32[1,3,2,32,128]{4,3,2,1,0:T(8,128)S(1)}, u32[]{:S(2)}, u32[]{:S(2)}) collective-permute-start(f32[1,3,2,32,128]{4,3,2,1,0:T(8,128)S(1)} %get-tuple-element.22), channel_id=1, source_target_pairs={{0,2},{1,3},{2,0},{3,1},{4,6},{5,7},{6,4},{7,5},{8,10},{9,11},{10,... | collective-permute-start | bytes 294920 | tf_op jit(solution)/shard_map/ppermute | solution.py:312
  18.8 11.1 %collective-permute-start.6 = (f32[2,3,2,32,128]{4,3,2,1,0:T(8,128)S(1)}, f32[2,3,2,32,128]{4,3,2,1,0:T(8,128)S(1)}, u32[]{:S(2)}, u32[]{:S(2)}) collective-permute-start(f32[2,3,2,32,128]{4,3,2,1,0:T(8,128)S(1)} %pad_maximum_fusion.2), channel_id=1, source_target_pairs={{0,4},{1,5},{2,6},{3,7},{4,0},{5,1},{6,2},{7,3},{8,12},{9,13},{10,... | collective-permute-start | bytes 589832 | tf_op jit(solution)/shard_map/ppermute | solution.py:315
  30.7 24.7 %collective-permute-start.7 = (f32[4,3,2,32,128]{4,3,2,1,0:T(8,128)}, f32[4,3,2,32,128]{4,3,2,1,0:T(8,128)}, u32[]{:S(2)}, u32[]{:S(2)}) collective-permute-start(f32[4,3,2,32,128]{4,3,2,1,0:T(8,128)} %pad_maximum_fusion.1), channel_id=1, source_target_pairs={{0,1},{1,0},{2,3},{3,2},{4,5},{5,4},{6,7},{7,6},{8,9},{9,8},{10,11... | collective-permute-start | bytes 1179656 | tf_op jit(solution)/shard_map/ppermute | solution.py:315
  60.5 9.8 %collective-permute-start.8 = (f32[5,3,2,32,128]{4,3,2,1,0:T(8,128)}, f32[5,3,2,32,128]{4,3,2,1,0:T(8,128)S(1)}, u32[]{:S(2)}, u32[]{:S(2)}) collective-permute-start(f32[5,3,2,32,128]{4,3,2,1,0:T(8,128)} %loads.4.load_ref), channel_id=1, source_target_pairs={{0,8},{8,0},{16,24},{24,16},{1,9},{9,1},{17,25},{25,17},{2,10},{10... | collective-permute-start | bytes 1474568 | tf_op jit(solution)/shard_map/ppermute | solution.py:240
  60.5 10.5 %collective-permute-start.9 = (f32[5,3,2,32,128]{4,3,2,1,0:T(8,128)}, f32[5,3,2,32,128]{4,3,2,1,0:T(8,128)}, u32[]{:S(2)}, u32[]{:S(2)}) collective-permute-start(f32[5,3,2,32,128]{4,3,2,1,0:T(8,128)} %loads.4.load_ref), channel_id=1, source_target_pairs={{8,16},{16,8},{9,17},{17,9},{10,18},{18,10},{11,19},{19,11},{12,20... | collective-permute-start | bytes 1474568 | tf_op jit(solution)/shard_map/ppermute | solution.py:240
  83.0 7.2 %collective-permute-start.11 = (f32[2,3,2,32,128]{4,3,2,1,0:T(8,128)}, f32[2,3,2,32,128]{4,3,2,1,0:T(8,128)S(1)}, u32[]{:S(2)}, u32[]{:S(2)}) collective-permute-start(f32[2,3,2,32,128]{4,3,2,1,0:T(8,128)} %loads.5.load_ref), channel_id=1, source_target_pairs={{8,16},{16,8},{9,17},{17,9},{10,18},{18,10},{11,19},{19,11},{12,20... | collective-permute-start | bytes 589832 | tf_op jit(solution)/shard_map/ppermute | solution.py:240
  95.5 12.3 %collective-permute-start.12 = (f32[2,3,2,32,128]{4,3,2,1,0:T(8,128)}, f32[2,3,2,32,128]{4,3,2,1,0:T(8,128)S(1)}, u32[]{:S(2)}, u32[]{:S(2)}) collective-permute-start(f32[2,3,2,32,128]{4,3,2,1,0:T(8,128)} %get-tuple-element.18.refs_0_), channel_id=1, source_target_pairs={{0,2},{1,3},{2,0},{3,1},{4,6},{5,7},{6,4},{7,5},{8,10},{9,11},{10,... | collective-permute-start | bytes 589832 | tf_op jit(solution)/shard_map/ppermute | solution.py:258
  105.3 7.3 %collective-permute-start.13 = (f32[2,3,2,32,128]{4,3,2,1,0:T(8,128)S(1)}, f32[2,3,2,32,128]{4,3,2,1,0:T(8,128)S(1)}, u32[]{:S(2)}, u32[]{:S(2)}) collective-permute-start(f32[2,3,2,32,128]{4,3,2,1,0:T(8,128)S(1)} %copy-done.10), channel_id=1, source_target_pairs={{2,4},{3,5},{4,2},{5,3},{10,12},{11,13},{12,10},{13,11},{18,20},{1... | collective-permute-start | bytes 589832 | tf_op jit(solution)/shard_map/ppermute | solution.py:258
  116.1 7.0 %collective-permute-start.17 = (f32[2,3,2,32,128]{4,3,2,1,0:T(8,128)S(1)}, f32[2,3,2,32,128]{4,3,2,1,0:T(8,128)S(1)}, u32[]{:S(2)}, u32[]{:S(2)}) collective-permute-start(f32[2,3,2,32,128]{4,3,2,1,0:T(8,128)S(1)} %copy-done.10), channel_id=1, source_target_pairs={{0,1},{1,0},{2,3},{3,2},{4,5},{5,4},{6,7},{7,6},{8,9},{9,8},{10,11... | collective-permute-start | bytes 589832 | tf_op jit(solution)/shard_map/ppermute | solution.py:258
  116.8 10.5 %collective-permute-start.18 = (f32[2,3,2,32,128]{4,3,2,1,0:T(8,128)S(1)}, f32[2,3,2,32,128]{4,3,2,1,0:T(8,128)S(1)}, u32[]{:S(2)}, u32[]{:S(2)}) collective-permute-start(f32[2,3,2,32,128]{4,3,2,1,0:T(8,128)S(1)} %collective-permute-done.12.refs_1_), channel_id=1, source_target_pairs={{0,1},{1,0},{2,3},{3,2},{4,5},{5,4},{6,7},{7,6},{8,9},{9,8},{10,11... | collective-permute-start | bytes 589832 | tf_op jit(solution)/shard_map/ppermute | solution.py:258
  118.3 12.9 %collective-permute-start.19 = (f32[2,3,2,32,128]{4,3,2,1,0:T(8,128)S(1)}, f32[2,3,2,32,128]{4,3,2,1,0:T(8,128)S(1)}, u32[]{:S(2)}, u32[]{:S(2)}) collective-permute-start(f32[2,3,2,32,128]{4,3,2,1,0:T(8,128)S(1)} %add.231.refs_2_), channel_id=1, source_target_pairs={{0,1},{1,0},{2,3},{3,2},{4,5},{5,4},{6,7},{7,6},{8,9},{9,8},{10,11... | collective-permute-start | bytes 589832 | tf_op jit(solution)/shard_map/ppermute | solution.py:258
  120.4 12.8 %collective-permute-start.20 = (f32[2,3,2,32,128]{4,3,2,1,0:T(8,128)S(1)}, f32[2,3,2,32,128]{4,3,2,1,0:T(8,128)S(1)}, u32[]{:S(2)}, u32[]{:S(2)}) collective-permute-start(f32[2,3,2,32,128]{4,3,2,1,0:T(8,128)S(1)} %add.232.refs_3_), channel_id=1, source_target_pairs={{0,1},{1,0},{2,3},{3,2},{4,5},{5,4},{6,7},{7,6},{8,9},{9,8},{10,11... | collective-permute-start | bytes 589832 | tf_op jit(solution)/shard_map/ppermute | solution.py:258
  136.6 10.4 %collective-permute-start.22 = (f32[5,3,2,32,128]{4,3,2,1,0:T(8,128)}, f32[5,3,2,32,128]{4,3,2,1,0:T(8,128)S(1)}, u32[]{:S(2)}, u32[]{:S(2)}) collective-permute-start(f32[5,3,2,32,128]{4,3,2,1,0:T(8,128)} %loads.6.load_ref), channel_id=1, source_target_pairs={{8,16},{16,8},{9,17},{17,9},{10,18},{18,10},{11,19},{19,11},{12,20... | collective-permute-start | bytes 1474568 | tf_op jit(solution)/shard_map/ppermute | solution.py:240
  156.6 8.2 %collective-permute-start.23 = (f32[5,3,2,32,128]{4,3,2,1,0:T(8,128)}, f32[5,3,2,32,128]{4,3,2,1,0:T(8,128)S(1)}, u32[]{:S(2)}, u32[]{:S(2)}) collective-permute-start(f32[5,3,2,32,128]{4,3,2,1,0:T(8,128)} %get-tuple-element.20.refs_0_), channel_id=1, source_target_pairs={{0,2},{1,3},{2,0},{3,1},{4,6},{5,7},{6,4},{7,5},{8,10},{9,11},{10,... | collective-permute-start | bytes 1474568 | tf_op jit(solution)/shard_map/ppermute | solution.py:258
  156.6 13.6 %collective-permute-start.24 = (f32[5,3,2,32,128]{4,3,2,1,0:T(8,128)}, f32[5,3,2,32,128]{4,3,2,1,0:T(8,128)S(1)}, u32[]{:S(2)}, u32[]{:S(2)}) collective-permute-start(f32[5,3,2,32,128]{4,3,2,1,0:T(8,128)} %get-tuple-element.20.refs_0_), channel_id=1, source_target_pairs={{2,4},{3,5},{4,2},{5,3},{10,12},{11,13},{12,10},{13,11},{18,20},{1... | collective-permute-start | bytes 1474568 | tf_op jit(solution)/shard_map/ppermute | solution.py:258
  164.7 12.3 %collective-permute-start.26 = (f32[5,3,2,32,128]{4,3,2,1,0:T(8,128)S(1)}, f32[5,3,2,32,128]{4,3,2,1,0:T(8,128)S(1)}, u32[]{:S(2)}, u32[]{:S(2)}) collective-permute-start(f32[5,3,2,32,128]{4,3,2,1,0:T(8,128)S(1)} %collective-permute-done.23.refs_1_), channel_id=1, source_target_pairs={{2,4},{3,5},{4,2},{5,3},{10,12},{11,13},{12,10},{13,11},{18,20},{1... | collective-permute-start | bytes 1474568 | tf_op jit(solution)/shard_map/ppermute | solution.py:258
  170.2 9.7 %collective-permute-start.25 = (f32[5,3,2,32,128]{4,3,2,1,0:T(8,128)S(1)}, f32[5,3,2,32,128]{4,3,2,1,0:T(8,128)S(1)}, u32[]{:S(2)}, u32[]{:S(2)}) collective-permute-start(f32[5,3,2,32,128]{4,3,2,1,0:T(8,128)S(1)} %collective-permute-done.24), channel_id=1, source_target_pairs={{2,0},{3,1},{4,6},{5,7},{10,8},{11,9},{12,14},{13,15},{18,16},{19,... | collective-permute-start | bytes 1474568 | tf_op jit(solution)/shard_map/ppermute | solution.py:258
  177.0 10.7 %collective-permute-start.27 = (f32[5,3,2,32,128]{4,3,2,1,0:T(8,128)S(1)}, f32[5,3,2,32,128]{4,3,2,1,0:T(8,128)S(1)}, u32[]{:S(2)}, u32[]{:S(2)}) collective-permute-start(f32[5,3,2,32,128]{4,3,2,1,0:T(8,128)S(1)} %collective-permute-done.26), channel_id=1, source_target_pairs={{2,0},{3,1},{4,6},{5,7},{10,8},{11,9},{12,14},{13,15},{18,16},{19,... | collective-permute-start | bytes 1474568 | tf_op jit(solution)/shard_map/ppermute | solution.py:258
  178.3 17.4 %collective-permute-start.28 = (f32[5,3,2,32,128]{4,3,2,1,0:T(8,128)}, f32[5,3,2,32,128]{4,3,2,1,0:T(8,128)}, u32[]{:S(2)}, u32[]{:S(2)}) collective-permute-start(f32[5,3,2,32,128]{4,3,2,1,0:T(8,128)} %get-tuple-element.20.refs_0_), channel_id=1, source_target_pairs={{0,1},{1,0},{2,3},{3,2},{4,5},{5,4},{6,7},{7,6},{8,9},{9,8},{10,11... | collective-permute-start | bytes 1474568 | tf_op jit(solution)/shard_map/ppermute | solution.py:258
  179.6 23.0 %collective-permute-start.29 = (f32[5,3,2,32,128]{4,3,2,1,0:T(8,128)S(1)}, f32[5,3,2,32,128]{4,3,2,1,0:T(8,128)}, u32[]{:S(2)}, u32[]{:S(2)}) collective-permute-start(f32[5,3,2,32,128]{4,3,2,1,0:T(8,128)S(1)} %collective-permute-done.23.refs_1_), channel_id=1, source_target_pairs={{0,1},{1,0},{2,3},{3,2},{4,5},{5,4},{6,7},{7,6},{8,9},{9,8},{10,11... | collective-permute-start | bytes 1474568 | tf_op jit(solution)/shard_map/ppermute | solution.py:258
  180.0 33.1 %collective-permute-start.30 = (f32[5,3,2,32,128]{4,3,2,1,0:T(8,128)S(1)}, f32[5,3,2,32,128]{4,3,2,1,0:T(8,128)}, u32[]{:S(2)}, u32[]{:S(2)}) collective-permute-start(f32[5,3,2,32,128]{4,3,2,1,0:T(8,128)S(1)} %add.246.refs_2_), channel_id=1, source_target_pairs={{0,1},{1,0},{2,3},{3,2},{4,5},{5,4},{6,7},{7,6},{8,9},{9,8},{10,11... | collective-permute-start | bytes 1474568 | tf_op jit(solution)/shard_map/ppermute | solution.py:258
  187.8 33.2 %collective-permute-start.31 = (f32[5,3,2,32,128]{4,3,2,1,0:T(8,128)S(1)}, f32[5,3,2,32,128]{4,3,2,1,0:T(8,128)}, u32[]{:S(2)}, u32[]{:S(2)}) collective-permute-start(f32[5,3,2,32,128]{4,3,2,1,0:T(8,128)S(1)} %add.247.refs_3_), channel_id=1, source_target_pairs={{0,1},{1,0},{2,3},{3,2},{4,5},{5,4},{6,7},{7,6},{8,9},{9,8},{10,11... | collective-permute-start | bytes 1474568 | tf_op jit(solution)/shard_map/ppermute | solution.py:258
  227.0 9.6 %collective-permute-start.33 = (f32[9,3,1,32,128]{4,3,2,1,0:T(8,128)S(1)}, f32[9,3,1,32,128]{4,3,2,1,0:T(8,128)S(1)}, u32[]{:S(2)}, u32[]{:S(2)}) collective-permute-start(f32[9,3,1,32,128]{4,3,2,1,0:T(8,128)S(1)} %get-tuple-element.23), channel_id=1, source_target_pairs={{8,16},{16,8},{9,17},{17,9},{10,18},{18,10},{11,19},{19,11},{12,20... | collective-permute-start | bytes 1327112 | tf_op jit(solution)/shard_map/ppermute | solution.py:240
  (46 other events, 336.9 us)

commit v2 on v1

v2 whole, which is shorter than its diff:
```python
import functools
import math

import jax
import jax.numpy as jnp
import numpy as np
from jax import lax
from jax.experimental import pallas as pl
from jax.experimental.pallas import tpu as pltpu
from jax.sharding import PartitionSpec as P

DIMS = 5
DEGREE = 4
F32 = jnp.float32
BF16 = jnp.bfloat16
ANY = pl.BlockSpec(memory_space=pl.ANY)
VMEM = pl.BlockSpec(memory_space=pltpu.VMEM)
SMEM = pl.BlockSpec(memory_space=pltpu.SMEM)
PARAMS = pltpu.CompilerParams(vmem_limit_bytes=20 * 2**20)


def compositions(total, pieces_left):
    if pieces_left == 1:
        return [[total]]
    result = []
    for leading in range(total, -1, -1):
        for remainder in compositions(total - leading, pieces_left - 1):
            result.append([leading] + remainder)
    return result


def chaos_links():
    indices = []
    for level in range(DEGREE + 1):
        indices.extend(compositions(level, DIMS))
    lookup = {tuple(vector): number for number, vector in enumerate(indices)}
    dims = np.zeros((len(indices), DEGREE), np.int32)
    parents = np.full((len(indices), DEGREE), -1, np.int32)
    for number, vector in enumerate(indices):
        place = 0
        for dim in range(DIMS):
            if vector[dim] > 0:
                lowered = list(vector)
                lowered[dim] -= 1
                dims[number, place] = dim
                parents[number, place] = lookup[tuple(lowered)]
                place += 1
    return dims, parents


LINK_DIMS, LINK_PARENTS = chaos_links()
LINKS = np.concatenate([LINK_PARENTS, LINK_DIMS], axis=1).T.astype(np.int32)
COUNTS = [math.comb(level + DIMS - 1, DIMS - 1) for level in range(DEGREE + 1)]
FIRSTS = [sum(COUNTS[:level]) for level in range(DEGREE + 1)]


def prologue_kernel(slot_ref, forcing_ref, out_ref):
    slot_dev = forcing_ref.shape[0]
    pltpu.sync_copy(forcing_ref.at[pl.ds(0, 2)], out_ref)
    filled = slot_ref[lax.axis_index("terms") * slot_dev] >= 0
    out_ref[0] = jnp.where(filled, out_ref[0], 0.0)


def matrix_kernel(stencil_ref, packed_ref):
    size = packed_ref.shape[1] // 3
    rows = size // 9
    lane = lax.broadcasted_iota(jnp.int32, (rows, size), 1)
    shift = lane % rows - lax.broadcasted_iota(jnp.int32, (rows, size), 0) + 1
    column = lane // rows
    for oz in range(3):
        for a in range(3):
            block = jnp.zeros((rows, size), F32)
            for oy in range(3):
                taps = jnp.zeros((rows, size), F32)
                for ox in range(3):
                    for b in range(3):
                        taps = jnp.where(column == 3 * ox + b, stencil_ref[a, b, 9 * ox + 3 * oy + oz], taps)
                block = jnp.where(shift == oy, taps, block)
            high = block.astype(BF16)
            place = pl.ds((3 * oz + a) * rows, rows)
            packed_ref[place, :size] = high
            packed_ref[place, size : 2 * size] = high
            packed_ref[place, 2 * size :] = (block - high.astype(F32)).astype(BF16)


def put_split(value, high_ref, low_ref, place):
    high = value.astype(BF16)
    high_ref[place] = high
    low_ref[place] = (value - high.astype(F32)).astype(BF16)


def apply_pair(high_ref, low_ref, packed_ref, place):
    def window(ref):
        return [jnp.concatenate([ref[place + k], ref[place + k + 1]], axis=1) for k in range(3)]

    high = window(high_ref)
    operand = jnp.concatenate(high + window(low_ref) + high, axis=0)
    product = jnp.dot(packed_ref[...], operand, preferred_element_type=F32)
    lanes = high_ref.shape[2]
    size = high_ref.shape[1]
    lane = lax.broadcasted_iota(jnp.int32, (size, lanes), 1)
    results = []
    for half in range(2):
        block = product[:, half * lanes : (half + 1) * lanes]
        before = pltpu.roll(block[:size], 1, 1)
        after = pltpu.roll(block[2 * size :], lanes - 1, 1)
        results.append(block[size : 2 * size] + jnp.where(lane > 0, before, 0.0) + jnp.where(lane < lanes - 1, after, 0.0))
    return results


def inverse_pivots(stencil_ref, rows, lanes):
    return jnp.concatenate([1.0 / jnp.full((rows, lanes), stencil_ref[a, a, 13], F32) for a in range(3)], axis=0)


def sweep_terms(terms, stencil_ref, packed, load_ref, even_ref, odd_ref, settled_ref, images, high, low, high2, low2):
    rows, lanes = load_ref.shape[3:]
    size = 3 * rows
    inverse = inverse_pivots(stencil_ref, rows, lanes)
    slab = lax.axis_index("space")
    is_even = slab % 2 == 0
    has_lower = slab > 0
    has_upper = slab < lax.axis_size("space") - 1

    def layer(ref, term, x):
        return ref[term, :, x].reshape(size, lanes)

    for term in range(terms):

        def load(x):
            if 2 <= x < 4:
                return layer(load_ref, term, x - 2)
            if x < 2:
                return jnp.where(is_even, layer(odd_ref, term, x), layer(even_ref, term, x))
            return jnp.where(is_even, layer(even_ref, term, x - 4), layer(odd_ref, term, x - 4))

        for x in range(6):
            put_split(load(x) * inverse, high.at[term], low.at[term], x)
        for pair in range(2):
            applied = apply_pair(high.at[term], low.at[term], packed, 2 * pair)
            for half in range(2):
                x = 2 * pair + half + 1
                load_x = load(x)
                settled = load_x * inverse + (load_x - applied[half]) * inverse
                if x == 1:
                    settled = jnp.where(has_lower, settled, 0.0)
                if x == 4:
                    settled = jnp.where(has_upper, settled, 0.0)
                if 2 <= x < 4:
                    settled_ref[term, :, x - 2] = settled.reshape(3, rows, lanes)
                put_split(settled, high2.at[term], low2.at[term], x - 1)
        applied = apply_pair(high2.at[term], low2.at[term], packed, 0)
        for half in range(2):
            images[term][:, half] = applied[half].reshape(3, rows, lanes)


def sweep_kernel(parts, stencil_ref, packed, load_ref, even_ref, odd_ref, settled_ref, *refs):
    images = [ref.at[i] for ref, part in zip(refs, parts, strict=False) for i in range(part)]
    sweep_terms(sum(parts), stencil_ref, packed, load_ref, even_ref, odd_ref, settled_ref, images, *refs[len(parts) :])


def child_load(links, group, slot_dev, start, slot, slot_ref, coupling_ref, links_ref, forcing, fields, image_of):
    child = slot_ref[group * slot_dev + start + slot]
    filled = child >= 0
    child = jnp.maximum(child, 0)
    total = forcing[slot]
    for link in range(links):
        parent = links_ref[link, child]
        dim = links_ref[DEGREE + link, child]
        weight = jnp.where(parent >= 0, coupling_ref[dim, child], 0.0)
        total = total - (fields[dim] * weight)[None] * image_of(jnp.maximum(parent, 0))
    return jnp.where(filled, total, 0.0)


def sweep_one_kernel(cap, start, slot_ref, coupling_ref, links_ref, stencil_ref, packed, load_ref, even_ref, odd_ref, fields_ref, forcing_ref, settled_ref, next_ref, image_ref, forcing, *scratch):
    slot_dev = forcing_ref.shape[0]
    pltpu.sync_copy(forcing_ref.at[pl.ds(start, cap)], forcing)
    sweep_terms(DIMS, stencil_ref, packed, load_ref, even_ref, odd_ref, settled_ref, [image_ref.at[i] for i in range(DIMS)], *scratch)
    group = lax.axis_index("terms")
    for slot in range(cap):
        next_ref[slot] = child_load(
            2, group, slot_dev, start, slot, slot_ref, coupling_ref, links_ref, forcing, fields_ref, lambda parent: image_ref[jnp.clip(parent - 1, 0, DIMS - 1)]
        )


def first_load_kernel(groups, slot_dev, slot_ref, coupling_ref, order_ref, fields_ref, image_ref, *refs):
    load_ref, gathered_ref, place = refs[-3:]
    for pair in range(groups // 2):
        gathered_ref[2 * pair : 2 * pair + 2] = refs[pair][...]
    group = lax.axis_index("terms")
    for source in range(groups):
        term = slot_ref[source * slot_dev + 1]

        @pl.when(term >= 0)
        def _():
            place[jnp.maximum(term, 0)] = order_ref[group, source]

    for dim in range(DIMS):
        load_ref[dim] = gathered_ref[place[dim + 1]] - (fields_ref[dim] * coupling_ref[dim, dim + 1])[None] * image_ref[0]


def load_kernel(level, cap, start, parts, old_start, blocks, slot_ref, coupling_ref, links_ref, order_ref, fields_ref, forcing_ref, *refs):
    old_cap = sum(parts)
    image_refs = refs[: blocks * len(parts)]
    load_ref = refs[len(image_refs)]
    pieces = refs[len(image_refs) + 1 : -3]
    images, forcing, place = refs[-3:]
    slot_dev = forcing_ref.shape[0]
    group = lax.axis_index("terms")
    pltpu.sync_copy(forcing_ref.at[pl.ds(start, cap)], forcing)
    for source in range(blocks):
        for slot in range(old_cap):
            term = slot_ref[source * slot_dev + old_start + slot]

            @pl.when(term >= 0)
            def _():
                place[jnp.maximum(term, 0)] = order_ref[group, source] * old_cap + slot

    for block in range(blocks):
        offset = block * old_cap
        for number, part in enumerate(parts):
            images[offset : offset + part] = image_refs[number * blocks + block][...]
            offset += part
    is_even = lax.axis_index("space") % 2 == 0
    for slot in range(cap):

        def image_of(parent):
            return images[jnp.clip(place[parent], 0, blocks * old_cap - 1)]

        load = child_load(level, group, slot_dev, start, slot, slot_ref, coupling_ref, links_ref, forcing, fields_ref, image_of)
        load_ref[slot] = load
        if pieces:
            pieces[0][slot] = jnp.where(is_even, load[:, 1], load[:, 0])
            pieces[1][slot] = jnp.where(is_even, load[:, 0], load[:, 1])


def last_kernel(starts, caps, slot_ref, stencil_ref, packed, load_ref, even_ref, odd_ref, zero_ref, one_ref, two_ref, three_ref, out_ref, high, low):
    rows, lanes = load_ref.shape[3:]
    size = 3 * rows
    slot_dev = out_ref.shape[0]
    first = lax.axis_index("terms") * slot_dev
    out_ref[0] = jnp.where(slot_ref[first] >= 0, zero_ref[0], 0.0)
    own = slot_ref[first + 1]
    out_ref[1] = jnp.where(own >= 0, one_ref[jnp.clip(own - 1, 0, DIMS - 1)], 0.0)
    out_ref[starts[2] : starts[2] + caps[2]] = two_ref[...]
    out_ref[starts[3] : starts[3] + caps[3]] = three_ref[...]
    inverse = inverse_pivots(stencil_ref, rows, lanes)
    is_even = lax.axis_index("space") % 2 == 0
    for term in range(caps[4]):
        even = even_ref[term].reshape(size, lanes)
        odd = odd_ref[term].reshape(size, lanes)
        put_split(jnp.where(is_even, odd, even) * inverse, high.at[term], low.at[term], 0)
        put_split(jnp.where(is_even, even, odd) * inverse, high.at[term], low.at[term], 3)
        for x in range(2):
            put_split(load_ref[term, :, x].reshape(size, lanes) * inverse, high.at[term], low.at[term], x + 1)
        applied = apply_pair(high.at[term], low.at[term], packed, 0)
        for x in range(2):
            load = load_ref[term, :, x].reshape(size, lanes)
            settled = load * inverse + (load - applied[x]) * inverse
            out_ref[starts[4] + term, :, x] = settled.reshape(3, rows, lanes)


def split_scratch(terms, layers, size, lanes):
    return [pltpu.VMEM((terms, layers, size, lanes), BF16)] * 2


def cost(flops, operands):
    return pl.CostEstimate(flops=flops, bytes_accessed=sum(4 * math.prod(o.shape) for o in operands), transcendentals=0)


def call(kernel, out_shape, specs, scratch, operands, name, flops=0):
    single = not isinstance(out_shape, list)
    return pl.pallas_call(
        kernel,
        out_shape=out_shape,
        in_specs=specs,
        out_specs=VMEM if single else [VMEM] * len(out_shape),
        scratch_shapes=scratch,
        compiler_params=PARAMS,
        cost_estimate=cost(flops, operands),
        name=name,
    )(*operands)


def beside(array, axis):
    count = lax.axis_size(axis)
    even = [(i, i ^ 1) for i in range(count)]
    odd = [(i, ((i + 1) ^ 1) - 1) for i in range(1, count - 1)]
    return lax.ppermute(array[0], axis, even), lax.ppermute(array[1], axis, odd)


def gather_blocks(block):
    count = lax.axis_size("terms")
    if count != 8:
        whole = lax.all_gather(block, "terms", axis=0, tiled=False)
        return [whole[i] for i in range(count)], np.tile(np.arange(count, dtype=np.int32), (count, 1))

    def columns(pairs):
        return [(2 * i + x, 2 * j + x) for i, j in pairs for x in range(2)]

    ends = columns([(0, 1), (1, 0), (2, 3), (3, 2)])
    middle = columns([(1, 2), (2, 1)])
    outward = columns([(1, 0), (2, 3)])
    across = [(i, i ^ 1) for i in range(8)]

    def send(array, pairs):
        return lax.ppermute(array, "terms", pairs)

    near, middle_one, across_own = lax.optimization_barrier((send(block, ends), send(block, middle), send(block, across)))
    second = middle_one + send(middle_one, outward)
    middle_two, second, across_near = lax.optimization_barrier((send(near, middle), second, send(near, across)))
    third = middle_two + send(middle_two, outward)
    third, across_second = lax.optimization_barrier((third, send(second, across)))
    column = np.array([[0, 1, 2, 3], [1, 0, 2, 3], [3, 2, 0, 1], [3, 2, 1, 0]], np.int32)
    order = [[column[i // 2, j // 2] + 4 * ((i ^ j) & 1) for j in range(8)] for i in range(8)]
    return [block, near, second, third, across_own, across_near, across_second, send(third, across)], np.array(order, np.int32)


def on_device(forcing, stencil, fields, coupling, slot_term):
    groups = lax.axis_size("terms")
    slot_dev = forcing.shape[0]
    group = lax.axis_index("terms")
    caps = [(count + groups - 1) // groups for count in COUNTS]
    starts = [sum(caps[:level]) for level in range(DEGREE + 1)]
    rows, lanes = forcing.shape[3:]
    size = 3 * rows
    field = forcing.shape[1:]

    def array(*shape):
        return jax.ShapeDtypeStruct(shape, F32)

    taps = jnp.transpose(stencil, (1, 2, 0))
    weights = coupling.T
    links = jnp.asarray(LINKS)
    first = call(prologue_kernel, array(2, *field), [SMEM, ANY], [], [slot_term, forcing], "prologue")
    packed = call(matrix_kernel, jax.ShapeDtypeStruct((3 * size, 9 * size), BF16), [SMEM], [], [taps], "matrix")

    def swap(operand, stride):
        return lax.ppermute(operand, "terms", [(i, i ^ stride) for i in range(groups)])

    other = swap(first, 1)
    load = first[:1] + other[:1]
    pair = jnp.concatenate([first[1:], other[1:]], axis=0)
    gathered, offsets = [pair], [0, 1]
    for offset in range(2, groups, 2):
        gathered.append(swap(pair, offset))
        offsets += [offset, offset ^ 1]
    stride = 2
    while stride < groups:
        load = load + swap(load, stride)
        stride *= 2
    order = np.zeros((groups, groups), np.int32)
    for device in range(groups):
        for place, offset in enumerate(offsets):
            order[device, device ^ offset] = place

    def dots(count):
        return count * 2 * 27 * size * size * 256

    def sweep(level_load, parts):
        terms = sum(parts)
        operands = [taps, packed, level_load, *beside((level_load, level_load), "space")]
        scratch = split_scratch(terms, 6, size, lanes) + split_scratch(terms, 4, size, lanes)
        shapes = [array(terms, *field)] + [array(part, *field) for part in parts]
        return call(functools.partial(sweep_kernel, parts), shapes, [SMEM] + [VMEM] * 4, scratch, operands, "sweep", dots(3 * terms))

    settled0, image0 = sweep(load, (1,))
    load = call(
        functools.partial(first_load_kernel, groups, slot_dev),
        array(DIMS, *field),
        [SMEM] * 3 + [VMEM] * (2 + len(gathered)),
        [pltpu.VMEM((groups, *field), F32), pltpu.SMEM((128,), jnp.int32)],
        [slot_term, weights, jnp.asarray(order), fields, image0, *gathered],
        "first_loads",
    )
    settled1, load = call(
        functools.partial(sweep_one_kernel, caps[2], starts[2]),
        [array(DIMS, *field), array(caps[2], *field)],
        [SMEM] * 4 + [VMEM] * 5 + [ANY],
        [pltpu.VMEM((DIMS, *field), F32), pltpu.VMEM((caps[2], *field), F32)] + split_scratch(DIMS, 6, size, lanes) + split_scratch(DIMS, 4, size, lanes),
        [slot_term, weights, links, taps, packed, load, *beside((load, load), "space"), fields, forcing],
        "sweep_one",
        dots(3 * DIMS),
    )
    settled = [settled0, settled1]
    for level in (3, 4):
        old = caps[level - 1]
        parts = (old,)
        result, *images = sweep(load, parts)
        settled.append(result)
        blocks = []
        for image in images:
            gathered, order = gather_blocks(image)
            blocks += gathered
        shapes = [array(caps[level], *field)]
        if level == DEGREE:
            shapes += [array(caps[level], 3, rows, lanes)] * 2
        load, *pieces = call(
            functools.partial(load_kernel, level, caps[level], starts[level], parts, starts[level - 1], groups),
            shapes,
            [SMEM] * 4 + [VMEM, ANY] + [VMEM] * len(blocks),
            [pltpu.VMEM((old * groups, *field), F32), pltpu.VMEM((caps[level], *field), F32), pltpu.SMEM((128,), jnp.int32)],
            [slot_term, weights, links, jnp.asarray(order), fields, forcing, *blocks],
            "loads",
        )
    return call(
        functools.partial(last_kernel, starts, caps),
        array(*forcing.shape),
        [SMEM] * 2 + [VMEM] * 8,
        split_scratch(caps[4], 4, size, lanes),
        [slot_term, taps, packed, load, *beside(pieces, "space"), *settled],
        "last_sweep",
        dots(caps[4]),
    )


def solution(mesh):
    return jax.shard_map(
        on_device,
        mesh=mesh,
        in_specs=(
            P("terms", None, "space", None, None),
            P(),
            P(None, "space", None, None),
            P(),
            P(),
        ),
        out_specs=P("terms", None, "space", None, None),
        check_vma=False,
    )
```

time: 247 us -> 184 us (0.74)
  the two profiles are of different devices: /device:TPU:9 before, /device:TPU:1 now
where the time goes in v2:
time: 184 us
  waiting for transfers between devices  98.4 us (53%)
  starting transfers between devices  57.4 us (31%)
  Pallas kernels  24.9 us (14%)
  local copies, waits for them, and re-layouts  2.2 us (1%)
    ppermute x18, waiting for transfers between devices, send(): return lax.ppermute(array, 'terms', pairs)  66.3 us
    ppermute x5, starting transfers between devices, beside(): lax.ppermute(array[1], axis, odd)  28.3 us
    ppermute x5, waiting for transfers between devices, beside(): lax.ppermute(array[1], axis, odd)  25.2 us
    pallas_call x10, Pallas kernels, call(): pl.pallas_call(kernel, out_shape=out_shape, in_specs=specs, out_specs=VME...  24.9 us
    ppermute x18, starting transfers between devices, send(): return lax.ppermute(array, 'terms', pairs)  19.1 us
    ppermute x6, starting transfers between devices, swap(): lax.ppermute(operand, 'terms', [(i, i ^ stride) for i in range(groups)])  9.32 us
    ppermute x6, waiting for transfers between devices, swap(): lax.ppermute(operand, 'terms', [(i, i ^ stride) for i in range(groups)])  6.88 us
  transfers between devices with their start and end apart: 34, of which 17 were waited for; matrix products, arithmetic and copies ran while one was open for 0% of the time, Pallas kernels for 2%

profile of v2, /device:TPU:1, one launch (start us, length us, event | category | flops | bytes accessed | tf_op | source)
XLA Modules:
  0.0 183.6 jit_solution(4525367652780091642)
XLA Ops:
  5.1 4.6 %collective-permute-done = f32[2,3,2,32,128]{4,3,2,1,0:T(8,128)S(1)} collective-permute-done((f32[2,3,2,32,128]{4,3,2,1,0:T(8,128)S(1)}, f32[2,3,2,32,128]{4,3,2,1,0:T(8,128)S(1)}, u32[]{:S(2)}, u32[]{:S(2)}) %collective-permute-start) | collective-permute-done | bytes 196640 | tf_op jit(solution)/shard_map/ppermute | solution.py:338
  19.3 15.4 %collective-permute-start.4 = (f32[1,3,2,32,128]{4,3,2,1,0:T(8,128)S(1)}, f32[1,3,2,32,128]{4,3,2,1,0:T(8,128)S(1)}, u32[]{:S(2)}, u32[]{:S(2)}) collective-permute-start(f32[1,3,2,32,128]{4,3,2,1,0:T(8,128)S(1)} %add.23.load_ref), channel_id=1, source_target_pairs={{8,16},{16,8},{9,17},{17,9},{10,18},{18,10},{11,19},{19,11},{12,20... | collective-permute-start | bytes 294920 | tf_op jit(solution)/shard_map/ppermute | solution.py:288
  40.1 3.3 %collective-permute-start.9 = (f32[5,3,2,32,128]{4,3,2,1,0:T(8,128)S(1)}, f32[5,3,2,32,128]{4,3,2,1,0:T(8,128)S(1)}, u32[]{:S(2)}, u32[]{:S(2)}) collective-permute-start(f32[5,3,2,32,128]{4,3,2,1,0:T(8,128)S(1)} %first_loads.1.load_ref), channel_id=1, source_target_pairs={{8,16},{16,8},{9,17},{17,9},{10,18},{18,10},{11,19},{19,11},{12,20... | collective-permute-start | bytes 1474568 | tf_op jit(solution)/shard_map/ppermute | solution.py:288
  43.5 6.7 %collective-permute-done.9.odd_ref = f32[5,3,2,32,128]{4,3,2,1,0:T(8,128)S(1)} collective-permute-done((f32[5,3,2,32,128]{4,3,2,1,0:T(8,128)S(1)}, f32[5,3,2,32,128]{4,3,2,1,0:T(8,128)S(1)}, u32[]{:S(2)}, u32[]{:S(2)}) %collective-permute-start.9) | collective-permute-done | bytes 491552 | tf_op jit(solution)/shard_map/ppermute | solution.py:288
  50.2 5.8 %sweep_one.1 = (f32[5,3,2,32,128]{4,3,2,1,0:T(8,128)S(1)}, f32[2,3,2,32,128]{4,3,2,1,0:T(8,128)S(1)}) custom-call(s32[144]{0:T(256)S(1)} %copy-done.5, f32[5,126]{1,0:T(8,128)S(1)} %bitcast.3, s32[8,126]{1,0:T(8,128)S(1)} %copy-done.7, f32[3,3,27]{2,1,0:T(4,128)S(1)} %bitcast.8, bf16[288,864]{1,0:T(8,128)(2,1)S(1)} %matrix.1.packed, ...), custom_call_target="tpu_custom_call" | custom-call | flops 1911029760 | bytes 4411300 | tf_op jit(solution)/shard_map/sweep_one/pallas_call | solution.py:272
  56.1 3.3 %collective-permute-start.11 = (f32[2,3,2,32,128]{4,3,2,1,0:T(8,128)S(1)}, f32[2,3,2,32,128]{4,3,2,1,0:T(8,128)S(1)}, u32[]{:S(2)}, u32[]{:S(2)}) collective-permute-start(f32[2,3,2,32,128]{4,3,2,1,0:T(8,128)S(1)} %get-tuple-element.33.load_ref), channel_id=1, source_target_pairs={{8,16},{16,8},{9,17},{17,9},{10,18},{18,10},{11,19},{19,11},{12,20... | collective-permute-start | bytes 589832 | tf_op jit(solution)/shard_map/ppermute | solution.py:288
  59.5 3.6 %collective-permute-done.11.odd_ref = f32[2,3,2,32,128]{4,3,2,1,0:T(8,128)S(1)} collective-permute-done((f32[2,3,2,32,128]{4,3,2,1,0:T(8,128)S(1)}, f32[2,3,2,32,128]{4,3,2,1,0:T(8,128)S(1)}, u32[]{:S(2)}, u32[]{:S(2)}) %collective-permute-start.11) | collective-permute-done | bytes 196640 | tf_op jit(solution)/shard_map/ppermute | solution.py:288
  63.1 2.6 %sweep.4 = (f32[2,3,2,32,128]{4,3,2,1,0:T(8,128)S(1)}, f32[2,3,2,32,128]{4,3,2,1,0:T(8,128)S(1)}) custom-call(f32[3,3,27]{2,1,0:T(4,128)S(1)} %bitcast.9, bf16[288,864]{1,0:T(8,128)(2,1)S(1)} %matrix.1.packed, f32[2,3,2,32,128]{4,3,2,1,0:T(8,128)S(1)} %get-tuple-element.33.load_ref, f32[2,3,2,32,128]{4,3,2,1,0:T(8,128)S(1)} %collective-permute-done.10.even_ref, ...), custom_call_target="tpu_custom_call" | custom-call | flops 764411904 | bytes 1586124 | tf_op jit(solution)/shard_map/sweep/pallas_call | solution.py:272
  68.1 3.1 %collective-permute-done.14.refs_4_ = f32[2,3,2,32,128]{4,3,2,1,0:T(8,128)S(1)} collective-permute-done((f32[2,3,2,32,128]{4,3,2,1,0:T(8,128)S(1)}, f32[2,3,2,32,128]{4,3,2,1,0:T(8,128)S(1)}, u32[]{:S(2)}, u32[]{:S(2)}) %collective-permute-start.14) | collective-permute-done | bytes 196640 | tf_op jit(solution)/shard_map/ppermute | solution.py:306
  75.4 6.3 %collective-permute-done.16 = f32[2,3,2,32,128]{4,3,2,1,0:T(8,128)S(1)} collective-permute-done((f32[2,3,2,32,128]{4,3,2,1,0:T(8,128)S(1)}, f32[2,3,2,32,128]{4,3,2,1,0:T(8,128)S(1)}, u32[]{:S(2)}, u32[]{:S(2)}) %collective-permute-start.16) | collective-permute-done | bytes 196640 | tf_op jit(solution)/shard_map/ppermute | solution.py:306
  83.3 7.8 %collective-permute-done.18 = f32[2,3,2,32,128]{4,3,2,1,0:T(8,128)S(1)} collective-permute-done((f32[2,3,2,32,128]{4,3,2,1,0:T(8,128)S(1)}, f32[2,3,2,32,128]{4,3,2,1,0:T(8,128)S(1)}, u32[]{:S(2)}, u32[]{:S(2)}) %collective-permute-start.18) | collective-permute-done | bytes 196640 | tf_op jit(solution)/shard_map/ppermute | solution.py:306
  92.4 3.9 %collective-permute-done.20.refs_7_ = f32[2,3,2,32,128]{4,3,2,1,0:T(8,128)S(1)} collective-permute-done((f32[2,3,2,32,128]{4,3,2,1,0:T(8,128)S(1)}, f32[2,3,2,32,128]{4,3,2,1,0:T(8,128)S(1)}, u32[]{:S(2)}, u32[]{:S(2)}) %collective-permute-start.20) | collective-permute-done | bytes 196640 | tf_op jit(solution)/shard_map/ppermute | solution.py:306
  97.6 3.5 %collective-permute-start.22 = (f32[5,3,2,32,128]{4,3,2,1,0:T(8,128)S(1)}, f32[5,3,2,32,128]{4,3,2,1,0:T(8,128)S(1)}, u32[]{:S(2)}, u32[]{:S(2)}) collective-permute-start(f32[5,3,2,32,128]{4,3,2,1,0:T(8,128)S(1)} %loads.2.load_ref), channel_id=1, source_target_pairs={{8,16},{16,8},{9,17},{17,9},{10,18},{18,10},{11,19},{19,11},{12,20... | collective-permute-start | bytes 1474568 | tf_op jit(solution)/shard_map/ppermute | solution.py:288
  101.2 6.5 %collective-permute-done.22.odd_ref = f32[5,3,2,32,128]{4,3,2,1,0:T(8,128)S(1)} collective-permute-done((f32[5,3,2,32,128]{4,3,2,1,0:T(8,128)S(1)}, f32[5,3,2,32,128]{4,3,2,1,0:T(8,128)S(1)}, u32[]{:S(2)}, u32[]{:S(2)}) %collective-permute-start.22) | collective-permute-done | bytes 491552 | tf_op jit(solution)/shard_map/ppermute | solution.py:288
  107.8 5.4 %sweep.5 = (f32[5,3,2,32,128]{4,3,2,1,0:T(8,128)S(1)}, f32[5,3,2,32,128]{4,3,2,1,0:T(8,128)S(1)}) custom-call(f32[3,3,27]{2,1,0:T(4,128)S(1)} %bitcast.10, bf16[288,864]{1,0:T(8,128)(2,1)S(1)} %matrix.1.packed, f32[5,3,2,32,128]{4,3,2,1,0:T(8,128)S(1)} %loads.2.load_ref, f32[5,3,2,32,128]{4,3,2,1,0:T(8,128)S(1)} %collective-permute-done.21.even_ref, ...), custom_call_target="tpu_custom_call" | custom-call | flops 1911029760 | bytes 2470860 | tf_op jit(solution)/shard_map/sweep/pallas_call | solution.py:272
  115.1 4.3 %collective-permute-start.23 = (f32[5,3,2,32,128]{4,3,2,1,0:T(8,128)S(1)}, f32[5,3,2,32,128]{4,3,2,1,0:T(8,128)S(1)}, u32[]{:S(2)}, u32[]{:S(2)}) collective-permute-start(f32[5,3,2,32,128]{4,3,2,1,0:T(8,128)S(1)} %get-tuple-element.43.refs_0_), channel_id=1, source_target_pairs={{0,2},{1,3},{2,0},{3,1},{4,6},{5,7},{6,4},{7,5},{8,10},{9,11},{10,... | collective-permute-start | bytes 1474568 | tf_op jit(solution)/shard_map/ppermute | solution.py:306
  119.4 2.9 %collective-permute-done.25.refs_4_ = f32[5,3,2,32,128]{4,3,2,1,0:T(8,128)S(1)} collective-permute-done((f32[5,3,2,32,128]{4,3,2,1,0:T(8,128)S(1)}, f32[5,3,2,32,128]{4,3,2,1,0:T(8,128)S(1)}, u32[]{:S(2)}, u32[]{:S(2)}) %collective-permute-start.25) | collective-permute-done | bytes 491552 | tf_op jit(solution)/shard_map/ppermute | solution.py:306
  122.4 4.9 %collective-permute-done.23.refs_1_ = f32[5,3,2,32,128]{4,3,2,1,0:T(8,128)S(1)} collective-permute-done((f32[5,3,2,32,128]{4,3,2,1,0:T(8,128)S(1)}, f32[5,3,2,32,128]{4,3,2,1,0:T(8,128)S(1)}, u32[]{:S(2)}, u32[]{:S(2)}) %collective-permute-start.23) | collective-permute-done | bytes 491552 | tf_op jit(solution)/shard_map/ppermute | solution.py:306
  129.5 9.9 %collective-permute-done.27 = f32[5,3,2,32,128]{4,3,2,1,0:T(8,128)S(1)} collective-permute-done((f32[5,3,2,32,128]{4,3,2,1,0:T(8,128)S(1)}, f32[5,3,2,32,128]{4,3,2,1,0:T(8,128)S(1)}, u32[]{:S(2)}, u32[]{:S(2)}) %collective-permute-start.27) | collective-permute-done | bytes 491552 | tf_op jit(solution)/shard_map/ppermute | solution.py:306
  141.3 13.9 %collective-permute-done.29 = f32[5,3,2,32,128]{4,3,2,1,0:T(8,128)S(1)} collective-permute-done((f32[5,3,2,32,128]{4,3,2,1,0:T(8,128)S(1)}, f32[5,3,2,32,128]{4,3,2,1,0:T(8,128)S(1)}, u32[]{:S(2)}, u32[]{:S(2)}) %collective-permute-start.29) | collective-permute-done | bytes 491552 | tf_op jit(solution)/shard_map/ppermute | solution.py:306
  156.6 11.7 %collective-permute-done.31.refs_7_ = f32[5,3,2,32,128]{4,3,2,1,0:T(8,128)S(1)} collective-permute-done((f32[5,3,2,32,128]{4,3,2,1,0:T(8,128)S(1)}, f32[5,3,2,32,128]{4,3,2,1,0:T(8,128)S(1)}, u32[]{:S(2)}, u32[]{:S(2)}) %collective-permute-start.31) | collective-permute-done | bytes 491552 | tf_op jit(solution)/shard_map/ppermute | solution.py:306
  170.4 2.7 %collective-permute-start.33 = (f32[9,3,32,128]{3,2,1,0:T(8,128)S(1)}, f32[9,3,32,128]{3,2,1,0:T(8,128)S(1)}, u32[]{:S(2)}, u32[]{:S(2)}) collective-permute-start(f32[9,3,32,128]{3,2,1,0:T(8,128)S(1)} %get-tuple-element.54), channel_id=1, source_target_pairs={{8,16},{16,8},{9,17},{17,9},{10,18},{18,10},{11,19},{19,11},{12,20... | collective-permute-start | bytes 1327112 | tf_op jit(solution)/shard_map/ppermute | solution.py:288
  173.1 6.9 %collective-permute-done.33.odd_ref = f32[9,3,32,128]{3,2,1,0:T(8,128)S(1)} collective-permute-done((f32[9,3,32,128]{3,2,1,0:T(8,128)S(1)}, f32[9,3,32,128]{3,2,1,0:T(8,128)S(1)}, u32[]{:S(2)}, u32[]{:S(2)}) %collective-permute-start.33) | collective-permute-done | bytes 442400 | tf_op jit(solution)/shard_map/ppermute | solution.py:288
  180.0 3.6 %last_sweep.1 = f32[18,3,2,32,128]{4,3,2,1,0:T(8,128)} custom-call(s32[144]{0:T(256)S(1)} %copy-done.5, f32[3,3,27]{2,1,0:T(4,128)S(1)} %bitcast.11, bf16[288,864]{1,0:T(8,128)(2,1)S(1)} %matrix.1.packed, f32[9,3,2,32,128]{4,3,2,1,0:T(8,128)S(1)} %get-tuple-element.52.load_ref, f32[9,3,32,128]{3,2,1,0:T(8,128)S(1)} %collective-permute-done.32.even_ref, ...), custom_call_target="tpu_custom_call" | custom-call | flops 1146617856 | bytes 4044300 | tf_op jit(solution)/shard_map/last_sweep/pallas_call | solution.py:272
  (82 shorter events, 40.5 us)
Async XLA Ops:
  3.0 6.7 %collective-permute-start = (f32[2,3,2,32,128]{4,3,2,1,0:T(8,128)S(1)}, f32[2,3,2,32,128]{4,3,2,1,0:T(8,128)S(1)}, u32[]{:S(2)}, u32[]{:S(2)}) collective-permute-start(f32[2,3,2,32,128]{4,3,2,1,0:T(8,128)S(1)} %prologue.1), channel_id=1, source_target_pairs={{0,1},{1,0},{2,3},{3,2},{4,5},{5,4},{6,7},{7,6},{8,9},{9,8},{10,11... | collective-permute-start | bytes 589832 | tf_op jit(solution)/shard_map/ppermute | solution.py:338
  15.7 23.5 %collective-permute-start.7 = (f32[2,3,2,32,128]{4,3,2,1,0:T(8,128)S(1)}, f32[2,3,2,32,128]{4,3,2,1,0:T(8,128)S(1)}, u32[]{:S(2)}, u32[]{:S(2)}) collective-permute-start(f32[2,3,2,32,128]{4,3,2,1,0:T(8,128)S(1)} %pad_maximum_fusion.refs_0_), channel_id=1, source_target_pairs={{0,6},{1,7},{2,4},{3,5},{4,2},{5,3},{6,0},{7,1},{8,14},{9,15},{10,... | collective-permute-start | bytes 589832 | tf_op jit(solution)/shard_map/ppermute | solution.py:338
  16.8 22.4 %collective-permute-start.6 = (f32[2,3,2,32,128]{4,3,2,1,0:T(8,128)S(1)}, f32[2,3,2,32,128]{4,3,2,1,0:T(8,128)S(1)}, u32[]{:S(2)}, u32[]{:S(2)}) collective-permute-start(f32[2,3,2,32,128]{4,3,2,1,0:T(8,128)S(1)} %pad_maximum_fusion.refs_0_), channel_id=1, source_target_pairs={{0,4},{1,5},{2,6},{3,7},{4,0},{5,1},{6,2},{7,3},{8,12},{9,13},{10,... | collective-permute-start | bytes 589832 | tf_op jit(solution)/shard_map/ppermute | solution.py:338
  18.2 21.0 %collective-permute-start.5 = (f32[2,3,2,32,128]{4,3,2,1,0:T(8,128)S(1)}, f32[2,3,2,32,128]{4,3,2,1,0:T(8,128)S(1)}, u32[]{:S(2)}, u32[]{:S(2)}) collective-permute-start(f32[2,3,2,32,128]{4,3,2,1,0:T(8,128)S(1)} %pad_maximum_fusion.refs_0_), channel_id=1, source_target_pairs={{0,2},{1,3},{2,0},{3,1},{4,6},{5,7},{6,4},{7,5},{8,10},{9,11},{10,... | collective-permute-start | bytes 589832 | tf_op jit(solution)/shard_map/ppermute | solution.py:338
  19.3 18.0 %collective-permute-start.4 = (f32[1,3,2,32,128]{4,3,2,1,0:T(8,128)S(1)}, f32[1,3,2,32,128]{4,3,2,1,0:T(8,128)S(1)}, u32[]{:S(2)}, u32[]{:S(2)}) collective-permute-start(f32[1,3,2,32,128]{4,3,2,1,0:T(8,128)S(1)} %add.23.load_ref), channel_id=1, source_target_pairs={{8,16},{16,8},{9,17},{17,9},{10,18},{18,10},{11,19},{19,11},{12,20... | collective-permute-start | bytes 294920 | tf_op jit(solution)/shard_map/ppermute | solution.py:288
  40.1 10.1 %collective-permute-start.9 = (f32[5,3,2,32,128]{4,3,2,1,0:T(8,128)S(1)}, f32[5,3,2,32,128]{4,3,2,1,0:T(8,128)S(1)}, u32[]{:S(2)}, u32[]{:S(2)}) collective-permute-start(f32[5,3,2,32,128]{4,3,2,1,0:T(8,128)S(1)} %first_loads.1.load_ref), channel_id=1, source_target_pairs={{8,16},{16,8},{9,17},{17,9},{10,18},{18,10},{11,19},{19,11},{12,20... | collective-permute-start | bytes 1474568 | tf_op jit(solution)/shard_map/ppermute | solution.py:288
  43.4 6.8 %collective-permute-start.8 = (f32[5,3,2,32,128]{4,3,2,1,0:T(8,128)S(1)}, f32[5,3,2,32,128]{4,3,2,1,0:T(8,128)S(1)}, u32[]{:S(2)}, u32[]{:S(2)}) collective-permute-start(f32[5,3,2,32,128]{4,3,2,1,0:T(8,128)S(1)} %first_loads.1.load_ref), channel_id=1, source_target_pairs={{0,8},{8,0},{16,24},{24,16},{1,9},{9,1},{17,25},{25,17},{2,10},{10... | collective-permute-start | bytes 1474568 | tf_op jit(solution)/shard_map/ppermute | solution.py:288
  56.1 7.0 %collective-permute-start.11 = (f32[2,3,2,32,128]{4,3,2,1,0:T(8,128)S(1)}, f32[2,3,2,32,128]{4,3,2,1,0:T(8,128)S(1)}, u32[]{:S(2)}, u32[]{:S(2)}) collective-permute-start(f32[2,3,2,32,128]{4,3,2,1,0:T(8,128)S(1)} %get-tuple-element.33.load_ref), channel_id=1, source_target_pairs={{8,16},{16,8},{9,17},{17,9},{10,18},{18,10},{11,19},{19,11},{12,20... | collective-permute-start | bytes 589832 | tf_op jit(solution)/shard_map/ppermute | solution.py:288
  73.1 8.5 %collective-permute-start.16 = (f32[2,3,2,32,128]{4,3,2,1,0:T(8,128)S(1)}, f32[2,3,2,32,128]{4,3,2,1,0:T(8,128)S(1)}, u32[]{:S(2)}, u32[]{:S(2)}) collective-permute-start(f32[2,3,2,32,128]{4,3,2,1,0:T(8,128)S(1)} %collective-permute-done.13), channel_id=1, source_target_pairs={{2,0},{3,1},{4,6},{5,7},{10,8},{11,9},{12,14},{13,15},{18,16},{19,... | collective-permute-start | bytes 589832 | tf_op jit(solution)/shard_map/ppermute | solution.py:306
  74.4 7.3 %collective-permute-start.17 = (f32[2,3,2,32,128]{4,3,2,1,0:T(8,128)S(1)}, f32[2,3,2,32,128]{4,3,2,1,0:T(8,128)S(1)}, u32[]{:S(2)}, u32[]{:S(2)}) collective-permute-start(f32[2,3,2,32,128]{4,3,2,1,0:T(8,128)S(1)} %collective-permute-done.12.refs_1_), channel_id=1, source_target_pairs={{0,1},{1,0},{2,3},{3,2},{4,5},{5,4},{6,7},{7,6},{8,9},{9,8},{10,11... | collective-permute-start | bytes 589832 | tf_op jit(solution)/shard_map/ppermute | solution.py:306
  74.7 7.0 %collective-permute-start.15 = (f32[2,3,2,32,128]{4,3,2,1,0:T(8,128)S(1)}, f32[2,3,2,32,128]{4,3,2,1,0:T(8,128)S(1)}, u32[]{:S(2)}, u32[]{:S(2)}) collective-permute-start(f32[2,3,2,32,128]{4,3,2,1,0:T(8,128)S(1)} %collective-permute-done.12.refs_1_), channel_id=1, source_target_pairs={{2,4},{3,5},{4,2},{5,3},{10,12},{11,13},{12,10},{13,11},{18,20},{1... | collective-permute-start | bytes 589832 | tf_op jit(solution)/shard_map/ppermute | solution.py:306
  81.7 9.4 %collective-permute-start.18 = (f32[2,3,2,32,128]{4,3,2,1,0:T(8,128)S(1)}, f32[2,3,2,32,128]{4,3,2,1,0:T(8,128)S(1)}, u32[]{:S(2)}, u32[]{:S(2)}) collective-permute-start(f32[2,3,2,32,128]{4,3,2,1,0:T(8,128)S(1)} %collective-permute-done.15), channel_id=1, source_target_pairs={{2,0},{3,1},{4,6},{5,7},{10,8},{11,9},{12,14},{13,15},{18,16},{19,... | collective-permute-start | bytes 589832 | tf_op jit(solution)/shard_map/ppermute | solution.py:306
  83.0 8.1 %collective-permute-start.19 = (f32[2,3,2,32,128]{4,3,2,1,0:T(8,128)S(1)}, f32[2,3,2,32,128]{4,3,2,1,0:T(8,128)S(1)}, u32[]{:S(2)}, u32[]{:S(2)}) collective-permute-start(f32[2,3,2,32,128]{4,3,2,1,0:T(8,128)S(1)} %add.24.refs_2_), channel_id=1, source_target_pairs={{0,1},{1,0},{2,3},{3,2},{4,5},{5,4},{6,7},{7,6},{8,9},{9,8},{10,11... | collective-permute-start | bytes 589832 | tf_op jit(solution)/shard_map/ppermute | solution.py:306
  97.6 10.1 %collective-permute-start.22 = (f32[5,3,2,32,128]{4,3,2,1,0:T(8,128)S(1)}, f32[5,3,2,32,128]{4,3,2,1,0:T(8,128)S(1)}, u32[]{:S(2)}, u32[]{:S(2)}) collective-permute-start(f32[5,3,2,32,128]{4,3,2,1,0:T(8,128)S(1)} %loads.2.load_ref), channel_id=1, source_target_pairs={{8,16},{16,8},{9,17},{17,9},{10,18},{18,10},{11,19},{19,11},{12,20... | collective-permute-start | bytes 1474568 | tf_op jit(solution)/shard_map/ppermute | solution.py:288
  113.2 9.2 %collective-permute-start.25 = (f32[5,3,2,32,128]{4,3,2,1,0:T(8,128)S(1)}, f32[5,3,2,32,128]{4,3,2,1,0:T(8,128)S(1)}, u32[]{:S(2)}, u32[]{:S(2)}) collective-permute-start(f32[5,3,2,32,128]{4,3,2,1,0:T(8,128)S(1)} %get-tuple-element.43.refs_0_), channel_id=1, source_target_pairs={{0,1},{1,0},{2,3},{3,2},{4,5},{5,4},{6,7},{7,6},{8,9},{9,8},{10,11... | collective-permute-start | bytes 1474568 | tf_op jit(solution)/shard_map/ppermute | solution.py:306
  114.4 7.9 %collective-permute-start.24 = (f32[5,3,2,32,128]{4,3,2,1,0:T(8,128)S(1)}, f32[5,3,2,32,128]{4,3,2,1,0:T(8,128)S(1)}, u32[]{:S(2)}, u32[]{:S(2)}) collective-permute-start(f32[5,3,2,32,128]{4,3,2,1,0:T(8,128)S(1)} %get-tuple-element.43.refs_0_), channel_id=1, source_target_pairs={{2,4},{3,5},{4,2},{5,3},{10,12},{11,13},{12,10},{13,11},{18,20},{1... | collective-permute-start | bytes 1474568 | tf_op jit(solution)/shard_map/ppermute | solution.py:306
  115.1 12.1 %collective-permute-start.23 = (f32[5,3,2,32,128]{4,3,2,1,0:T(8,128)S(1)}, f32[5,3,2,32,128]{4,3,2,1,0:T(8,128)S(1)}, u32[]{:S(2)}, u32[]{:S(2)}) collective-permute-start(f32[5,3,2,32,128]{4,3,2,1,0:T(8,128)S(1)} %get-tuple-element.43.refs_0_), channel_id=1, source_target_pairs={{0,2},{1,3},{2,0},{3,1},{4,6},{5,7},{6,4},{7,5},{8,10},{9,11},{10,... | collective-permute-start | bytes 1474568 | tf_op jit(solution)/shard_map/ppermute | solution.py:306
  127.2 12.2 %collective-permute-start.27 = (f32[5,3,2,32,128]{4,3,2,1,0:T(8,128)S(1)}, f32[5,3,2,32,128]{4,3,2,1,0:T(8,128)S(1)}, u32[]{:S(2)}, u32[]{:S(2)}) collective-permute-start(f32[5,3,2,32,128]{4,3,2,1,0:T(8,128)S(1)} %collective-permute-done.24), channel_id=1, source_target_pairs={{2,0},{3,1},{4,6},{5,7},{10,8},{11,9},{12,14},{13,15},{18,16},{19,... | collective-permute-start | bytes 1474568 | tf_op jit(solution)/shard_map/ppermute | solution.py:306
  128.5 11.0 %collective-permute-start.28 = (f32[5,3,2,32,128]{4,3,2,1,0:T(8,128)S(1)}, f32[5,3,2,32,128]{4,3,2,1,0:T(8,128)S(1)}, u32[]{:S(2)}, u32[]{:S(2)}) collective-permute-start(f32[5,3,2,32,128]{4,3,2,1,0:T(8,128)S(1)} %collective-permute-done.23.refs_1_), channel_id=1, source_target_pairs={{0,1},{1,0},{2,3},{3,2},{4,5},{5,4},{6,7},{7,6},{8,9},{9,8},{10,11... | collective-permute-start | bytes 1474568 | tf_op jit(solution)/shard_map/ppermute | solution.py:306
  128.8 10.7 %collective-permute-start.26 = (f32[5,3,2,32,128]{4,3,2,1,0:T(8,128)S(1)}, f32[5,3,2,32,128]{4,3,2,1,0:T(8,128)S(1)}, u32[]{:S(2)}, u32[]{:S(2)}) collective-permute-start(f32[5,3,2,32,128]{4,3,2,1,0:T(8,128)S(1)} %collective-permute-done.23.refs_1_), channel_id=1, source_target_pairs={{2,4},{3,5},{4,2},{5,3},{10,12},{11,13},{12,10},{13,11},{18,20},{1... | collective-permute-start | bytes 1474568 | tf_op jit(solution)/shard_map/ppermute | solution.py:306
  139.5 15.7 %collective-permute-start.29 = (f32[5,3,2,32,128]{4,3,2,1,0:T(8,128)S(1)}, f32[5,3,2,32,128]{4,3,2,1,0:T(8,128)S(1)}, u32[]{:S(2)}, u32[]{:S(2)}) collective-permute-start(f32[5,3,2,32,128]{4,3,2,1,0:T(8,128)S(1)} %collective-permute-done.26), channel_id=1, source_target_pairs={{2,0},{3,1},{4,6},{5,7},{10,8},{11,9},{12,14},{13,15},{18,16},{19,... | collective-permute-start | bytes 1474568 | tf_op jit(solution)/shard_map/ppermute | solution.py:306
  141.0 14.3 %collective-permute-start.30 = (f32[5,3,2,32,128]{4,3,2,1,0:T(8,128)S(1)}, f32[5,3,2,32,128]{4,3,2,1,0:T(8,128)S(1)}, u32[]{:S(2)}, u32[]{:S(2)}) collective-permute-start(f32[5,3,2,32,128]{4,3,2,1,0:T(8,128)S(1)} %add.26.refs_2_), channel_id=1, source_target_pairs={{0,1},{1,0},{2,3},{3,2},{4,5},{5,4},{6,7},{7,6},{8,9},{9,8},{10,11... | collective-permute-start | bytes 1474568 | tf_op jit(solution)/shard_map/ppermute | solution.py:306
  155.3 13.0 %collective-permute-start.31 = (f32[5,3,2,32,128]{4,3,2,1,0:T(8,128)S(1)}, f32[5,3,2,32,128]{4,3,2,1,0:T(8,128)S(1)}, u32[]{:S(2)}, u32[]{:S(2)}) collective-permute-start(f32[5,3,2,32,128]{4,3,2,1,0:T(8,128)S(1)} %add.27.refs_3_), channel_id=1, source_target_pairs={{0,1},{1,0},{2,3},{3,2},{4,5},{5,4},{6,7},{7,6},{8,9},{9,8},{10,11... | collective-permute-start | bytes 1474568 | tf_op jit(solution)/shard_map/ppermute | solution.py:306
  170.4 9.6 %collective-permute-start.33 = (f32[9,3,32,128]{3,2,1,0:T(8,128)S(1)}, f32[9,3,32,128]{3,2,1,0:T(8,128)S(1)}, u32[]{:S(2)}, u32[]{:S(2)}) collective-permute-start(f32[9,3,32,128]{3,2,1,0:T(8,128)S(1)} %get-tuple-element.54), channel_id=1, source_target_pairs={{8,16},{16,8},{9,17},{17,9},{10,18},{18,10},{11,19},{19,11},{12,20... | collective-permute-start | bytes 1327112 | tf_op jit(solution)/shard_map/ppermute | solution.py:288
  (20 other events, 327.6 us)

commit v3 on v0

v3 whole, which is shorter than its diff:
```python
import functools
import math

import jax
import jax.numpy as jnp
import numpy as np
from jax import lax
from jax.experimental import pallas as pl
from jax.experimental.pallas import tpu as pltpu
from jax.sharding import PartitionSpec as P

DIMS = 5
DEGREE = 4
UNROLL = 5
F32 = jnp.float32
BF16 = jnp.bfloat16
ANY = pl.BlockSpec(memory_space=pl.ANY)
VMEM = pl.BlockSpec(memory_space=pltpu.VMEM)
HBM = pl.BlockSpec(memory_space=pltpu.HBM)
SMEM = pl.BlockSpec(memory_space=pltpu.SMEM)


def compositions(total, pieces_left):
    if pieces_left == 1:
        return [[total]]
    result = []
    for leading in range(total, -1, -1):
        for remainder in compositions(total - leading, pieces_left - 1):
            result.append([leading] + remainder)
    return result


def chaos_links():
    indices = []
    for level in range(DEGREE + 1):
        indices.extend(compositions(level, DIMS))
    lookup = {tuple(vector): number for number, vector in enumerate(indices)}
    dims = np.zeros((len(indices), DEGREE), np.int32)
    parents = np.full((len(indices), DEGREE), -1, np.int32)
    for number, vector in enumerate(indices):
        place = 0
        for dim in range(DIMS):
            if vector[dim] > 0:
                lowered = list(vector)
                lowered[dim] -= 1
                dims[number, place] = dim
                parents[number, place] = lookup[tuple(lowered)]
                place += 1
    return dims, parents


LINK_DIMS, LINK_PARENTS = chaos_links()
COUNTS = [math.comb(level + DIMS - 1, DIMS - 1) for level in range(DEGREE + 1)]
FIRSTS = [sum(COUNTS[:level]) for level in range(DEGREE + 1)]


def matrix_kernel(stencil_ref, packed_ref):
    fill_matrix(0, stencil_ref, packed_ref)


def fill_matrix(shift, stencil_ref, packed_ref):
    size = packed_ref.shape[1] // 3
    rows = size // 9
    out_rows = packed_ref.shape[0] // 9
    lane = lax.broadcasted_iota(jnp.int32, (out_rows, size), 1)
    step = lane % rows - lax.broadcasted_iota(jnp.int32, (out_rows, size), 0) + (1 - shift)
    column = lane // rows
    for oz in range(3):
        for a in range(3):
            block = jnp.zeros((out_rows, size), F32)
            for oy in range(3):
                taps = jnp.zeros((out_rows, size), F32)
                for ox in range(3):
                    for b in range(3):
                        taps = jnp.where(column == 3 * ox + b, stencil_ref[a, b, 9 * ox + 3 * oy + oz], taps)
                block = jnp.where(step == oy, taps, block)
            high = block.astype(BF16)
            place = pl.ds((3 * oz + a) * out_rows, out_rows)
            packed_ref[place, :size] = high
            packed_ref[place, size : 2 * size] = high
            packed_ref[place, 2 * size :] = (block - high.astype(F32)).astype(BF16)


def put_split(value, high_ref, low_ref, place):
    high = value.astype(BF16)
    high_ref[place] = high
    low_ref[place] = (value - high.astype(F32)).astype(BF16)


def apply_pair(high_ref, low_ref, packed_ref, place):
    def window(ref):
        return [jnp.concatenate([ref[place + k], ref[place + k + 1]], axis=1) for k in range(3)]

    high = window(high_ref)
    operand = jnp.concatenate(high + window(low_ref) + high, axis=0)
    product = jnp.dot(packed_ref[...], operand, preferred_element_type=F32)
    lanes = high_ref.shape[2]
    size = packed_ref.shape[0] // 3
    lane = lax.broadcasted_iota(jnp.int32, (size, lanes), 1)
    results = []
    for half in range(2):
        block = product[:, half * lanes : (half + 1) * lanes]
        before = pltpu.roll(block[:size], 1, 1)
        after = pltpu.roll(block[2 * size :], lanes - 1, 1)
        results.append(block[size : 2 * size] + jnp.where(lane > 0, before, 0.0) + jnp.where(lane < lanes - 1, after, 0.0))
    return results


def start_copies(sources, targets, semaphores):
    copies = [pltpu.make_async_copy(source, target, semaphores.at[i]) for i, (source, target) in enumerate(zip(sources, targets, strict=True))]
    for copy in copies:
        copy.start()
    return copies


def eight(rows):
    return (rows + 7) // 8 * 8


def inverse_pivots(stencil_ref, rows, lanes):
    return jnp.concatenate([1.0 / jnp.full((rows, lanes), stencil_ref[a, a, 13], F32) for a in range(3)], axis=0)


def edge_flags():
    slab = lax.axis_index("space")
    return slab % 2 == 0, slab > 0, slab < lax.axis_size("space") - 1


def window(start, width, rows):
    first = max(start, 0)
    last = min(start + width, rows)
    return first, first - start, last - first


def fields_window(own, halo, fields_ref, out):
    group = lax.axis_index("terms")
    rows, lanes = fields_ref.shape[2:]
    width = own + 2 * halo
    for case in range(lax.axis_size("terms")):

        @pl.when(group == case)
        def _():
            first, place, length = window(own * case - halo, width, rows)
            for dim in range(DIMS):
                for plane in range(6):
                    base = plane * width
                    if place:
                        out[dim, base : base + place] = jnp.zeros((place, lanes), F32)
                    out[dim, base + place : base + place + length] = fields_ref[dim, plane % 2, first : first + length]
                    if place + length < width:
                        out[dim, base + place + length : base + width] = jnp.zeros((width - place - length, lanes), F32)


def places(place, start, cap, stride, offset, groups, slot_dev, slot_ref):
    for source in range(groups):
        for slot in range(cap):
            term = slot_ref[source * slot_dev + start + slot]
            place[jnp.where(term >= 0, term, 127)] = source * stride + offset + slot


def own_kernel(own, first, layout, stencil_ref, packed, forcing_ref, even_ref, odd_ref, settled_ref, out_ref, image, high, low, high2, low2):
    rows, lanes = forcing_ref.shape[3:]
    size = 3 * rows
    groups = out_ref.shape[0]
    inverse = inverse_pivots(stencil_ref, rows, lanes)
    is_even, has_lower, has_upper = edge_flags()

    def load(number, x):
        slot = first + number
        if 2 <= x < 4:
            return forcing_ref[slot, :, x - 2].reshape(size, lanes)
        even = even_ref[slot, :, x % 2].reshape(size, lanes)
        odd = odd_ref[slot, :, x % 2].reshape(size, lanes)
        return jnp.where(is_even, odd, even) if x < 2 else jnp.where(is_even, even, odd)

    for number in range(len(layout)):
        for x in range(6):
            put_split(load(number, x) * inverse, high.at[number], low.at[number], x)
    for number in range(len(layout)):
        for pair in range(2):
            applied = apply_pair(high.at[number], low.at[number], packed, 2 * pair)
            for half in range(2):
                x = 2 * pair + half + 1
                load_x = load(number, x)
                value = load_x * inverse + (load_x - applied[half]) * inverse
                if x == 1:
                    value = jnp.where(has_lower, value, 0.0)
                if x == 4:
                    value = jnp.where(has_upper, value, 0.0)
                if 2 <= x < 4:
                    settled_ref[number, :, x - 2] = value.reshape(3, rows, lanes)
                put_split(value, high2.at[number], low2.at[number], x - 1)
    for number, (halo, row) in enumerate(layout):
        applied = apply_pair(high2.at[number], low2.at[number], packed, 0)
        for x in range(2):
            image[number, x] = applied[x]
        width = own + 2 * halo
        for group in range(groups):
            begin, place, length = window(own * group - halo, width, rows)
            for plane in range(6):
                target = row + plane * width
                start = plane // 2 * rows + begin
                if place:
                    out_ref[group, target : target + place] = jnp.zeros((place, lanes), F32)
                out_ref[group, target + place : target + place + length] = image[number, plane % 2, start : start + length]
                if place + length < width:
                    out_ref[group, target + place + length : target + width] = jnp.zeros((width - place - length, lanes), F32)


def own_last_kernel(first, stencil_ref, packed, forcing_ref, even_ref, odd_ref, settled_ref, high, low):
    rows, lanes = forcing_ref.shape[3:]
    size = 3 * rows
    inverse = inverse_pivots(stencil_ref, rows, lanes)
    is_even = edge_flags()[0]
    for number in range(settled_ref.shape[0]):
        even = even_ref[number].reshape(size, lanes)
        odd = odd_ref[number].reshape(size, lanes)
        put_split(jnp.where(is_even, odd, even) * inverse, high.at[number], low.at[number], 0)
        put_split(jnp.where(is_even, even, odd) * inverse, high.at[number], low.at[number], 3)
        for x in range(2):
            put_split(forcing_ref[first + number, :, x].reshape(size, lanes) * inverse, high.at[number], low.at[number], x + 1)
        applied = apply_pair(high.at[number], low.at[number], packed, 0)
        for x in range(2):
            load = forcing_ref[first + number, :, x].reshape(size, lanes)
            value = load * inverse + (load - applied[x]) * inverse
            settled_ref[number, :, x] = value.reshape(3, rows, lanes)


def first_kernel(own, halo, groups, slot_dev, slot_ref, coupling_ref, fields_ref, image_ref, next_ref, modes):
    fields_window(own, halo, fields_ref, modes)
    source = jnp.int32(0)
    for group in range(groups):
        source = jnp.where(slot_ref[group * slot_dev] >= 0, group, source)
    rows = next_ref.shape[1]
    image = image_ref[source, :rows]
    for dim in range(DIMS):
        next_ref[dim] = -(modes[dim] * coupling_ref[dim, dim + 1]) * image


def level_kernel(level, own, halo, rows, caps, starts, base, slot_dev, slot_ref, coupling_ref, stencil_ref, load_hbm, even_hbm, odd_hbm, fields_ref, image_ref, *refs):
    load_ref, even_ref, odd_ref, semaphores, modes, packed, packed2, images, in_place, out_place, ext, ext2, high, low, high2, low2 = refs[-16:]
    olds = refs[:1] if level > 1 else ()
    copies = start_copies((load_hbm, even_hbm, odd_hbm), (load_ref, even_ref, odd_ref), semaphores)
    settled_ref, next_ref, *pieces = refs[len(olds) : -16]
    groups = lax.axis_size("terms")
    group = lax.axis_index("terms")
    lanes = load_ref.shape[2]
    width = own + 2 * halo
    height, height2, height3 = eight(width), eight(width - 2), eight(width - 4)
    next_width = width - 4
    offset = sum(caps[1:level])
    stride = offset + caps[level]
    places(in_place, starts[level], caps[level], caps[level], 0, groups, slot_dev, slot_ref)
    places(out_place, starts[level], caps[level], stride, offset, groups, slot_dev, slot_ref)
    inverse = inverse_pivots(stencil_ref, height, lanes)
    inverse2 = inverse_pivots(stencil_ref, height2, lanes)
    place = lax.broadcasted_iota(jnp.int32, (3 * height2, lanes), 0) % height2 + (own * group - halo + 1)
    inside = ((place >= 0) & (place < rows)).astype(F32)
    is_even, has_lower, has_upper = edge_flags()
    ext[...] = jnp.zeros(ext.shape, F32)
    ext2[...] = jnp.zeros(ext2.shape, F32)
    fill_matrix(1, stencil_ref, packed)
    fill_matrix(1, stencil_ref, packed2)
    fields_window(own, halo - 2, fields_ref, modes)
    for copy in copies:
        copy.wait()
    for old_ref in olds:
        for source in range(groups):
            settled_ref[source * stride : source * stride + offset] = old_ref[source * offset : (source + 1) * offset]

    def plane_of(ref, term, a, x):
        start = (2 * a + x) * width
        return ref[term, start : start + width]

    def terms(step, carry):
        lanes_of = [(lane, step * UNROLL + lane) for lane in range(UNROLL)]
        for lane, term in lanes_of:
            for x in range(6):
                for a in range(3):
                    if 2 <= x < 4:
                        value = plane_of(load_ref, term, a, x - 2)
                    else:
                        even, odd = plane_of(even_ref, term, a, x % 2), plane_of(odd_ref, term, a, x % 2)
                        value = jnp.where(is_even, odd, even) if x < 2 else jnp.where(is_even, even, odd)
                    ext[lane, x, a * height : a * height + width] = value
                    if 1 <= x < 5:
                        ext2[lane, x - 1, a * height2 : a * height2 + width - 2] = value[1 : width - 1]
                put_split(ext[lane, x] * inverse, high.at[lane], low.at[lane], x)
        for lane, term in lanes_of:
            out_slot = out_place[FIRSTS[level] + term]
            for pair in range(2):
                applied = apply_pair(high.at[lane], low.at[lane], packed, 2 * pair)
                for half in range(2):
                    x = 2 * pair + half
                    load = ext2[lane, x]
                    value = (load * inverse2 + (load - applied[half]) * inverse2) * inside
                    if x == 0:
                        value = jnp.where(has_lower, value, 0.0)
                    if x == 3:
                        value = jnp.where(has_upper, value, 0.0)
                    if 1 <= x < 3:
                        for a in range(3):
                            plane = 2 * a + x - 1
                            begin = a * height2 + halo - 1
                            settled_ref[out_slot, plane * own : (plane + 1) * own] = value[begin : begin + own]
                    put_split(value, high2.at[lane], low2.at[lane], x)
        for lane, term in lanes_of:
            in_slot = in_place[FIRSTS[level] + term]
            applied = apply_pair(high2.at[lane], low2.at[lane], packed2, 0)
            for a in range(3):
                for x in range(2):
                    begin = (2 * a + x) * next_width
                    part = pl.ds(begin, next_width)
                    images[term, part] = applied[x][a * height3 : a * height3 + next_width] + image_ref[in_slot, pl.ds(base + begin, next_width)]
        return carry

    lax.fori_loop(0, COUNTS[level] // UNROLL, terms, 0)

    for child in range(COUNTS[level + 1]):
        number = FIRSTS[level + 1] + child
        total = 0.0
        for dim, parent in zip(LINK_DIMS[number], LINK_PARENTS[number], strict=True):
            if parent >= 0:
                total = total - (modes[int(dim)] * coupling_ref[int(dim), number]) * images[int(parent) - FIRSTS[level]]
        next_ref[child] = total
    if pieces:

        def cut(pair, carry):
            for lane in range(2):
                for a in range(3):
                    layers = [next_ref[2 * pair + lane, (2 * a + x) * next_width : (2 * a + x + 1) * next_width] for x in range(2)]
                    begin = (3 * lane + a) * next_width
                    pieces[0][pair, begin : begin + next_width] = jnp.where(is_even, layers[1], layers[0])
                    pieces[1][pair, begin : begin + next_width] = jnp.where(is_even, layers[0], layers[1])
            return carry

        lax.fori_loop(0, COUNTS[level + 1] // 2, cut, 0)


def last_kernel(own, caps, starts, slot_dev, slot_ref, stencil_ref, load_hbm, even_hbm, odd_hbm, settled_ref, load_ref, even_ref, odd_ref, semaphores, packed, place, ext, high, low):
    groups = lax.axis_size("terms")
    lanes = load_ref.shape[2]
    width = own + 2
    height, height2 = eight(width), eight(own)
    places(place, starts[DEGREE], caps[DEGREE], caps[DEGREE], 0, groups, slot_dev, slot_ref)
    inverse = inverse_pivots(stencil_ref, height, lanes)
    is_even = edge_flags()[0]
    copies = start_copies((load_hbm, even_hbm, odd_hbm), (load_ref, even_ref, odd_ref), semaphores)
    ext[...] = jnp.zeros(ext.shape, F32)
    fill_matrix(1, stencil_ref, packed)
    for copy in copies:
        copy.wait()

    def terms(step, carry):
        for lane in range(2 * UNROLL):
            term = step * 2 * UNROLL + lane
            pair = step * UNROLL + lane // 2
            for a in range(3):
                begin = (3 * (lane % 2) + a) * width
                even = even_ref[pair, begin : begin + width]
                odd = odd_ref[pair, begin : begin + width]
                ext[lane, 0, a * height : a * height + width] = jnp.where(is_even, odd, even)
                ext[lane, 3, a * height : a * height + width] = jnp.where(is_even, even, odd)
                for x in range(2):
                    begin = (2 * a + x) * width
                    ext[lane, x + 1, a * height : a * height + width] = load_ref[term, begin : begin + width]
            for x in range(4):
                put_split(ext[lane, x] * inverse, high.at[lane], low.at[lane], x)
        for lane in range(2 * UNROLL):
            term = step * 2 * UNROLL + lane
            applied = apply_pair(high.at[lane], low.at[lane], packed, 0)
            slot = place[FIRSTS[DEGREE] + term]
            for a in range(3):
                scale = inverse[a * height : a * height + own]
                for x in range(2):
                    begin = (2 * a + x) * width + 1
                    load = load_ref[term, begin : begin + own]
                    plane = 2 * a + x
                    settled_ref[slot, plane * own : (plane + 1) * own] = load * scale + (load - applied[x][a * height2 : a * height2 + own]) * scale
        return carry

    lax.fori_loop(0, COUNTS[DEGREE] // (2 * UNROLL), terms, 0)


def assemble_kernel(own, starts, slot_ref, *refs):
    out_ref = refs[-1]
    parts = refs[: DEGREE + 1]
    links = refs[DEGREE + 1 : -1]
    slot_dev, _, _, rows, lanes = out_ref.shape
    groups = rows // own
    first = lax.axis_index("terms") * slot_dev
    out_ref[0] = jnp.where(slot_ref[first] >= 0, parts[0][0], 0.0)
    for level in range(1, DEGREE + 1):
        ref = links[level // DEGREE]
        offset = starts[level] - starts[1] if level < DEGREE else 0
        for slot in range(parts[level].shape[0]):
            filled = slot_ref[first + starts[level] + slot] >= 0
            for plane in range(6):
                begin = ((offset + slot) * 6 + plane) * own
                value = jnp.concatenate([ref[group, begin : begin + own] for group in range(groups)], axis=0)
                value = value + parts[level][slot, plane // 2, plane % 2]
                out_ref[starts[level] + slot, plane // 2, plane % 2] = jnp.where(filled, value, 0.0)


def call(kernel, out_shape, specs, scratch, operands, name, flops=0, megabytes=12):
    single = not isinstance(out_shape, list)
    return pl.pallas_call(
        kernel,
        out_shape=out_shape,
        in_specs=specs,
        out_specs=VMEM if single else [VMEM] * len(out_shape),
        scratch_shapes=scratch,
        compiler_params=pltpu.CompilerParams(vmem_limit_bytes=megabytes * 2**20),
        cost_estimate=pl.CostEstimate(flops=flops, bytes_accessed=sum(4 * math.prod(o.shape) for o in operands), transcendentals=0),
        name=name,
    )(*operands)


def beside(array, axis):
    count = lax.axis_size(axis)
    even = [(i, i ^ 1) for i in range(count)]
    odd = [(i, ((i + 1) ^ 1) - 1) for i in range(1, count - 1)]
    return lax.ppermute(array[0], axis, even), lax.ppermute(array[1], axis, odd)


def exchange(blocks):
    return lax.all_to_all(blocks, "terms", 0, 0, tiled=True)


def on_device(forcing, stencil, fields, coupling, slot_term):
    groups = lax.axis_size("terms")
    slot_dev = forcing.shape[0]
    caps = [(count + groups - 1) // groups for count in COUNTS]
    starts = [sum(caps[:level]) for level in range(DEGREE + 1)]
    rows, lanes = forcing.shape[3:]
    field = forcing.shape[1:]
    own = rows // groups
    halos = [None] + [2 * (DEGREE - level) + 1 for level in range(1, DEGREE + 1)]
    widths = [None] + [own + 2 * halo for halo in halos[1:]]
    strides = [None] + [eight(6 * width) for width in widths[1:]]

    def array(*shape):
        return jax.ShapeDtypeStruct(shape, F32)

    taps = jnp.transpose(stencil, (1, 2, 0))
    weights = coupling.T
    whole = call(matrix_kernel, jax.ShapeDtypeStruct((9 * rows, 27 * rows), BF16), [SMEM], [], [taps], "matrix")

    def splits(lead, layers, size):
        return [pltpu.VMEM((lead, layers, size, lanes), BF16)] * 2

    def own_part(slots, beside_pair, base, levels):
        layout, row = [], 0
        for level in levels:
            for _ in range(caps[level]):
                layout.append((halos[level + 1], row))
                row += strides[level + 1]
        count = len(layout)
        size = 3 * rows
        return call(
            functools.partial(own_kernel, own, starts[levels[0]] - base, layout),
            [pltpu.HBM((count, *field), F32), pltpu.HBM((groups, row, lanes), F32)],
            [SMEM] + [VMEM] * 4,
            [pltpu.VMEM((count, 2, size, lanes), F32)] + splits(count, 6, size) + splits(count, 4, size),
            [taps, whole, slots, *beside_pair],
            "own",
            count * 3 * 2 * 27 * size * size * 256,
        )

    front = forcing[: starts[2]]
    part01, packed = own_part(front, beside((front, front), "space"), 0, (0, 1))
    packed, forcing = lax.optimization_barrier((packed, forcing))
    back = forcing[starts[2] : starts[4]]
    back_pair = beside((back, back), "space")
    part2, packed2 = own_part(back, back_pair, starts[2], (2,))
    part3, packed3 = own_part(back, back_pair, starts[2], (3,))
    is_even = lax.axis_index("space") % 2 == 0
    layers = [forcing[starts[4] :, :, x] for x in range(2)]
    pieces = (jnp.where(is_even, layers[1], layers[0]), jnp.where(is_even, layers[0], layers[1]))
    front_images, packed2, packed3, last_pair = lax.optimization_barrier((exchange(packed), packed2, packed3, beside(pieces, "space")))
    part4 = call(
        functools.partial(own_last_kernel, starts[4]),
        pltpu.HBM((caps[4], *field), F32),
        [SMEM] + [VMEM] * 4,
        splits(caps[4], 4, 3 * rows),
        [taps, whole, forcing, *last_pair],
        "own_last",
        caps[4] * 2 * 27 * 9 * rows * rows * 256,
    )
    load = call(
        functools.partial(first_kernel, own, halos[1], groups, slot_dev),
        pltpu.HBM((DIMS, strides[1], lanes), F32),
        [SMEM] * 2 + [VMEM] * 2,
        [pltpu.VMEM((DIMS, strides[1], lanes), F32)],
        [slot_term, weights, fields, front_images],
        "first",
    )
    images = [None, front_images, None, None]
    waiting = [None, packed2, packed3]
    table = pltpu.SMEM((128,), jnp.int32)
    settled = []
    for level in range(1, DEGREE):
        height, height2 = eight(widths[level]), eight(widths[level] - 2)
        base = strides[1] if level == 1 else 0
        image = images[level].reshape(groups * (1 if level == 1 else caps[level]), -1, lanes)
        olds = settled
        total = sum(caps[1 : level + 1])
        shapes = [pltpu.HBM((groups * total, 6 * own, lanes), F32), pltpu.HBM((COUNTS[level + 1], strides[level + 1], lanes), F32)]
        if level == DEGREE - 1:
            shapes += [pltpu.HBM((COUNTS[DEGREE] // 2, 6 * widths[DEGREE], lanes), F32)] * 2
        size, size2 = 3 * height, 3 * height2
        even, odd = beside((load, load), "space")
        if level < 3:
            even, block = lax.optimization_barrier((even, waiting[level]))
            images[level + 1] = exchange(block)
        result, load, *pieces = call(
            functools.partial(level_kernel, level, own, halos[level], rows, caps, starts, base, slot_dev),
            shapes,
            [SMEM] * 3 + [HBM] * 3 + [VMEM] * (2 + len(olds)),
            [pltpu.VMEM((COUNTS[level], strides[level], lanes), F32)] * 3
            + [pltpu.SemaphoreType.DMA((3,)), pltpu.VMEM((DIMS, strides[level + 1], lanes), F32)]
            + [pltpu.VMEM((3 * size2, 9 * size), BF16), pltpu.VMEM((9 * eight(widths[level] - 4), 9 * size2), BF16)]
            + [pltpu.VMEM((COUNTS[level], strides[level + 1], lanes), F32), table, table]
            + [pltpu.VMEM((UNROLL, 6, size, lanes), F32), pltpu.VMEM((UNROLL, 4, size2, lanes), F32)]
            + splits(UNROLL, 6, size)
            + splits(UNROLL, 4, size2),
            [slot_term, weights, taps, load, even, odd, fields, image, *olds],
            "level",
            COUNTS[level] * 2 * 27 * size2 * (2 * size + size2) * 256,
            60,
        )
        settled = [result]
    middle = exchange(result.reshape(groups, -1, lanes))
    even, odd = beside(pieces, "space")
    height, height2 = eight(widths[DEGREE]), eight(own)
    result = call(
        functools.partial(last_kernel, own, caps, starts, slot_dev),
        pltpu.HBM((groups * caps[DEGREE], 6 * own, lanes), F32),
        [SMEM] * 2 + [HBM] * 3,
        [pltpu.VMEM((COUNTS[DEGREE], strides[DEGREE], lanes), F32)]
        + [pltpu.VMEM((COUNTS[DEGREE] // 2, 6 * widths[DEGREE], lanes), F32)] * 2
        + [pltpu.SemaphoreType.DMA((3,)), pltpu.VMEM((9 * height2, 27 * height), BF16), table, pltpu.VMEM((2 * UNROLL, 4, 3 * height, lanes), F32)] + splits(2 * UNROLL, 4, 3 * height),
        [slot_term, taps, load, even, odd],
        "level_last",
        COUNTS[DEGREE] * 2 * 27 * 9 * height * height2 * 256,
        60,
    )
    result, middle = lax.optimization_barrier((result, middle))
    final = exchange(result.reshape(groups, -1, lanes))
    return call(
        functools.partial(assemble_kernel, own, starts),
        array(*forcing.shape),
        [SMEM] + [VMEM] * (DEGREE + 3),
        [],
        [slot_term, part01[:1], part01[1:], part2, part3, part4, middle, final],
        "assemble",
    )


def solution(mesh):
    return jax.shard_map(
        on_device,
        mesh=mesh,
        in_specs=(
            P("terms", None, "space", None, None),
            P(),
            P(None, "space", None, None),
            P(),
            P(),
        ),
        out_specs=P("terms", None, "space", None, None),
        check_vma=False,
    )
```

time: 556 us -> 162 us (0.29); the launches traced: 547 us -> 160 us
  matrix products: 247 us -> 0 us
  waiting for transfers between devices: 136 us -> 44.9 us
  blocking collectives: 53.9 us -> 0 us
  Pallas kernels: 0 us -> 51.2 us
  between operations: 17.5 us -> 0.33 us
  local copies, waits for them, and re-layouts: 30.1 us -> 14.8 us
  starting transfers between devices: 58.4 us -> 49.1 us
    dot_general x255 -> x0, matrix products: 247 us -> none  [the longest x243 221 us: apply_stencil(): jnp.einsum('ab,sbxyz->saxyz', block_coef, window, precision=lax.Precision...]
    all_gather x2 -> x0, waiting for transfers between devices: 106 us -> none  [on_device(): piece = lax.all_gather(prev_image, 'terms', axis=0, tiled=True)]
    all_gather x2 -> x0, blocking collectives: 53.9 us -> none  [on_device(): piece = lax.all_gather(prev_image, 'terms', axis=0, tiled=True)]
    pallas_call x0 -> x11, Pallas kernels: none -> 51.2 us  [call(): pl.pallas_call(kernel, out_shape=out_shape, in_specs=specs, out_specs=VME...]
    ppermute x18 -> x14, starting transfers between devices: 58.3 us -> 23.3 us  [the longest x7 22.9 us: beside(): lax.ppermute(array[1], axis, odd)]
    all_to_all x0 -> x5, starting transfers between devices: none -> 25.8 us  [exchange(): return lax.all_to_all(blocks, 'terms', 0, 0, tiled=True)]
    slice x59 -> x3, local copies, waits for them, and re-layouts: 24.6 us -> 2.59 us  [the longest x1 1.6 us: on_device(): part01[1:]]
    all_to_all x0 -> x5, waiting for transfers between devices: none -> 13.1 us  [exchange(): return lax.all_to_all(blocks, 'terms', 0, 0, tiled=True)]
  transfers between devices with their start and end apart: 20 -> 19, of which waited for: 13 -> 6; matrix products, arithmetic and copies ran while one was open for 3% -> 1% of each run, Pallas kernels for 0% -> 20%
where the time goes in v3:
time: 162 us; the launch traced here: 160 us
  Pallas kernels  51.2 us (32%)
  starting transfers between devices  49.1 us (30%)
  waiting for transfers between devices  44.9 us (28%)
  local copies, waits for them, and re-layouts  14.8 us (9%)
    pallas_call x11, Pallas kernels, call(): pl.pallas_call(kernel, out_shape=out_shape, in_specs=specs, out_specs=VME...  51.2 us
    ppermute x7, waiting for transfers between devices, beside(): lax.ppermute(array[1], axis, odd)  31.8 us
    all_to_all x5, starting transfers between devices, exchange(): return lax.all_to_all(blocks, 'terms', 0, 0, tiled=True)  25.8 us
    ppermute x7, starting transfers between devices, beside(): lax.ppermute(array[1], axis, odd)  22.9 us
    all_to_all x5, waiting for transfers between devices, exchange(): return lax.all_to_all(blocks, 'terms', 0, 0, tiled=True)  13.1 us
    unnamed x50, local copies, waits for them, and re-layouts  12.2 us
  transfers between devices with their start and end apart: 19, of which 6 were waited for; matrix products, arithmetic and copies ran while one was open for 1% of the time, Pallas kernels for 20%

profile of v3, /device:TPU:1, one launch (start us, length us, event | category | flops | bytes accessed | tf_op | source)
XLA Modules:
  0.0 160.4 jit_solution(13775233327844885046)
XLA Ops:
  0.9 4.5 %collective-permute-start.1 = (f32[2,3,2,32,128]{4,3,2,1,0:T(8,128)S(1)}, f32[2,3,2,32,128]{4,3,2,1,0:T(8,128)S(1)}, u32[]{:S(2)}, u32[]{:S(2)}) collective-permute-start(f32[2,3,2,32,128]{4,3,2,1,0:T(8,128)S(1)} %slice.18.forcing_ref), channel_id=1, source_target_pairs={{8,16},{16,8},{9,17},{17,9},{10,18},{18,10},{11,19},{19,11},{12,20... | collective-permute-start | bytes 589832 | tf_op jit(solution)/shard_map/ppermute | solution.py:423
  8.8 3.1 %own.3 = (f32[2,3,2,32,128]{4,3,2,1,0:T(8,128)}, f32[8,200,128]{2,1,0:T(8,128)}) custom-call(f32[3,3,27]{2,1,0:T(4,128)S(1)} %bitcast.15, bf16[288,864]{1,0:T(8,128)(2,1)S(1)} %matrix.1.packed, f32[2,3,2,32,128]{4,3,2,1,0:T(8,128)S(1)} %slice.18.forcing_ref, f32[2,3,2,32,128]{4,3,2,1,0:T(8,128)S(1)} %collective-permute-done.even_ref, ...), custom_call_target="tpu_custom_call" | custom-call | flops 764411904 | bytes 1586124 | tf_op jit(solution)/shard_map/own/pallas_call | solution.py:407
  12.7 5.5 %all-to-all-start = ((f32[8,200,128]{2,1,0:T(8,128)}), f32[8,200,128]{2,1,0:T(8,128)S(1)}, u32[]{:S(2)}, u32[]{:S(2)}) async-start(f32[8,200,128]{2,1,0:T(8,128)} %get-tuple-element.37), calls=%async_computation | async-start | bytes 1638400 | tf_op jit(solution)/shard_map/all_to_all | solution.py:427
  18.3 3.9 %collective-permute-start.3 = (f32[7,3,2,32,128]{4,3,2,1,0:T(8,128)S(1)}, f32[7,3,2,32,128]{4,3,2,1,0:T(8,128)}, u32[]{:S(2)}, u32[]{:S(2)}) collective-permute-start(f32[7,3,2,32,128]{4,3,2,1,0:T(8,128)S(1)} %slice.21.forcing_ref), channel_id=1, source_target_pairs={{8,16},{16,8},{9,17},{17,9},{10,18},{18,10},{11,19},{19,11},{12,20... | collective-permute-start | bytes 2064392 | tf_op jit(solution)/shard_map/ppermute | solution.py:423
  24.5 6.6 %collective-permute-done.3.odd_ref = f32[7,3,2,32,128]{4,3,2,1,0:T(8,128)} collective-permute-done((f32[7,3,2,32,128]{4,3,2,1,0:T(8,128)S(1)}, f32[7,3,2,32,128]{4,3,2,1,0:T(8,128)}, u32[]{:S(2)}, u32[]{:S(2)}) %collective-permute-start.3) | collective-permute-done | bytes 688160 | tf_op jit(solution)/shard_map/ppermute | solution.py:423
  31.1 3.7 %own.4 = (f32[2,3,2,32,128]{4,3,2,1,0:T(8,128)}, f32[8,128,128]{2,1,0:T(8,128)}) custom-call(f32[3,3,27]{2,1,0:T(4,128)S(1)} %bitcast.16, bf16[288,864]{1,0:T(8,128)(2,1)S(1)} %copy-done.4, f32[7,3,2,32,128]{4,3,2,1,0:T(8,128)S(1)} %slice.21.forcing_ref, f32[7,3,2,32,128]{4,3,2,1,0:T(8,128)} %collective-permute-done.2.even_ref, ...), custom_call_target="tpu_custom_call" | custom-call | flops 764411904 | bytes 3060684 | tf_op jit(solution)/shard_map/own/pallas_call | solution.py:407
  34.8 5.0 %own.5 = (f32[5,3,2,32,128]{4,3,2,1,0:T(8,128)}, f32[8,200,128]{2,1,0:T(8,128)}) custom-call(f32[3,3,27]{2,1,0:T(4,128)S(1)} %bitcast.17, bf16[288,864]{1,0:T(8,128)(2,1)S(1)} %copy-done.4, f32[7,3,2,32,128]{4,3,2,1,0:T(8,128)S(1)} %slice.21.forcing_ref, f32[7,3,2,32,128]{4,3,2,1,0:T(8,128)} %collective-permute-done.2.even_ref, ...), custom_call_target="tpu_custom_call" | custom-call | flops 1911029760 | bytes 3060684 | tf_op jit(solution)/shard_map/own/pallas_call | solution.py:407
  42.9 3.4 %collective-permute-start.7 = (f32[5,112,128]{2,1,0:T(8,128)}, f32[5,112,128]{2,1,0:T(8,128)}, u32[]{:S(2)}, u32[]{:S(2)}) collective-permute-start(f32[5,112,128]{2,1,0:T(8,128)} %first.1.load_hbm), channel_id=1, source_target_pairs={{8,16},{16,8},{9,17},{17,9},{10,18},{18,10},{11,19},{19,11},{12,20... | collective-permute-start | bytes 860168 | tf_op jit(solution)/shard_map/ppermute | solution.py:423
  46.3 5.7 %all-to-all-start.1 = ((f32[8,128,128]{2,1,0:T(8,128)}), f32[8,128,128]{2,1,0:T(8,128)S(1)}, u32[]{:S(2)}, u32[]{:S(2)}) async-start(f32[8,128,128]{2,1,0:T(8,128)} %get-tuple-element.48), calls=%async_computation.1 | async-start | bytes 1048576 | tf_op jit(solution)/shard_map/all_to_all | solution.py:427
  52.1 5.0 %level.3 = (f32[8,24,128]{2,1,0:T(8,128)}, f32[15,88,128]{2,1,0:T(8,128)}) custom-call(s32[144]{0:T(256)} %slot_ref.11, f32[5,126]{1,0:T(8,128)} %bitcast.19, f32[3,3,27]{2,1,0:T(4,128)} %bitcast.10, f32[5,112,128]{2,1,0:T(8,128)} %first.1.load_hbm, f32[5,112,128]{2,1,0:T(8,128)} %copy-done.24, f32[5,112,128]{2,1,0:T(8,128)} %collective-permute-done.7.odd_hbm, ...), custom_call_target="tpu_custom_call" | custom-call | flops 637009920 | bytes 1847268 | tf_op jit(solution)/shard_map/level/pallas_call | solution.py:407
  57.2 2.5 %collective-permute-start.9 = (f32[15,88,128]{2,1,0:T(8,128)}, f32[15,88,128]{2,1,0:T(8,128)}, u32[]{:S(2)}, u32[]{:S(2)}) collective-permute-start(f32[15,88,128]{2,1,0:T(8,128)} %get-tuple-element.45.load_hbm), channel_id=1, source_target_pairs={{8,16},{16,8},{9,17},{17,9},{10,18},{18,10},{11,19},{19,11},{12,20... | collective-permute-start | bytes 2027528 | tf_op jit(solution)/shard_map/ppermute | solution.py:423
  59.7 6.3 %all-to-all-done.1 = f32[8,128,128]{2,1,0:T(8,128)S(1)} async-done(((f32[8,128,128]{2,1,0:T(8,128)}), f32[8,128,128]{2,1,0:T(8,128)S(1)}, u32[]{:S(2)}, u32[]{:S(2)}) %all-to-all-start.1) | async-done | bytes 524320 | tf_op jit(solution)/shard_map/all_to_all | solution.py:427
  66.0 3.6 %all-to-all-start.2 = ((f32[8,200,128]{2,1,0:T(8,128)}), f32[8,200,128]{2,1,0:T(8,128)S(1)}, u32[]{:S(2)}, u32[]{:S(2)}) async-start(f32[8,200,128]{2,1,0:T(8,128)} %get-tuple-element.51), calls=%async_computation.2 | async-start | bytes 1638400 | tf_op jit(solution)/shard_map/all_to_all | solution.py:427
  69.6 7.6 %level.4 = (f32[24,24,128]{2,1,0:T(8,128)}, f32[35,64,128]{2,1,0:T(8,128)}) custom-call(s32[144]{0:T(256)} %slot_ref.11, f32[5,126]{1,0:T(8,128)} %bitcast.20, f32[3,3,27]{2,1,0:T(4,128)} %bitcast.11, f32[15,88,128]{2,1,0:T(8,128)} %get-tuple-element.45.load_hbm, f32[15,88,128]{2,1,0:T(8,128)} %collective-permute-done.8.even_hbm, ...), custom_call_target="tpu_custom_call" | custom-call | flops 1433272320 | bytes 2818020 | tf_op jit(solution)/shard_map/level/pallas_call | solution.py:407
  77.2 2.9 %collective-permute-start.11 = (f32[35,64,128]{2,1,0:T(8,128)}, f32[35,64,128]{2,1,0:T(8,128)S(1)}, u32[]{:S(2)}, u32[]{:S(2)}) collective-permute-start(f32[35,64,128]{2,1,0:T(8,128)} %get-tuple-element.50.load_hbm), channel_id=1, source_target_pairs={{8,16},{16,8},{9,17},{17,9},{10,18},{18,10},{11,19},{19,11},{12,20... | collective-permute-start | bytes 3440648 | tf_op jit(solution)/shard_map/ppermute | solution.py:423
  80.2 14.3 %collective-permute-done.11.odd_hbm = f32[35,64,128]{2,1,0:T(8,128)S(1)} collective-permute-done((f32[35,64,128]{2,1,0:T(8,128)}, f32[35,64,128]{2,1,0:T(8,128)S(1)}, u32[]{:S(2)}, u32[]{:S(2)}) %collective-permute-start.11) | collective-permute-done | bytes 1146912 | tf_op jit(solution)/shard_map/ppermute | solution.py:423
  96.5 12.4 %level.5 = (f32[64,24,128]{2,1,0:T(8,128)}, f32[70,40,128]{2,1,0:T(8,128)}, f32[35,36,128]{2,1,0:T(8,128)}, f32[35,36,128]{2,1,0:T(8,128)}) custom-call(s32[144]{0:T(256)} %slot_ref.11, f32[5,126]{1,0:T(8,128)} %bitcast.21, f32[3,3,27]{2,1,0:T(4,128)} %bitcast.12, f32[35,64,128]{2,1,0:T(8,128)} %get-tuple-element.50.load_hbm, ...), custom_call_target="tpu_custom_call" | custom-call | flops 1393459200 | bytes 4722660 | tf_op jit(solution)/shard_map/level/pallas_call | solution.py:407
  108.9 5.4 %all-to-all-start.3 = ((f32[8,192,128]{2,1,0:T(8,128)}), f32[8,192,128]{2,1,0:T(8,128)S(1)}, u32[]{:S(2)}, u32[]{:S(2)}) async-start(f32[8,192,128]{2,1,0:T(8,128)} %bitcast.25), calls=%async_computation.3 | async-start | bytes 1572864 | tf_op jit(solution)/shard_map/all_to_all | solution.py:427
  114.3 3.5 %collective-permute-start.13 = (f32[35,36,128]{2,1,0:T(8,128)}, f32[35,36,128]{2,1,0:T(8,128)}, u32[]{:S(2)}, u32[]{:S(2)}) collective-permute-start(f32[35,36,128]{2,1,0:T(8,128)} %get-tuple-element.55), channel_id=1, source_target_pairs={{8,16},{16,8},{9,17},{17,9},{10,18},{18,10},{11,19},{19,11},{12,20... | collective-permute-start | bytes 1935368 | tf_op jit(solution)/shard_map/ppermute | solution.py:423
  117.9 9.3 %collective-permute-done.13.odd_hbm = f32[35,36,128]{2,1,0:T(8,128)} collective-permute-done((f32[35,36,128]{2,1,0:T(8,128)}, f32[35,36,128]{2,1,0:T(8,128)}, u32[]{:S(2)}, u32[]{:S(2)}) %collective-permute-start.13) | collective-permute-done | bytes 645152 | tf_op jit(solution)/shard_map/ppermute | solution.py:423
  127.2 6.8 %level_last.1 = f32[72,24,128]{2,1,0:T(8,128)} custom-call(s32[144]{0:T(256)} %slot_ref.11, f32[3,3,27]{2,1,0:T(4,128)} %bitcast.13, f32[70,40,128]{2,1,0:T(8,128)} %get-tuple-element.53.load_hbm, f32[35,36,128]{2,1,0:T(8,128)} %copy-done.21, f32[35,36,128]{2,1,0:T(8,128)} %collective-permute-done.13.odd_hbm), custom_call_target="tpu_custom_call" | custom-call | flops 557383680 | bytes 2725388 | tf_op jit(solution)/shard_map/level_last/pallas_call | solution.py:407
  134.1 5.6 %all-to-all-start.4 = ((f32[8,216,128]{2,1,0:T(8,128)}), f32[8,216,128]{2,1,0:T(8,128)S(1)}, u32[]{:S(2)}, u32[]{:S(2)}) async-start(f32[8,216,128]{2,1,0:T(8,128)} %bitcast.23), calls=%async_computation.4 | async-start | bytes 1769472 | tf_op jit(solution)/shard_map/all_to_all | solution.py:427
  144.3 3.3 %own_last.1.refs_4_ = f32[9,3,2,32,128]{4,3,2,1,0:T(8,128)} custom-call(f32[3,3,27]{2,1,0:T(4,128)S(1)} %bitcast.18, bf16[288,864]{1,0:T(8,128)(2,1)S(1)} %copy-done.5, f32[18,3,2,32,128]{4,3,2,1,0:T(8,128)S(1)} %copy-done.1, f32[9,3,32,128]{3,2,1,0:T(8,128)S(1)} %copy-done.19, f32[9,3,32,128]{3,2,1,0:T(8,128)S(1)} %copy-done.17), custom_call_target="tpu_custom_call" | custom-call | flops 1146617856 | bytes 3650508 | tf_op jit(solution)/shard_map/own_last/pallas_call | solution.py:407
  147.6 6.7 %all-to-all-done.4.refs_6_ = f32[8,216,128]{2,1,0:T(8,128)S(1)} async-done(((f32[8,216,128]{2,1,0:T(8,128)}), f32[8,216,128]{2,1,0:T(8,128)S(1)}, u32[]{:S(2)}, u32[]{:S(2)}) %all-to-all-start.4) | async-done | bytes 884768 | tf_op jit(solution)/shard_map/all_to_all | solution.py:427
  (79 shorter events, 23.3 us)
Async XLA Ops:
  0.9 7.9 %collective-permute-start.1 = (f32[2,3,2,32,128]{4,3,2,1,0:T(8,128)S(1)}, f32[2,3,2,32,128]{4,3,2,1,0:T(8,128)S(1)}, u32[]{:S(2)}, u32[]{:S(2)}) collective-permute-start(f32[2,3,2,32,128]{4,3,2,1,0:T(8,128)S(1)} %slice.18.forcing_ref), channel_id=1, source_target_pairs={{8,16},{16,8},{9,17},{17,9},{10,18},{18,10},{11,19},{19,11},{12,20... | collective-permute-start | bytes 589832 | tf_op jit(solution)/shard_map/ppermute | solution.py:423
  5.5 3.3 %collective-permute-start = (f32[2,3,2,32,128]{4,3,2,1,0:T(8,128)S(1)}, f32[2,3,2,32,128]{4,3,2,1,0:T(8,128)S(1)}, u32[]{:S(2)}, u32[]{:S(2)}) collective-permute-start(f32[2,3,2,32,128]{4,3,2,1,0:T(8,128)S(1)} %slice.18.forcing_ref), channel_id=1, source_target_pairs={{0,8},{8,0},{16,24},{24,16},{1,9},{9,1},{17,25},{25,17},{2,10},{10... | collective-permute-start | bytes 589832 | tf_op jit(solution)/shard_map/ppermute | solution.py:423
  7.3 10.9 %copy-start.1 = (f32[18,3,2,32,128]{4,3,2,1,0:T(8,128)S(1)}, f32[18,3,2,32,128]{4,3,2,1,0:T(8,128)}, u32[]{:S(2)}) copy-start(f32[18,3,2,32,128]{4,3,2,1,0:T(8,128)} %forcing_ref) | copy-start | bytes 5308420
  12.7 28.8 %all-to-all-start = ((f32[8,200,128]{2,1,0:T(8,128)}), f32[8,200,128]{2,1,0:T(8,128)S(1)}, u32[]{:S(2)}, u32[]{:S(2)}) async-start(f32[8,200,128]{2,1,0:T(8,128)} %get-tuple-element.37), calls=%async_computation | async-start | bytes 1638400 | tf_op jit(solution)/shard_map/all_to_all | solution.py:427
  18.2 12.9 %copy-start.11 = (f32[27,3,3]{0,2,1:T(4,128)S(1)}, f32[27,3,3]{0,2,1:T(4,128)}, u32[]{:S(2)}) copy-start(f32[27,3,3]{0,2,1:T(4,128)} %param.6) | copy-start | bytes 2920
  18.3 12.8 %collective-permute-start.3 = (f32[7,3,2,32,128]{4,3,2,1,0:T(8,128)S(1)}, f32[7,3,2,32,128]{4,3,2,1,0:T(8,128)}, u32[]{:S(2)}, u32[]{:S(2)}) collective-permute-start(f32[7,3,2,32,128]{4,3,2,1,0:T(8,128)S(1)} %slice.21.forcing_ref), channel_id=1, source_target_pairs={{8,16},{16,8},{9,17},{17,9},{10,18},{18,10},{11,19},{19,11},{12,20... | collective-permute-start | bytes 2064392 | tf_op jit(solution)/shard_map/ppermute | solution.py:423
  22.2 8.9 %collective-permute-start.2 = (f32[7,3,2,32,128]{4,3,2,1,0:T(8,128)S(1)}, f32[7,3,2,32,128]{4,3,2,1,0:T(8,128)}, u32[]{:S(2)}, u32[]{:S(2)}) collective-permute-start(f32[7,3,2,32,128]{4,3,2,1,0:T(8,128)S(1)} %slice.21.forcing_ref), channel_id=1, source_target_pairs={{0,8},{8,0},{16,24},{24,16},{1,9},{9,1},{17,25},{25,17},{2,10},{10... | collective-permute-start | bytes 2064392 | tf_op jit(solution)/shard_map/ppermute | solution.py:423
  22.4 17.4 %collective-permute-start.5 = (f32[9,3,32,128]{3,2,1,0:T(8,128)S(1)}, f32[9,3,32,128]{3,2,1,0:T(8,128)S(1)}, u32[]{:S(2)}, u32[]{:S(2)}) collective-permute-start(f32[9,3,32,128]{3,2,1,0:T(8,128)S(1)} %get-tuple-element.59), channel_id=1, source_target_pairs={{8,16},{16,8},{9,17},{17,9},{10,18},{18,10},{11,19},{19,11},{12,20... | collective-permute-start | bytes 1327112 | tf_op jit(solution)/shard_map/ppermute | solution.py:423
  24.5 16.1 %collective-permute-start.4 = (f32[9,3,32,128]{3,2,1,0:T(8,128)S(1)}, f32[9,3,32,128]{3,2,1,0:T(8,128)S(1)}, u32[]{:S(2)}, u32[]{:S(2)}) collective-permute-start(f32[9,3,32,128]{3,2,1,0:T(8,128)S(1)} %get-tuple-element.60), channel_id=1, source_target_pairs={{0,8},{8,0},{16,24},{24,16},{1,9},{9,1},{17,25},{25,17},{2,10},{10... | collective-permute-start | bytes 1327112 | tf_op jit(solution)/shard_map/ppermute | solution.py:423
  41.4 10.6 %copy-start = (f32[8,200,128]{2,1,0:T(8,128)}, f32[8,200,128]{2,1,0:T(8,128)S(1)}, u32[]{:S(2)}) copy-start(f32[8,200,128]{2,1,0:T(8,128)S(1)} %all-to-all-done.image_ref) | copy-start | bytes 2457604
  42.9 3.5 %collective-permute-start.6 = (f32[5,112,128]{2,1,0:T(8,128)}, f32[5,112,128]{2,1,0:T(8,128)S(1)}, u32[]{:S(2)}, u32[]{:S(2)}) collective-permute-start(f32[5,112,128]{2,1,0:T(8,128)} %first.1.load_hbm), channel_id=1, source_target_pairs={{0,8},{8,0},{16,24},{24,16},{1,9},{9,1},{17,25},{25,17},{2,10},{10... | collective-permute-start | bytes 860168 | tf_op jit(solution)/shard_map/ppermute | solution.py:423
  42.9 9.2 %collective-permute-start.7 = (f32[5,112,128]{2,1,0:T(8,128)}, f32[5,112,128]{2,1,0:T(8,128)}, u32[]{:S(2)}, u32[]{:S(2)}) collective-permute-start(f32[5,112,128]{2,1,0:T(8,128)} %first.1.load_hbm), channel_id=1, source_target_pairs={{8,16},{16,8},{9,17},{17,9},{10,18},{18,10},{11,19},{19,11},{12,20... | collective-permute-start | bytes 860168 | tf_op jit(solution)/shard_map/ppermute | solution.py:423
  46.3 19.6 %all-to-all-start.1 = ((f32[8,128,128]{2,1,0:T(8,128)}), f32[8,128,128]{2,1,0:T(8,128)S(1)}, u32[]{:S(2)}, u32[]{:S(2)}) async-start(f32[8,128,128]{2,1,0:T(8,128)} %get-tuple-element.48), calls=%async_computation.1 | async-start | bytes 1048576 | tf_op jit(solution)/shard_map/all_to_all | solution.py:427
  57.1 2.6 %collective-permute-start.8 = (f32[15,88,128]{2,1,0:T(8,128)}, f32[15,88,128]{2,1,0:T(8,128)}, u32[]{:S(2)}, u32[]{:S(2)}) collective-permute-start(f32[15,88,128]{2,1,0:T(8,128)} %get-tuple-element.45.load_hbm), channel_id=1, source_target_pairs={{0,8},{8,0},{16,24},{24,16},{1,9},{9,1},{17,25},{25,17},{2,10},{10... | collective-permute-start | bytes 2027528 | tf_op jit(solution)/shard_map/ppermute | solution.py:423
  57.2 12.4 %collective-permute-start.9 = (f32[15,88,128]{2,1,0:T(8,128)}, f32[15,88,128]{2,1,0:T(8,128)}, u32[]{:S(2)}, u32[]{:S(2)}) collective-permute-start(f32[15,88,128]{2,1,0:T(8,128)} %get-tuple-element.45.load_hbm), channel_id=1, source_target_pairs={{8,16},{16,8},{9,17},{17,9},{10,18},{18,10},{11,19},{19,11},{12,20... | collective-permute-start | bytes 2027528 | tf_op jit(solution)/shard_map/ppermute | solution.py:423
  66.0 29.6 %all-to-all-start.2 = ((f32[8,200,128]{2,1,0:T(8,128)}), f32[8,200,128]{2,1,0:T(8,128)S(1)}, u32[]{:S(2)}, u32[]{:S(2)}) async-start(f32[8,200,128]{2,1,0:T(8,128)} %get-tuple-element.51), calls=%async_computation.2 | async-start | bytes 1638400 | tf_op jit(solution)/shard_map/all_to_all | solution.py:427
  77.2 17.4 %collective-permute-start.11 = (f32[35,64,128]{2,1,0:T(8,128)}, f32[35,64,128]{2,1,0:T(8,128)S(1)}, u32[]{:S(2)}, u32[]{:S(2)}) collective-permute-start(f32[35,64,128]{2,1,0:T(8,128)} %get-tuple-element.50.load_hbm), channel_id=1, source_target_pairs={{8,16},{16,8},{9,17},{17,9},{10,18},{18,10},{11,19},{19,11},{12,20... | collective-permute-start | bytes 3440648 | tf_op jit(solution)/shard_map/ppermute | solution.py:423
  80.2 15.4 %collective-permute-start.10 = (f32[35,64,128]{2,1,0:T(8,128)}, f32[35,64,128]{2,1,0:T(8,128)}, u32[]{:S(2)}, u32[]{:S(2)}) collective-permute-start(f32[35,64,128]{2,1,0:T(8,128)} %get-tuple-element.50.load_hbm), channel_id=1, source_target_pairs={{0,8},{8,0},{16,24},{24,16},{1,9},{9,1},{17,25},{25,17},{2,10},{10... | collective-permute-start | bytes 3440648 | tf_op jit(solution)/shard_map/ppermute | solution.py:423
  108.9 25.2 %all-to-all-start.3 = ((f32[8,192,128]{2,1,0:T(8,128)}), f32[8,192,128]{2,1,0:T(8,128)S(1)}, u32[]{:S(2)}, u32[]{:S(2)}) async-start(f32[8,192,128]{2,1,0:T(8,128)} %bitcast.25), calls=%async_computation.3 | async-start | bytes 1572864 | tf_op jit(solution)/shard_map/all_to_all | solution.py:427
  114.3 3.5 %collective-permute-start.12 = (f32[35,36,128]{2,1,0:T(8,128)}, f32[35,36,128]{2,1,0:T(8,128)S(1)}, u32[]{:S(2)}, u32[]{:S(2)}) collective-permute-start(f32[35,36,128]{2,1,0:T(8,128)} %get-tuple-element.54), channel_id=1, source_target_pairs={{0,8},{8,0},{16,24},{24,16},{1,9},{9,1},{17,25},{25,17},{2,10},{10... | collective-permute-start | bytes 1935368 | tf_op jit(solution)/shard_map/ppermute | solution.py:423
  114.3 12.9 %collective-permute-start.13 = (f32[35,36,128]{2,1,0:T(8,128)}, f32[35,36,128]{2,1,0:T(8,128)}, u32[]{:S(2)}, u32[]{:S(2)}) collective-permute-start(f32[35,36,128]{2,1,0:T(8,128)} %get-tuple-element.55), channel_id=1, source_target_pairs={{8,16},{16,8},{9,17},{17,9},{10,18},{18,10},{11,19},{19,11},{12,20... | collective-permute-start | bytes 1935368 | tf_op jit(solution)/shard_map/ppermute | solution.py:423
  117.9 9.4 %copy-start.21 = (f32[35,36,128]{2,1,0:T(8,128)}, f32[35,36,128]{2,1,0:T(8,128)S(1)}, u32[]{:S(2)}) copy-start(f32[35,36,128]{2,1,0:T(8,128)S(1)} %collective-permute-done.12.even_hbm) | copy-start | bytes 1935364
  134.1 20.3 %all-to-all-start.4 = ((f32[8,216,128]{2,1,0:T(8,128)}), f32[8,216,128]{2,1,0:T(8,128)S(1)}, u32[]{:S(2)}, u32[]{:S(2)}) async-start(f32[8,216,128]{2,1,0:T(8,128)} %bitcast.23), calls=%async_computation.4 | async-start | bytes 1769472 | tf_op jit(solution)/shard_map/all_to_all | solution.py:427
  144.3 10.0 %copy-start.14 = (s32[144]{0:T(256)S(1)}, s32[144]{0:T(256)}, u32[]{:S(2)}) copy-start(s32[144]{0:T(256)} %slot_ref.11) | copy-start | bytes 1732
  (20 other events, 57.5 us)

commit v4 on v3

--- a/solution.py
+++ b/solution.py
@@ -132,7 +132,7 @@
     return first, first - start, last - first
 
 
-def fields_window(own, halo, fields_ref, out):
+def fields_window(own, halo, layers, fields_ref, out):
     group = lax.axis_index("terms")
     rows, lanes = fields_ref.shape[2:]
     width = own + 2 * halo
@@ -142,13 +142,23 @@
         def _():
             first, place, length = window(own * case - halo, width, rows)
             for dim in range(DIMS):
-                for plane in range(6):
+                for plane in range(3 * len(layers)):
                     base = plane * width
                     if place:
                         out[dim, base : base + place] = jnp.zeros((place, lanes), F32)
-                    out[dim, base + place : base + place + length] = fields_ref[dim, plane % 2, first : first + length]
+                    out[dim, base + place : base + place + length] = fields_ref[dim, layers[plane % len(layers)], first : first + length]
                     if place + length < width:
                         out[dim, base + place + length : base + width] = jnp.zeros((width - place - length, lanes), F32)
+
+
+def link_sums(level, coupling_ref, modes, image_of, out):
+    for child in range(COUNTS[level]):
+        number = FIRSTS[level] + child
+        total = 0.0
+        for dim, parent in zip(LINK_DIMS[number], LINK_PARENTS[number], strict=True):
+            if parent >= 0:
+                total = total - (modes[int(dim)] * coupling_ref[int(dim), number]) * image_of(int(parent) - FIRSTS[level - 1])
+        out[child] = total
 
 
 def places(place, start, cap, stride, offset, groups, slot_dev, slot_ref):
@@ -226,25 +236,28 @@
             settled_ref[number, :, x] = value.reshape(3, rows, lanes)
 
 
-def first_kernel(own, halo, groups, slot_dev, slot_ref, coupling_ref, fields_ref, image_ref, next_ref, modes):
-    fields_window(own, halo, fields_ref, modes)
+def first_kernel(groups, slot_dev, slot_ref, image_ref, out_ref):
     source = jnp.int32(0)
     for group in range(groups):
         source = jnp.where(slot_ref[group * slot_dev] >= 0, group, source)
-    rows = next_ref.shape[1]
-    image = image_ref[source, :rows]
-    for dim in range(DIMS):
-        next_ref[dim] = -(modes[dim] * coupling_ref[dim, dim + 1]) * image
-
-
-def level_kernel(level, own, halo, rows, caps, starts, base, slot_dev, slot_ref, coupling_ref, stencil_ref, load_hbm, even_hbm, odd_hbm, fields_ref, image_ref, *refs):
-    load_ref, even_ref, odd_ref, semaphores, modes, packed, packed2, images, in_place, out_place, ext, ext2, high, low, high2, low2 = refs[-16:]
+    out_ref[0] = image_ref[source, : out_ref.shape[1]]
+
+
+def level_kernel(level, own, halo, rows, caps, starts, base, slot_dev, slot_ref, coupling_ref, stencil_ref, own_hbm, even_hbm, odd_hbm, fields_hbm, fields_even, fields_odd, image_ref, *refs):
+    slabs, fields, semaphores, modes, loads, packed, packed2, in_place, out_place, ext, ext2, high, low, high2, low2 = refs[-15:]
     olds = refs[:1] if level > 1 else ()
-    copies = start_copies((load_hbm, even_hbm, odd_hbm), (load_ref, even_ref, odd_ref), semaphores)
-    settled_ref, next_ref, *pieces = refs[len(olds) : -16]
+    is_even, has_lower, has_upper = edge_flags()
+    side = jnp.where(is_even, 2, 0)
+    places_of = (1, side, 2 - side)
+    copies = start_copies(
+        (own_hbm, even_hbm, odd_hbm, fields_hbm, fields_even, fields_odd),
+        [slabs.at[place] for place in places_of] + [fields.at[place] for place in places_of],
+        semaphores,
+    )
+    settled_ref, images, *pieces = refs[len(olds) : -15]
     groups = lax.axis_size("terms")
     group = lax.axis_index("terms")
-    lanes = load_ref.shape[2]
+    lanes = images.shape[2]
     width = own + 2 * halo
     height, height2, height3 = eight(width), eight(width - 2), eight(width - 4)
     next_width = width - 4
@@ -256,32 +269,26 @@
     inverse2 = inverse_pivots(stencil_ref, height2, lanes)
     place = lax.broadcasted_iota(jnp.int32, (3 * height2, lanes), 0) % height2 + (own * group - halo + 1)
     inside = ((place >= 0) & (place < rows)).astype(F32)
-    is_even, has_lower, has_upper = edge_flags()
     ext[...] = jnp.zeros(ext.shape, F32)
     ext2[...] = jnp.zeros(ext2.shape, F32)
     fill_matrix(1, stencil_ref, packed)
     fill_matrix(1, stencil_ref, packed2)
-    fields_window(own, halo - 2, fields_ref, modes)
     for copy in copies:
         copy.wait()
+    for slab in range(3):
+        fields_window(own, halo, (0, 1), fields.at[slab], modes.at[slab])
+        link_sums(level, coupling_ref, modes.at[slab], lambda parent, slab=slab: slabs[slab, parent], loads.at[slab])
     for old_ref in olds:
         for source in range(groups):
             settled_ref[source * stride : source * stride + offset] = old_ref[source * offset : (source + 1) * offset]
-
-    def plane_of(ref, term, a, x):
-        start = (2 * a + x) * width
-        return ref[term, start : start + width]
 
     def terms(step, carry):
         lanes_of = [(lane, step * UNROLL + lane) for lane in range(UNROLL)]
         for lane, term in lanes_of:
             for x in range(6):
                 for a in range(3):
-                    if 2 <= x < 4:
-                        value = plane_of(load_ref, term, a, x - 2)
-                    else:
-                        even, odd = plane_of(even_ref, term, a, x % 2), plane_of(odd_ref, term, a, x % 2)
-                        value = jnp.where(is_even, odd, even) if x < 2 else jnp.where(is_even, even, odd)
+                    start = (2 * a + x % 2) * width
+                    value = loads[x // 2, term, start : start + width]
                     ext[lane, x, a * height : a * height + width] = value
                     if 1 <= x < 5:
                         ext2[lane, x - 1, a * height2 : a * height2 + width - 2] = value[1 : width - 1]
@@ -316,54 +323,52 @@
 
     lax.fori_loop(0, COUNTS[level] // UNROLL, terms, 0)
 
-    for child in range(COUNTS[level + 1]):
-        number = FIRSTS[level + 1] + child
-        total = 0.0
-        for dim, parent in zip(LINK_DIMS[number], LINK_PARENTS[number], strict=True):
-            if parent >= 0:
-                total = total - (modes[int(dim)] * coupling_ref[int(dim), number]) * images[int(parent) - FIRSTS[level]]
-        next_ref[child] = total
     if pieces:
-
-        def cut(pair, carry):
-            for lane in range(2):
-                for a in range(3):
-                    layers = [next_ref[2 * pair + lane, (2 * a + x) * next_width : (2 * a + x + 1) * next_width] for x in range(2)]
-                    begin = (3 * lane + a) * next_width
-                    pieces[0][pair, begin : begin + next_width] = jnp.where(is_even, layers[1], layers[0])
-                    pieces[1][pair, begin : begin + next_width] = jnp.where(is_even, layers[0], layers[1])
-            return carry
-
-        lax.fori_loop(0, COUNTS[level + 1] // 2, cut, 0)
-
-
-def last_kernel(own, caps, starts, slot_dev, slot_ref, stencil_ref, load_hbm, even_hbm, odd_hbm, settled_ref, load_ref, even_ref, odd_ref, semaphores, packed, place, ext, high, low):
+        for term in range(COUNTS[level]):
+            for a in range(3):
+                layers = [images[term, (2 * a + x) * next_width : (2 * a + x + 1) * next_width] for x in range(2)]
+                begin = (3 * (term % 4) + a) * next_width
+                pieces[0][term // 4, begin : begin + next_width] = jnp.where(is_even, layers[1], layers[0])
+                pieces[1][term // 4, begin : begin + next_width] = jnp.where(is_even, layers[0], layers[1])
+
+
+def last_kernel(own, caps, starts, slot_dev, slot_ref, coupling_ref, stencil_ref, own_hbm, even_hbm, odd_hbm, fields_hbm, fields_even, fields_odd, settled_ref, images, sides, fields, semaphores, modes, side_modes, loads, side_loads, packed, place, ext, high, low):
     groups = lax.axis_size("terms")
-    lanes = load_ref.shape[2]
+    lanes = settled_ref.shape[2]
     width = own + 2
     height, height2 = eight(width), eight(own)
+    side = jnp.where(edge_flags()[0], 1, 0)
+    copies = start_copies(
+        (own_hbm, even_hbm, odd_hbm, fields_hbm, fields_even, fields_odd),
+        (images, sides.at[side], sides.at[1 - side], fields.at[2], fields.at[side], fields.at[1 - side]),
+        semaphores,
+    )
     places(place, starts[DEGREE], caps[DEGREE], caps[DEGREE], 0, groups, slot_dev, slot_ref)
     inverse = inverse_pivots(stencil_ref, height, lanes)
-    is_even = edge_flags()[0]
-    copies = start_copies((load_hbm, even_hbm, odd_hbm), (load_ref, even_ref, odd_ref), semaphores)
     ext[...] = jnp.zeros(ext.shape, F32)
     fill_matrix(1, stencil_ref, packed)
     for copy in copies:
         copy.wait()
+    fields_window(own, 1, (0, 1), fields.at[2], modes)
+    link_sums(DEGREE, coupling_ref, modes, lambda parent: images[parent], loads)
+    for upper in range(2):
+
+        def side_image(parent, upper=upper):
+            begin = 3 * (parent % 4) * width
+            return sides[upper, parent // 4, begin : begin + 3 * width]
+
+        fields_window(own, 1, (1 - upper,), fields.at[upper], side_modes.at[upper])
+        link_sums(DEGREE, coupling_ref, side_modes.at[upper], side_image, side_loads.at[upper])
 
     def terms(step, carry):
         for lane in range(2 * UNROLL):
             term = step * 2 * UNROLL + lane
-            pair = step * UNROLL + lane // 2
             for a in range(3):
-                begin = (3 * (lane % 2) + a) * width
-                even = even_ref[pair, begin : begin + width]
-                odd = odd_ref[pair, begin : begin + width]
-                ext[lane, 0, a * height : a * height + width] = jnp.where(is_even, odd, even)
-                ext[lane, 3, a * height : a * height + width] = jnp.where(is_even, even, odd)
+                for upper in range(2):
+                    ext[lane, 3 * upper, a * height : a * height + width] = side_loads[upper, term, a * width : (a + 1) * width]
                 for x in range(2):
                     begin = (2 * a + x) * width
-                    ext[lane, x + 1, a * height : a * height + width] = load_ref[term, begin : begin + width]
+                    ext[lane, x + 1, a * height : a * height + width] = loads[term, begin : begin + width]
             for x in range(4):
                 put_split(ext[lane, x] * inverse, high.at[lane], low.at[lane], x)
         for lane in range(2 * UNROLL):
@@ -374,7 +379,7 @@
                 scale = inverse[a * height : a * height + own]
                 for x in range(2):
                     begin = (2 * a + x) * width + 1
-                    load = load_ref[term, begin : begin + own]
+                    load = loads[term, begin : begin + own]
                     plane = 2 * a + x
                     settled_ref[slot, plane * own : (plane + 1) * own] = load * scale + (load - applied[x][a * height2 : a * height2 + own]) * scale
         return carry
@@ -382,24 +387,45 @@
     lax.fori_loop(0, COUNTS[DEGREE] // (2 * UNROLL), terms, 0)
 
 
-def assemble_kernel(own, starts, slot_ref, *refs):
-    out_ref = refs[-1]
-    parts = refs[: DEGREE + 1]
-    links = refs[DEGREE + 1 : -1]
+def assemble_kernel(own, start, slot_ref, *refs):
+    *parts, links_ref, out_ref = refs
     slot_dev, _, _, rows, lanes = out_ref.shape
     groups = rows // own
     first = lax.axis_index("terms") * slot_dev
     out_ref[0] = jnp.where(slot_ref[first] >= 0, parts[0][0], 0.0)
-    for level in range(1, DEGREE + 1):
-        ref = links[level // DEGREE]
-        offset = starts[level] - starts[1] if level < DEGREE else 0
-        for slot in range(parts[level].shape[0]):
-            filled = slot_ref[first + starts[level] + slot] >= 0
+    begin = 1
+    for number, part in enumerate(parts):
+        skip = 1 if number == 0 else 0
+        for slot in range(part.shape[0] - skip):
+            filled = slot_ref[first + begin] >= 0
             for plane in range(6):
-                begin = ((offset + slot) * 6 + plane) * own
-                value = jnp.concatenate([ref[group, begin : begin + own] for group in range(groups)], axis=0)
-                value = value + parts[level][slot, plane // 2, plane % 2]
-                out_ref[starts[level] + slot, plane // 2, plane % 2] = jnp.where(filled, value, 0.0)
+                place = ((begin - 1) * 6 + plane) * own
+                value = part[skip + slot, plane // 2, plane % 2]
+                if begin < start:
+                    value = value + jnp.concatenate([links_ref[group, place : place + own] for group in range(groups)], axis=0)
+                out_ref[begin, plane // 2, plane % 2] = jnp.where(filled, value, 0.0)
+            begin += 1
+
+
+def finish_kernel(own, start, slot_ref, partial_ref, links_hbm, out_ref, block, links_ref, semaphores):
+    slot_dev = out_ref.shape[0]
+    rows = out_ref.shape[3]
+    count = slot_dev - start
+    groups = rows // own
+    first = lax.axis_index("terms") * slot_dev + start
+    copies = start_copies([links_hbm, *[partial_ref.at[start + slot] for slot in range(count)]], [links_ref, *[block.at[slot] for slot in range(count)]], semaphores)
+    copies.pop(0).wait()
+    back = [pltpu.make_async_copy(block.at[slot], out_ref.at[start + slot], semaphores.at[1 + slot]) for slot in range(count)]
+    for slot in range(count):
+        copies[slot].wait()
+        filled = slot_ref[first + slot] >= 0
+        for plane in range(6):
+            place = (slot * 6 + plane) * own
+            value = jnp.concatenate([links_ref[group, place : place + own] for group in range(groups)], axis=0)
+            block[slot, plane // 2, plane % 2] += jnp.where(filled, value, 0.0)
+        back[slot].start()
+    for copy in back:
+        copy.wait()
 
 
 def call(kernel, out_shape, specs, scratch, operands, name, flops=0, megabytes=12):
@@ -469,92 +495,111 @@
 
     front = forcing[: starts[2]]
     part01, packed = own_part(front, beside((front, front), "space"), 0, (0, 1))
-    packed, forcing = lax.optimization_barrier((packed, forcing))
-    back = forcing[starts[2] : starts[4]]
-    back_pair = beside((back, back), "space")
-    part2, packed2 = own_part(back, back_pair, starts[2], (2,))
-    part3, packed3 = own_part(back, back_pair, starts[2], (3,))
+    packed, forcing, fields = lax.optimization_barrier((packed, forcing, fields))
+    back2, back3 = forcing[starts[2] : starts[3]], forcing[starts[3] : starts[4]]
+    part2, packed2 = own_part(back2, beside((back2, back2), "space"), starts[2], (2,))
+    part3, packed3 = own_part(back3, beside((back3, back3), "space"), starts[3], (3,))
+    fields_pair = beside((fields, fields), "space")
     is_even = lax.axis_index("space") % 2 == 0
     layers = [forcing[starts[4] :, :, x] for x in range(2)]
-    pieces = (jnp.where(is_even, layers[1], layers[0]), jnp.where(is_even, layers[0], layers[1]))
-    front_images, packed2, packed3, last_pair = lax.optimization_barrier((exchange(packed), packed2, packed3, beside(pieces, "space")))
-    part4 = call(
-        functools.partial(own_last_kernel, starts[4]),
-        pltpu.HBM((caps[4], *field), F32),
-        [SMEM] + [VMEM] * 4,
-        splits(caps[4], 4, 3 * rows),
-        [taps, whole, forcing, *last_pair],
-        "own_last",
-        caps[4] * 2 * 27 * 9 * rows * rows * 256,
-    )
-    load = call(
-        functools.partial(first_kernel, own, halos[1], groups, slot_dev),
-        pltpu.HBM((DIMS, strides[1], lanes), F32),
-        [SMEM] * 2 + [VMEM] * 2,
-        [pltpu.VMEM((DIMS, strides[1], lanes), F32)],
-        [slot_term, weights, fields, front_images],
+    borders = (jnp.where(is_even, layers[1], layers[0]), jnp.where(is_even, layers[0], layers[1]))
+    front_images, packed2, packed3, fields_pair = lax.optimization_barrier((exchange(packed), packed2, packed3, fields_pair))
+    def own_last(pair):
+        return call(
+            functools.partial(own_last_kernel, starts[4]),
+            pltpu.HBM((caps[4], *field), F32),
+            [SMEM] + [VMEM] * 4,
+            splits(caps[4], 4, 3 * rows),
+            [taps, whole, forcing, *pair],
+            "own_last",
+            caps[4] * 2 * 27 * 9 * rows * rows * 256,
+        )
+
+    image = call(
+        functools.partial(first_kernel, groups, slot_dev),
+        pltpu.HBM((1, strides[1], lanes), F32),
+        [SMEM, VMEM],
+        [],
+        [slot_term, front_images],
         "first",
     )
-    images = [None, front_images, None, None]
-    waiting = [None, packed2, packed3]
+    arrived = [None, front_images, exchange(packed2), None]
     table = pltpu.SMEM((128,), jnp.int32)
     settled = []
     for level in range(1, DEGREE):
         height, height2 = eight(widths[level]), eight(widths[level] - 2)
         base = strides[1] if level == 1 else 0
-        image = images[level].reshape(groups * (1 if level == 1 else caps[level]), -1, lanes)
+        part = arrived[level].reshape(groups * (1 if level == 1 else caps[level]), -1, lanes)
         olds = settled
         total = sum(caps[1 : level + 1])
-        shapes = [pltpu.HBM((groups * total, 6 * own, lanes), F32), pltpu.HBM((COUNTS[level + 1], strides[level + 1], lanes), F32)]
+        shapes = [pltpu.HBM((groups * total, 6 * own, lanes), F32), pltpu.HBM((COUNTS[level], strides[level + 1], lanes), F32)]
         if level == DEGREE - 1:
-            shapes += [pltpu.HBM((COUNTS[DEGREE] // 2, 6 * widths[DEGREE], lanes), F32)] * 2
+            shapes += [pltpu.HBM(((COUNTS[level] + 3) // 4, 12 * widths[DEGREE], lanes), F32)] * 2
         size, size2 = 3 * height, 3 * height2
-        even, odd = beside((load, load), "space")
-        if level < 3:
-            even, block = lax.optimization_barrier((even, waiting[level]))
-            images[level + 1] = exchange(block)
-        result, load, *pieces = call(
+        even, odd = beside((image, image), "space")
+        if level == 2:
+            even, packed3 = lax.optimization_barrier((even, packed3))
+            arrived[3] = exchange(packed3)
+        result, image, *pieces = call(
             functools.partial(level_kernel, level, own, halos[level], rows, caps, starts, base, slot_dev),
             shapes,
-            [SMEM] * 3 + [HBM] * 3 + [VMEM] * (2 + len(olds)),
-            [pltpu.VMEM((COUNTS[level], strides[level], lanes), F32)] * 3
-            + [pltpu.SemaphoreType.DMA((3,)), pltpu.VMEM((DIMS, strides[level + 1], lanes), F32)]
+            [SMEM] * 3 + [HBM] * 6 + [VMEM] * (1 + len(olds)),
+            [pltpu.VMEM((3, COUNTS[level - 1], strides[level], lanes), F32), pltpu.VMEM((3, *fields.shape), F32), pltpu.SemaphoreType.DMA((6,))]
+            + [pltpu.VMEM((3, DIMS, strides[level], lanes), F32), pltpu.VMEM((3, COUNTS[level], strides[level], lanes), F32)]
             + [pltpu.VMEM((3 * size2, 9 * size), BF16), pltpu.VMEM((9 * eight(widths[level] - 4), 9 * size2), BF16)]
-            + [pltpu.VMEM((COUNTS[level], strides[level + 1], lanes), F32), table, table]
+            + [table, table]
             + [pltpu.VMEM((UNROLL, 6, size, lanes), F32), pltpu.VMEM((UNROLL, 4, size2, lanes), F32)]
             + splits(UNROLL, 6, size)
             + splits(UNROLL, 4, size2),
-            [slot_term, weights, taps, load, even, odd, fields, image, *olds],
+            [slot_term, weights, taps, image, even, odd, fields, *fields_pair, part, *olds],
             "level",
-            COUNTS[level] * 2 * 27 * size2 * (2 * size + size2) * 256,
-            60,
+            (1 if level == 1 else 30) * COUNTS[level] * 2 * 27 * size2 * (2 * size + size2) * 256,
+            63,
         )
         settled = [result]
     middle = exchange(result.reshape(groups, -1, lanes))
     even, odd = beside(pieces, "space")
+    even, odd, borders = lax.optimization_barrier((even, odd, borders))
+    part4 = own_last(beside(borders, "space"))
     height, height2 = eight(widths[DEGREE]), eight(own)
     result = call(
         functools.partial(last_kernel, own, caps, starts, slot_dev),
         pltpu.HBM((groups * caps[DEGREE], 6 * own, lanes), F32),
-        [SMEM] * 2 + [HBM] * 3,
-        [pltpu.VMEM((COUNTS[DEGREE], strides[DEGREE], lanes), F32)]
-        + [pltpu.VMEM((COUNTS[DEGREE] // 2, 6 * widths[DEGREE], lanes), F32)] * 2
-        + [pltpu.SemaphoreType.DMA((3,)), pltpu.VMEM((9 * height2, 27 * height), BF16), table, pltpu.VMEM((2 * UNROLL, 4, 3 * height, lanes), F32)] + splits(2 * UNROLL, 4, 3 * height),
-        [slot_term, taps, load, even, odd],
+        [SMEM] * 3 + [HBM] * 6,
+        [pltpu.VMEM((COUNTS[3], strides[DEGREE], lanes), F32), pltpu.VMEM((2, *pieces[0].shape), F32)]
+        + [pltpu.VMEM((3, *fields.shape), F32), pltpu.SemaphoreType.DMA((6,))]
+        + [pltpu.VMEM((DIMS, strides[DEGREE], lanes), F32), pltpu.VMEM((2, DIMS, 3 * widths[DEGREE], lanes), F32)]
+        + [pltpu.VMEM((COUNTS[DEGREE], strides[DEGREE], lanes), F32), pltpu.VMEM((2, COUNTS[DEGREE], 3 * widths[DEGREE], lanes), F32)]
+        + [pltpu.VMEM((9 * height2, 27 * height), BF16), table, pltpu.VMEM((2 * UNROLL, 4, 3 * height, lanes), F32)]
+        + splits(2 * UNROLL, 4, 3 * height),
+        [slot_term, weights, taps, image, even, odd, fields, *fields_pair],
         "level_last",
         COUNTS[DEGREE] * 2 * 27 * 9 * height * height2 * 256,
-        60,
+        63,
     )
     result, middle = lax.optimization_barrier((result, middle))
     final = exchange(result.reshape(groups, -1, lanes))
-    return call(
-        functools.partial(assemble_kernel, own, starts),
-        array(*forcing.shape),
-        [SMEM] + [VMEM] * (DEGREE + 3),
+    partial = call(
+        functools.partial(assemble_kernel, own, starts[DEGREE]),
+        pltpu.HBM(forcing.shape, F32),
+        [SMEM] + [VMEM] * (DEGREE + 1),
         [],
-        [slot_term, part01[:1], part01[1:], part2, part3, part4, middle, final],
+        [slot_term, part01, part2, part3, part4, middle],
         "assemble",
+        0,
+        60,
     )
+    partial, final = lax.optimization_barrier((partial, final))
+    return pl.pallas_call(
+        functools.partial(finish_kernel, own, starts[DEGREE]),
+        out_shape=array(*forcing.shape),
+        in_specs=[SMEM, ANY, ANY],
+        out_specs=ANY,
+        scratch_shapes=[pltpu.VMEM((caps[DEGREE], *field), F32), pltpu.VMEM(final.shape, F32), pltpu.SemaphoreType.DMA((1 + caps[DEGREE],))],
+        input_output_aliases={1: 0},
+        compiler_params=pltpu.CompilerParams(vmem_limit_bytes=60 * 2**20),
+        name="finish",
+    )(slot_term, partial, final)
 
 
 def solution(mesh):

time: 162 us -> 156 us (0.963); the launches traced: 160 us -> 152 us
  waiting for transfers between devices: 44.9 us -> 35.4 us
  local copies, waits for them, and re-layouts: 14.8 us -> 6.71 us
  starting transfers between devices: 49.1 us -> 54.8 us
  other arithmetic: 0.07 us -> 2 us
  Pallas kernels: 51.2 us -> 53.1 us
    unnamed x50 -> x32, local copies, waits for them, and re-layouts: 12.2 us -> 3.76 us
    ppermute x7 -> x9, waiting for transfers between devices: 31.8 us -> 26.2 us  [beside(): lax.ppermute(array[1], axis, odd)]
    ppermute x7 -> x9, starting transfers between devices: 22.9 us -> 27.2 us  [beside(): lax.ppermute(array[1], axis, odd)]
    all_to_all x5, waiting for transfers between devices: 13.1 us -> 9.18 us  [exchange(): return lax.all_to_all(blocks, 'terms', 0, 0, tiled=True)]
    pallas_call x0 -> x1, Pallas kernels: none -> 2.86 us  [on_device(): pl.pallas_call(functools.partial(finish_kernel, own, starts[DEGREE]), out...]
    select_n x1, other arithmetic: 0.07 us -> 2 us  [on_device(): jnp.where(is_even, layers[0], layers[1])]
  transfers between devices with their start and end apart: 19 -> 23, of which waited for: 6 -> 9; matrix products, arithmetic and copies ran while one was open for 1% -> 3% of each run, Pallas kernels for 20% -> 23%
where the time goes in v4:
time: 156 us; the launch traced here: 152 us
  starting transfers between devices  54.8 us (35%)
  Pallas kernels  53.1 us (34%)
  waiting for transfers between devices  35.4 us (23%)
  local copies, waits for them, and re-layouts  6.71 us (4%)
  other arithmetic  2 us (1%)
    pallas_call x11, Pallas kernels, call(): pl.pallas_call(kernel, out_shape=out_shape, in_specs=specs, out_specs=VME...  50.2 us
    ppermute x9, starting transfers between devices, beside(): lax.ppermute(array[1], axis, odd)  27.2 us
    ppermute x9, waiting for transfers between devices, beside(): lax.ppermute(array[1], axis, odd)  26.2 us
    all_to_all x5, starting transfers between devices, exchange(): return lax.all_to_all(blocks, 'terms', 0, 0, tiled=True)  25.8 us
    all_to_all x5, waiting for transfers between devices, exchange(): return lax.all_to_all(blocks, 'terms', 0, 0, tiled=True)  9.18 us
    unnamed x32, local copies, waits for them, and re-layouts  3.76 us
  transfers between devices with their start and end apart: 23, of which 9 were waited for; matrix products, arithmetic and copies ran while one was open for 3% of the time, Pallas kernels for 23%

profile of v4, /device:TPU:1, one launch (start us, length us, event | category | flops | bytes accessed | tf_op | source)
XLA Modules:
  0.0 152.5 jit_solution(18087769952942785628)
XLA Ops:
  1.1 4.5 %collective-permute-start.1 = (f32[2,3,2,32,128]{4,3,2,1,0:T(8,128)S(1)}, f32[2,3,2,32,128]{4,3,2,1,0:T(8,128)S(1)}, u32[]{:S(2)}, u32[]{:S(2)}) collective-permute-start(f32[2,3,2,32,128]{4,3,2,1,0:T(8,128)S(1)} %slice.15.forcing_ref), channel_id=1, source_target_pairs={{8,16},{16,8},{9,17},{17,9},{10,18},{18,10},{11,19},{19,11},{12,20... | collective-permute-start | bytes 589832 | tf_op jit(solution)/shard_map/ppermute | solution.py:449
  8.9 3.1 %own.3 = (f32[2,3,2,32,128]{4,3,2,1,0:T(8,128)}, f32[8,200,128]{2,1,0:T(8,128)}) custom-call(f32[3,3,27]{2,1,0:T(4,128)S(1)} %bitcast.15, bf16[288,864]{1,0:T(8,128)(2,1)S(1)} %matrix.1.packed, f32[2,3,2,32,128]{4,3,2,1,0:T(8,128)S(1)} %slice.15.forcing_ref, f32[2,3,2,32,128]{4,3,2,1,0:T(8,128)S(1)} %collective-permute-done.even_ref, ...), custom_call_target="tpu_custom_call" | custom-call | flops 764411904 | bytes 1586124 | tf_op jit(solution)/shard_map/own/pallas_call | solution.py:433
  12.0 6.2 %all-to-all-start = ((f32[8,200,128]{2,1,0:T(8,128)}), f32[8,200,128]{2,1,0:T(8,128)S(1)}, u32[]{:S(2)}, u32[]{:S(2)}) async-start(f32[8,200,128]{2,1,0:T(8,128)} %get-tuple-element.42), calls=%async_computation | async-start | bytes 1638400 | tf_op jit(solution)/shard_map/all_to_all | solution.py:453
  19.4 3.3 %collective-permute-start.5 = (f32[5,3,2,32,128]{4,3,2,1,0:T(8,128)S(1)}, f32[5,3,2,32,128]{4,3,2,1,0:T(8,128)S(1)}, u32[]{:S(2)}, u32[]{:S(2)}) collective-permute-start(f32[5,3,2,32,128]{4,3,2,1,0:T(8,128)S(1)} %slice.17.forcing_ref), channel_id=1, source_target_pairs={{8,16},{16,8},{9,17},{17,9},{10,18},{18,10},{11,19},{19,11},{12,20... | collective-permute-start | bytes 1474568 | tf_op jit(solution)/shard_map/ppermute | solution.py:449
  26.1 3.3 %collective-permute-start.7 = (f32[5,2,32,128]{3,2,1,0:T(8,128)S(1)}, f32[5,2,32,128]{3,2,1,0:T(8,128)}, u32[]{:S(2)}, u32[]{:S(2)}) collective-permute-start(f32[5,2,32,128]{3,2,1,0:T(8,128)S(1)} %copy-done.11), channel_id=1, source_target_pairs={{8,16},{16,8},{9,17},{17,9},{10,18},{18,10},{11,19},{19,11},{12,20... | collective-permute-start | bytes 491528 | tf_op jit(solution)/shard_map/ppermute | solution.py:449
  31.9 3.0 %own.4 = (f32[2,3,2,32,128]{4,3,2,1,0:T(8,128)}, f32[8,128,128]{2,1,0:T(8,128)}) custom-call(f32[3,3,27]{2,1,0:T(4,128)S(1)} %bitcast.16, bf16[288,864]{1,0:T(8,128)(2,1)S(1)} %matrix.1.packed, f32[2,3,2,32,128]{4,3,2,1,0:T(8,128)S(1)} %slice.16.forcing_ref, f32[2,3,2,32,128]{4,3,2,1,0:T(8,128)S(1)} %collective-permute-done.2.even_ref, ...), custom_call_target="tpu_custom_call" | custom-call | flops 764411904 | bytes 1586124 | tf_op jit(solution)/shard_map/own/pallas_call | solution.py:433
  34.9 4.3 %own.5 = (f32[5,3,2,32,128]{4,3,2,1,0:T(8,128)}, f32[8,200,128]{2,1,0:T(8,128)}) custom-call(f32[3,3,27]{2,1,0:T(4,128)S(1)} %bitcast.17, bf16[288,864]{1,0:T(8,128)(2,1)S(1)} %matrix.1.packed, f32[5,3,2,32,128]{4,3,2,1,0:T(8,128)S(1)} %slice.17.forcing_ref, f32[5,3,2,32,128]{4,3,2,1,0:T(8,128)S(1)} %collective-permute-done.4.even_ref, ...), custom_call_target="tpu_custom_call" | custom-call | flops 1911029760 | bytes 2470860 | tf_op jit(solution)/shard_map/own/pallas_call | solution.py:433
  39.2 5.4 %all-to-all-start.1 = ((f32[8,128,128]{2,1,0:T(8,128)}), f32[8,128,128]{2,1,0:T(8,128)}, u32[]{:S(2)}, u32[]{:S(2)}) async-start(f32[8,128,128]{2,1,0:T(8,128)} %get-tuple-element.52), calls=%async_computation.1 | async-start | bytes 1048576 | tf_op jit(solution)/shard_map/all_to_all | solution.py:453
  45.9 3.6 %collective-permute-start.9 = (f32[1,112,128]{2,1,0:T(8,128)}, f32[1,112,128]{2,1,0:T(8,128)S(1)}, u32[]{:S(2)}, u32[]{:S(2)}) collective-permute-start(f32[1,112,128]{2,1,0:T(8,128)} %first.1.own_hbm), channel_id=1, source_target_pairs={{8,16},{16,8},{9,17},{17,9},{10,18},{18,10},{11,19},{19,11},{12,20... | collective-permute-start | bytes 172040 | tf_op jit(solution)/shard_map/ppermute | solution.py:449
  52.6 4.9 %level.3 = (f32[8,24,128]{2,1,0:T(8,128)}, f32[5,88,128]{2,1,0:T(8,128)}) custom-call(s32[144]{0:T(256)} %slot_ref.13, f32[5,126]{1,0:T(8,128)} %bitcast.22, f32[3,3,27]{2,1,0:T(4,128)} %bitcast.10, f32[1,112,128]{2,1,0:T(8,128)} %first.1.own_hbm, f32[1,112,128]{2,1,0:T(8,128)} %copy-done.14, f32[1,112,128]{2,1,0:T(8,128)} %copy-done.15, ...), custom_call_target="tpu_custom_call" | custom-call | flops 637009920 | bytes 1486820 | tf_op jit(solution)/shard_map/level/pallas_call | solution.py:433
  57.6 3.2 %collective-permute-start.11 = (f32[5,88,128]{2,1,0:T(8,128)}, f32[5,88,128]{2,1,0:T(8,128)}, u32[]{:S(2)}, u32[]{:S(2)}) collective-permute-start(f32[5,88,128]{2,1,0:T(8,128)} %get-tuple-element.49.own_hbm), channel_id=1, source_target_pairs={{8,16},{16,8},{9,17},{17,9},{10,18},{18,10},{11,19},{19,11},{12,20... | collective-permute-start | bytes 675848 | tf_op jit(solution)/shard_map/ppermute | solution.py:449
  60.8 5.7 %all-to-all-start.2 = ((f32[8,200,128]{2,1,0:T(8,128)}), f32[8,200,128]{2,1,0:T(8,128)S(1)}, u32[]{:S(2)}, u32[]{:S(2)}) async-start(f32[8,200,128]{2,1,0:T(8,128)} %get-tuple-element.55), calls=%async_computation.2 | async-start | bytes 1638400 | tf_op jit(solution)/shard_map/all_to_all | solution.py:453
  66.5 7.3 %level.4 = (f32[24,24,128]{2,1,0:T(8,128)}, f32[15,64,128]{2,1,0:T(8,128)}) custom-call(s32[144]{0:T(256)} %slot_ref.13, f32[5,126]{1,0:T(8,128)} %bitcast.23, f32[3,3,27]{2,1,0:T(4,128)} %bitcast.11, f32[5,88,128]{2,1,0:T(8,128)} %get-tuple-element.49.own_hbm, f32[5,88,128]{2,1,0:T(8,128)} %collective-permute-done.10.even_hbm, ...), custom_call_target="tpu_custom_call" | custom-call | flops 42998169600 | bytes 1794020 | tf_op jit(solution)/shard_map/level/pallas_call | solution.py:433
  77.5 6.9 %collective-permute-done.13.odd_hbm = f32[15,64,128]{2,1,0:T(8,128)} collective-permute-done((f32[15,64,128]{2,1,0:T(8,128)}, f32[15,64,128]{2,1,0:T(8,128)}, u32[]{:S(2)}, u32[]{:S(2)}) %collective-permute-start.13) | collective-permute-done | bytes 491552 | tf_op jit(solution)/shard_map/ppermute | solution.py:449
  84.4 3.0 %all-to-all-done.2 = f32[8,200,128]{2,1,0:T(8,128)S(1)} async-done(((f32[8,200,128]{2,1,0:T(8,128)}), f32[8,200,128]{2,1,0:T(8,128)S(1)}, u32[]{:S(2)}, u32[]{:S(2)}) %all-to-all-start.2) | async-done | bytes 819232 | tf_op jit(solution)/shard_map/all_to_all | solution.py:453
  88.3 11.3 %level.5 = (f32[64,24,128]{2,1,0:T(8,128)}, f32[35,40,128]{2,1,0:T(8,128)}, f32[9,72,128]{2,1,0:T(8,128)}, f32[9,72,128]{2,1,0:T(8,128)}) custom-call(s32[144]{0:T(256)} %slot_ref.13, f32[5,126]{1,0:T(8,128)} %bitcast.24, f32[3,3,27]{2,1,0:T(4,128)} %bitcast.12, f32[15,64,128]{2,1,0:T(8,128)} %get-tuple-element.54.own_hbm, f32[15,64,128]{2,1,0:T(8,128)} %copy-done.13, ...), custom_call_target="tpu_custom_call" | custom-call | flops 41803776000 | bytes 3084260 | tf_op jit(solution)/shard_map/level/pallas_call | solution.py:433
  99.6 4.2 %all-to-all-start.3 = ((f32[8,192,128]{2,1,0:T(8,128)}), f32[8,192,128]{2,1,0:T(8,128)}, u32[]{:S(2)}, u32[]{:S(2)}) async-start(f32[8,192,128]{2,1,0:T(8,128)} %bitcast.21), calls=%async_computation.3 | async-start | bytes 1572864 | tf_op jit(solution)/shard_map/all_to_all | solution.py:453
  108.4 4.7 %collective-permute-done.15.odd_hbm = f32[9,72,128]{2,1,0:T(8,128)S(1)} collective-permute-done((f32[9,72,128]{2,1,0:T(8,128)}, f32[9,72,128]{2,1,0:T(8,128)S(1)}, u32[]{:S(2)}, u32[]{:S(2)}) %collective-permute-start.15) | collective-permute-done | bytes 331808 | tf_op jit(solution)/shard_map/ppermute | solution.py:449
  113.9 7.8 %level_last.1 = f32[72,24,128]{2,1,0:T(8,128)} custom-call(s32[144]{0:T(256)} %slot_ref.13, f32[5,126]{1,0:T(8,128)} %bitcast.25, f32[3,3,27]{2,1,0:T(4,128)} %bitcast.13, f32[35,40,128]{2,1,0:T(8,128)} %get-tuple-element.61.own_hbm, f32[9,72,128]{2,1,0:T(8,128)} %copy-done.9, f32[9,72,128]{2,1,0:T(8,128)} %copy-done.10, f32[5,2,32,128]{3,2,1,0:T(8,128)} %fields_hbm.3, ...), custom_call_target="tpu_custom_call" | custom-call | flops 557383680 | bytes 1875940 | tf_op jit(solution)/shard_map/level_last/pallas_call | solution.py:433
  124.0 4.2 %all-to-all-start.4 = ((f32[8,216,128]{2,1,0:T(8,128)}), f32[8,216,128]{2,1,0:T(8,128)}, u32[]{:S(2)}, u32[]{:S(2)}) async-start(f32[8,216,128]{2,1,0:T(8,128)} %bitcast.19), calls=%async_computation.4 | async-start | bytes 1769472 | tf_op jit(solution)/shard_map/all_to_all | solution.py:453
  131.2 8.1 %collective-permute-done.17.odd_ref = f32[9,3,32,128]{3,2,1,0:T(8,128)S(1)} collective-permute-done((f32[9,3,32,128]{3,2,1,0:T(8,128)S(1)}, f32[9,3,32,128]{3,2,1,0:T(8,128)S(1)}, u32[]{:S(2)}, u32[]{:S(2)}) %collective-permute-start.17) | collective-permute-done | bytes 442400 | tf_op jit(solution)/shard_map/ppermute | solution.py:449
  139.3 3.3 %own_last.1.refs_3_ = f32[9,3,2,32,128]{4,3,2,1,0:T(8,128)} custom-call(f32[3,3,27]{2,1,0:T(4,128)S(1)} %bitcast.18, bf16[288,864]{1,0:T(8,128)(2,1)S(1)} %copy-done.3, f32[18,3,2,32,128]{4,3,2,1,0:T(8,128)S(1)} %copy-done.1, f32[9,3,32,128]{3,2,1,0:T(8,128)S(1)} %collective-permute-done.16.even_ref, f32[9,3,32,128]{3,2,1,0:T(8,128)S(1)} %collective-permute-done.17.odd_ref), custom_call_target="tpu_custom_call" | custom-call | flops 1146617856 | bytes 3650508 | tf_op jit(solution)/shard_map/own_last/pallas_call | solution.py:433
  142.6 3.1 %assemble.1.partial_ref = f32[18,3,2,32,128]{4,3,2,1,0:T(8,128)} custom-call(s32[144]{0:T(256)} %slot_ref.13, f32[2,3,2,32,128]{4,3,2,1,0:T(8,128)} %get-tuple-element.37.refs_0_, f32[2,3,2,32,128]{4,3,2,1,0:T(8,128)} %get-tuple-element.40.refs_1_, f32[5,3,2,32,128]{4,3,2,1,0:T(8,128)} %get-tuple-element.41.refs_2_, f32[9,3,2,32,128]{4,3,2,1,0:T(8,128)} %own_last.1.refs_3_, ...), custom_call_target="tpu_custom_call" | custom-call | bytes 2556480 | tf_op jit(solution)/shard_map/assemble/pallas_call | solution.py:433
  145.7 3.8 %all-to-all-done.4.links_hbm = f32[8,216,128]{2,1,0:T(8,128)} async-done(((f32[8,216,128]{2,1,0:T(8,128)}), f32[8,216,128]{2,1,0:T(8,128)}, u32[]{:S(2)}, u32[]{:S(2)}) %all-to-all-start.4) | async-done | bytes 884768 | tf_op jit(solution)/shard_map/all_to_all | solution.py:453
  (70 shorter events, 33.7 us)
Async XLA Ops:
  0.9 6.3 %collective-permute-start = (f32[2,3,2,32,128]{4,3,2,1,0:T(8,128)S(1)}, f32[2,3,2,32,128]{4,3,2,1,0:T(8,128)S(1)}, u32[]{:S(2)}, u32[]{:S(2)}) collective-permute-start(f32[2,3,2,32,128]{4,3,2,1,0:T(8,128)S(1)} %slice.15.forcing_ref), channel_id=1, source_target_pairs={{0,8},{8,0},{16,24},{24,16},{1,9},{9,1},{17,25},{25,17},{2,10},{10... | collective-permute-start | bytes 589832 | tf_op jit(solution)/shard_map/ppermute | solution.py:449
  1.1 7.8 %collective-permute-start.1 = (f32[2,3,2,32,128]{4,3,2,1,0:T(8,128)S(1)}, f32[2,3,2,32,128]{4,3,2,1,0:T(8,128)S(1)}, u32[]{:S(2)}, u32[]{:S(2)}) collective-permute-start(f32[2,3,2,32,128]{4,3,2,1,0:T(8,128)S(1)} %slice.15.forcing_ref), channel_id=1, source_target_pairs={{8,16},{16,8},{9,17},{17,9},{10,18},{18,10},{11,19},{19,11},{12,20... | collective-permute-start | bytes 589832 | tf_op jit(solution)/shard_map/ppermute | solution.py:449
  7.3 27.6 %copy-start.2 = (bf16[288,864]{1,0:T(8,128)(2,1)}, bf16[288,864]{1,0:T(8,128)(2,1)S(1)}, u32[]{:S(2)}) copy-start(bf16[288,864]{1,0:T(8,128)(2,1)S(1)} %matrix.1.packed) | copy-start | bytes 1492996
  12.0 27.2 %all-to-all-start = ((f32[8,200,128]{2,1,0:T(8,128)}), f32[8,200,128]{2,1,0:T(8,128)S(1)}, u32[]{:S(2)}, u32[]{:S(2)}) async-start(f32[8,200,128]{2,1,0:T(8,128)} %get-tuple-element.42), calls=%async_computation | async-start | bytes 1638400 | tf_op jit(solution)/shard_map/all_to_all | solution.py:453
  19.3 15.6 %collective-permute-start.4 = (f32[5,3,2,32,128]{4,3,2,1,0:T(8,128)S(1)}, f32[5,3,2,32,128]{4,3,2,1,0:T(8,128)S(1)}, u32[]{:S(2)}, u32[]{:S(2)}) collective-permute-start(f32[5,3,2,32,128]{4,3,2,1,0:T(8,128)S(1)} %slice.17.forcing_ref), channel_id=1, source_target_pairs={{0,8},{8,0},{16,24},{24,16},{1,9},{9,1},{17,25},{25,17},{2,10},{10... | collective-permute-start | bytes 1474568 | tf_op jit(solution)/shard_map/ppermute | solution.py:449
  19.4 15.5 %collective-permute-start.5 = (f32[5,3,2,32,128]{4,3,2,1,0:T(8,128)S(1)}, f32[5,3,2,32,128]{4,3,2,1,0:T(8,128)S(1)}, u32[]{:S(2)}, u32[]{:S(2)}) collective-permute-start(f32[5,3,2,32,128]{4,3,2,1,0:T(8,128)S(1)} %slice.17.forcing_ref), channel_id=1, source_target_pairs={{8,16},{16,8},{9,17},{17,9},{10,18},{18,10},{11,19},{19,11},{12,20... | collective-permute-start | bytes 1474568 | tf_op jit(solution)/shard_map/ppermute | solution.py:449
  23.7 2.4 %collective-permute-start.2 = (f32[2,3,2,32,128]{4,3,2,1,0:T(8,128)S(1)}, f32[2,3,2,32,128]{4,3,2,1,0:T(8,128)S(1)}, u32[]{:S(2)}, u32[]{:S(2)}) collective-permute-start(f32[2,3,2,32,128]{4,3,2,1,0:T(8,128)S(1)} %slice.16.forcing_ref), channel_id=1, source_target_pairs={{0,8},{8,0},{16,24},{24,16},{1,9},{9,1},{17,25},{25,17},{2,10},{10... | collective-permute-start | bytes 589832 | tf_op jit(solution)/shard_map/ppermute | solution.py:449
  23.8 8.2 %collective-permute-start.3 = (f32[2,3,2,32,128]{4,3,2,1,0:T(8,128)S(1)}, f32[2,3,2,32,128]{4,3,2,1,0:T(8,128)S(1)}, u32[]{:S(2)}, u32[]{:S(2)}) collective-permute-start(f32[2,3,2,32,128]{4,3,2,1,0:T(8,128)S(1)} %slice.16.forcing_ref), channel_id=1, source_target_pairs={{8,16},{16,8},{9,17},{17,9},{10,18},{18,10},{11,19},{19,11},{12,20... | collective-permute-start | bytes 589832 | tf_op jit(solution)/shard_map/ppermute | solution.py:449
  26.0 13.2 %collective-permute-start.6 = (f32[5,2,32,128]{3,2,1,0:T(8,128)S(1)}, f32[5,2,32,128]{3,2,1,0:T(8,128)S(1)}, u32[]{:S(2)}, u32[]{:S(2)}) collective-permute-start(f32[5,2,32,128]{3,2,1,0:T(8,128)S(1)} %copy-done.11), channel_id=1, source_target_pairs={{0,8},{8,0},{16,24},{24,16},{1,9},{9,1},{17,25},{25,17},{2,10},{10... | collective-permute-start | bytes 491528 | tf_op jit(solution)/shard_map/ppermute | solution.py:449
  26.1 13.1 %collective-permute-start.7 = (f32[5,2,32,128]{3,2,1,0:T(8,128)S(1)}, f32[5,2,32,128]{3,2,1,0:T(8,128)}, u32[]{:S(2)}, u32[]{:S(2)}) collective-permute-start(f32[5,2,32,128]{3,2,1,0:T(8,128)S(1)} %copy-done.11), channel_id=1, source_target_pairs={{8,16},{16,8},{9,17},{17,9},{10,18},{18,10},{11,19},{19,11},{12,20... | collective-permute-start | bytes 491528 | tf_op jit(solution)/shard_map/ppermute | solution.py:449
  39.2 21.6 %all-to-all-start.1 = ((f32[8,128,128]{2,1,0:T(8,128)}), f32[8,128,128]{2,1,0:T(8,128)}, u32[]{:S(2)}, u32[]{:S(2)}) async-start(f32[8,128,128]{2,1,0:T(8,128)} %get-tuple-element.52), calls=%async_computation.1 | async-start | bytes 1048576 | tf_op jit(solution)/shard_map/all_to_all | solution.py:453
  45.9 3.6 %collective-permute-start.8 = (f32[1,112,128]{2,1,0:T(8,128)}, f32[1,112,128]{2,1,0:T(8,128)S(1)}, u32[]{:S(2)}, u32[]{:S(2)}) collective-permute-start(f32[1,112,128]{2,1,0:T(8,128)} %first.1.own_hbm), channel_id=1, source_target_pairs={{0,8},{8,0},{16,24},{24,16},{1,9},{9,1},{17,25},{25,17},{2,10},{10... | collective-permute-start | bytes 172040 | tf_op jit(solution)/shard_map/ppermute | solution.py:449
  45.9 6.1 %collective-permute-start.9 = (f32[1,112,128]{2,1,0:T(8,128)}, f32[1,112,128]{2,1,0:T(8,128)S(1)}, u32[]{:S(2)}, u32[]{:S(2)}) collective-permute-start(f32[1,112,128]{2,1,0:T(8,128)} %first.1.own_hbm), channel_id=1, source_target_pairs={{8,16},{16,8},{9,17},{17,9},{10,18},{18,10},{11,19},{19,11},{12,20... | collective-permute-start | bytes 172040 | tf_op jit(solution)/shard_map/ppermute | solution.py:449
  57.5 3.3 %collective-permute-start.10 = (f32[5,88,128]{2,1,0:T(8,128)}, f32[5,88,128]{2,1,0:T(8,128)}, u32[]{:S(2)}, u32[]{:S(2)}) collective-permute-start(f32[5,88,128]{2,1,0:T(8,128)} %get-tuple-element.49.own_hbm), channel_id=1, source_target_pairs={{0,8},{8,0},{16,24},{24,16},{1,9},{9,1},{17,25},{25,17},{2,10},{10... | collective-permute-start | bytes 675848 | tf_op jit(solution)/shard_map/ppermute | solution.py:449
  57.6 8.9 %collective-permute-start.11 = (f32[5,88,128]{2,1,0:T(8,128)}, f32[5,88,128]{2,1,0:T(8,128)}, u32[]{:S(2)}, u32[]{:S(2)}) collective-permute-start(f32[5,88,128]{2,1,0:T(8,128)} %get-tuple-element.49.own_hbm), channel_id=1, source_target_pairs={{8,16},{16,8},{9,17},{17,9},{10,18},{18,10},{11,19},{19,11},{12,20... | collective-permute-start | bytes 675848 | tf_op jit(solution)/shard_map/ppermute | solution.py:449
  60.8 26.6 %all-to-all-start.2 = ((f32[8,200,128]{2,1,0:T(8,128)}), f32[8,200,128]{2,1,0:T(8,128)S(1)}, u32[]{:S(2)}, u32[]{:S(2)}) async-start(f32[8,200,128]{2,1,0:T(8,128)} %get-tuple-element.55), calls=%async_computation.2 | async-start | bytes 1638400 | tf_op jit(solution)/shard_map/all_to_all | solution.py:453
  73.8 2.9 %collective-permute-start.12 = (f32[15,64,128]{2,1,0:T(8,128)}, f32[15,64,128]{2,1,0:T(8,128)S(1)}, u32[]{:S(2)}, u32[]{:S(2)}) collective-permute-start(f32[15,64,128]{2,1,0:T(8,128)} %get-tuple-element.54.own_hbm), channel_id=1, source_target_pairs={{0,8},{8,0},{16,24},{24,16},{1,9},{9,1},{17,25},{25,17},{2,10},{10... | collective-permute-start | bytes 1474568 | tf_op jit(solution)/shard_map/ppermute | solution.py:449
  73.9 10.5 %collective-permute-start.13 = (f32[15,64,128]{2,1,0:T(8,128)}, f32[15,64,128]{2,1,0:T(8,128)}, u32[]{:S(2)}, u32[]{:S(2)}) collective-permute-start(f32[15,64,128]{2,1,0:T(8,128)} %get-tuple-element.54.own_hbm), channel_id=1, source_target_pairs={{8,16},{16,8},{9,17},{17,9},{10,18},{18,10},{11,19},{19,11},{12,20... | collective-permute-start | bytes 1474568 | tf_op jit(solution)/shard_map/ppermute | solution.py:449
  99.6 24.4 %all-to-all-start.3 = ((f32[8,192,128]{2,1,0:T(8,128)}), f32[8,192,128]{2,1,0:T(8,128)}, u32[]{:S(2)}, u32[]{:S(2)}) async-start(f32[8,192,128]{2,1,0:T(8,128)} %bitcast.21), calls=%async_computation.3 | async-start | bytes 1572864 | tf_op jit(solution)/shard_map/all_to_all | solution.py:453
  103.9 4.6 %collective-permute-start.14 = (f32[9,72,128]{2,1,0:T(8,128)}, f32[9,72,128]{2,1,0:T(8,128)S(1)}, u32[]{:S(2)}, u32[]{:S(2)}) collective-permute-start(f32[9,72,128]{2,1,0:T(8,128)} %get-tuple-element.57), channel_id=1, source_target_pairs={{0,8},{8,0},{16,24},{24,16},{1,9},{9,1},{17,25},{25,17},{2,10},{10... | collective-permute-start | bytes 995336 | tf_op jit(solution)/shard_map/ppermute | solution.py:449
  104.1 9.0 %collective-permute-start.15 = (f32[9,72,128]{2,1,0:T(8,128)}, f32[9,72,128]{2,1,0:T(8,128)S(1)}, u32[]{:S(2)}, u32[]{:S(2)}) collective-permute-start(f32[9,72,128]{2,1,0:T(8,128)} %get-tuple-element.58), channel_id=1, source_target_pairs={{8,16},{16,8},{9,17},{17,9},{10,18},{18,10},{11,19},{19,11},{12,20... | collective-permute-start | bytes 995336 | tf_op jit(solution)/shard_map/ppermute | solution.py:449
  124.0 25.5 %all-to-all-start.4 = ((f32[8,216,128]{2,1,0:T(8,128)}), f32[8,216,128]{2,1,0:T(8,128)}, u32[]{:S(2)}, u32[]{:S(2)}) async-start(f32[8,216,128]{2,1,0:T(8,128)} %bitcast.19), calls=%async_computation.4 | async-start | bytes 1769472 | tf_op jit(solution)/shard_map/all_to_all | solution.py:453
  128.2 3.0 %collective-permute-start.16 = (f32[9,3,32,128]{3,2,1,0:T(8,128)}, f32[9,3,32,128]{3,2,1,0:T(8,128)S(1)}, u32[]{:S(2)}, u32[]{:S(2)}) collective-permute-start(f32[9,3,32,128]{3,2,1,0:T(8,128)} %get-tuple-element.59), channel_id=1, source_target_pairs={{0,8},{8,0},{16,24},{24,16},{1,9},{9,1},{17,25},{25,17},{2,10},{10... | collective-permute-start | bytes 1327112 | tf_op jit(solution)/shard_map/ppermute | solution.py:449
  129.3 10.0 %collective-permute-start.17 = (f32[9,3,32,128]{3,2,1,0:T(8,128)S(1)}, f32[9,3,32,128]{3,2,1,0:T(8,128)S(1)}, u32[]{:S(2)}, u32[]{:S(2)}) collective-permute-start(f32[9,3,32,128]{3,2,1,0:T(8,128)S(1)} %get-tuple-element.60), channel_id=1, source_target_pairs={{8,16},{16,8},{9,17},{17,9},{10,18},{18,10},{11,19},{19,11},{12,20... | collective-permute-start | bytes 1327112 | tf_op jit(solution)/shard_map/ppermute | solution.py:449
  (15 other events, 142.6 us)

commit v5 on v4

--- a/solution.py
+++ b/solution.py
@@ -11,7 +11,7 @@
 
 DIMS = 5
 DEGREE = 4
-UNROLL = 5
+UNROLL = {1: 5, 2: 15, 3: 35, 4: 35}
 F32 = jnp.float32
 BF16 = jnp.bfloat16
 ANY = pl.BlockSpec(memory_space=pl.ANY)
@@ -255,6 +255,7 @@
         semaphores,
     )
     settled_ref, images, *pieces = refs[len(olds) : -15]
+    unroll = UNROLL[level]
     groups = lax.axis_size("terms")
     group = lax.axis_index("terms")
     lanes = images.shape[2]
@@ -283,7 +284,7 @@
             settled_ref[source * stride : source * stride + offset] = old_ref[source * offset : (source + 1) * offset]
 
     def terms(step, carry):
-        lanes_of = [(lane, step * UNROLL + lane) for lane in range(UNROLL)]
+        lanes_of = [(lane, step * unroll + lane) for lane in range(unroll)]
         for lane, term in lanes_of:
             for x in range(6):
                 for a in range(3):
@@ -321,7 +322,7 @@
                     images[term, part] = applied[x][a * height3 : a * height3 + next_width] + image_ref[in_slot, pl.ds(base + begin, next_width)]
         return carry
 
-    lax.fori_loop(0, COUNTS[level] // UNROLL, terms, 0)
+    lax.fori_loop(0, COUNTS[level] // unroll, terms, 0)
 
     if pieces:
         for term in range(COUNTS[level]):
@@ -361,8 +362,8 @@
         link_sums(DEGREE, coupling_ref, side_modes.at[upper], side_image, side_loads.at[upper])
 
     def terms(step, carry):
-        for lane in range(2 * UNROLL):
-            term = step * 2 * UNROLL + lane
+        for lane in range(UNROLL[DEGREE]):
+            term = step * UNROLL[DEGREE] + lane
             for a in range(3):
                 for upper in range(2):
                     ext[lane, 3 * upper, a * height : a * height + width] = side_loads[upper, term, a * width : (a + 1) * width]
@@ -371,8 +372,8 @@
                     ext[lane, x + 1, a * height : a * height + width] = loads[term, begin : begin + width]
             for x in range(4):
                 put_split(ext[lane, x] * inverse, high.at[lane], low.at[lane], x)
-        for lane in range(2 * UNROLL):
-            term = step * 2 * UNROLL + lane
+        for lane in range(UNROLL[DEGREE]):
+            term = step * UNROLL[DEGREE] + lane
             applied = apply_pair(high.at[lane], low.at[lane], packed, 0)
             slot = place[FIRSTS[DEGREE] + term]
             for a in range(3):
@@ -384,7 +385,7 @@
                     settled_ref[slot, plane * own : (plane + 1) * own] = load * scale + (load - applied[x][a * height2 : a * height2 + own]) * scale
         return carry
 
-    lax.fori_loop(0, COUNTS[DEGREE] // (2 * UNROLL), terms, 0)
+    lax.fori_loop(0, COUNTS[DEGREE] // UNROLL[DEGREE], terms, 0)
 
 
 def assemble_kernel(own, start, slot_ref, *refs):
@@ -480,7 +481,8 @@
         for level in levels:
             for _ in range(caps[level]):
                 layout.append((halos[level + 1], row))
-                row += strides[level + 1]
+                row += strides[level + 1] if len(levels) == 1 else 6 * widths[level + 1]
+        row = eight(row)
         count = len(layout)
         size = 3 * rows
         return call(
@@ -503,7 +505,7 @@
     is_even = lax.axis_index("space") % 2 == 0
     layers = [forcing[starts[4] :, :, x] for x in range(2)]
     borders = (jnp.where(is_even, layers[1], layers[0]), jnp.where(is_even, layers[0], layers[1]))
-    front_images, packed2, packed3, fields_pair = lax.optimization_barrier((exchange(packed), packed2, packed3, fields_pair))
+    front_images, packed2, fields_pair = lax.optimization_barrier((exchange(packed), packed2, fields_pair))
     def own_last(pair):
         return call(
             functools.partial(own_last_kernel, starts[4]),
@@ -528,7 +530,7 @@
     settled = []
     for level in range(1, DEGREE):
         height, height2 = eight(widths[level]), eight(widths[level] - 2)
-        base = strides[1] if level == 1 else 0
+        base = 6 * widths[1] if level == 1 else 0
         part = arrived[level].reshape(groups * (1 if level == 1 else caps[level]), -1, lanes)
         olds = settled
         total = sum(caps[1 : level + 1])
@@ -537,6 +539,8 @@
             shapes += [pltpu.HBM(((COUNTS[level] + 3) // 4, 12 * widths[DEGREE], lanes), F32)] * 2
         size, size2 = 3 * height, 3 * height2
         even, odd = beside((image, image), "space")
+        if level == 1:
+            even, packed3 = lax.optimization_barrier((even, packed3))
         if level == 2:
             even, packed3 = lax.optimization_barrier((even, packed3))
             arrived[3] = exchange(packed3)
@@ -548,9 +552,9 @@
             + [pltpu.VMEM((3, DIMS, strides[level], lanes), F32), pltpu.VMEM((3, COUNTS[level], strides[level], lanes), F32)]
             + [pltpu.VMEM((3 * size2, 9 * size), BF16), pltpu.VMEM((9 * eight(widths[level] - 4), 9 * size2), BF16)]
             + [table, table]
-            + [pltpu.VMEM((UNROLL, 6, size, lanes), F32), pltpu.VMEM((UNROLL, 4, size2, lanes), F32)]
-            + splits(UNROLL, 6, size)
-            + splits(UNROLL, 4, size2),
+            + [pltpu.VMEM((UNROLL[level], 6, size, lanes), F32), pltpu.VMEM((UNROLL[level], 4, size2, lanes), F32)]
+            + splits(UNROLL[level], 6, size)
+            + splits(UNROLL[level], 4, size2),
             [slot_term, weights, taps, image, even, odd, fields, *fields_pair, part, *olds],
             "level",
             (1 if level == 1 else 30) * COUNTS[level] * 2 * 27 * size2 * (2 * size + size2) * 256,
@@ -570,8 +574,8 @@
         + [pltpu.VMEM((3, *fields.shape), F32), pltpu.SemaphoreType.DMA((6,))]
         + [pltpu.VMEM((DIMS, strides[DEGREE], lanes), F32), pltpu.VMEM((2, DIMS, 3 * widths[DEGREE], lanes), F32)]
         + [pltpu.VMEM((COUNTS[DEGREE], strides[DEGREE], lanes), F32), pltpu.VMEM((2, COUNTS[DEGREE], 3 * widths[DEGREE], lanes), F32)]
-        + [pltpu.VMEM((9 * height2, 27 * height), BF16), table, pltpu.VMEM((2 * UNROLL, 4, 3 * height, lanes), F32)]
-        + splits(2 * UNROLL, 4, 3 * height),
+        + [pltpu.VMEM((9 * height2, 27 * height), BF16), table, pltpu.VMEM((UNROLL[DEGREE], 4, 3 * height, lanes), F32)]
+        + splits(UNROLL[DEGREE], 4, 3 * height),
         [slot_term, weights, taps, image, even, odd, fields, *fields_pair],
         "level_last",
         COUNTS[DEGREE] * 2 * 27 * 9 * height * height2 * 256,

time: 156 us -> 147 us (0.942)
  the two profiles are of different devices: /device:TPU:1 before, /device:TPU:0 now
where the time goes in v5:
time: 147 us; the launch traced here: 146 us
  Pallas kernels  48.6 us (33%)
  starting transfers between devices  47.8 us (33%)
  waiting for transfers between devices  41.1 us (28%)
  local copies, waits for them, and re-layouts  5.87 us (4%)
  other arithmetic  2 us (1%)
    pallas_call x11, Pallas kernels, call(): pl.pallas_call(kernel, out_shape=out_shape, in_specs=specs, out_specs=VME...  45.7 us
    all_to_all x5, waiting for transfers between devices, exchange(): return lax.all_to_all(blocks, 'terms', 0, 0, tiled=True)  38.7 us
    all_to_all x5, starting transfers between devices, exchange(): return lax.all_to_all(blocks, 'terms', 0, 0, tiled=True)  26.3 us
    ppermute x9, starting transfers between devices, beside(): lax.ppermute(array[0], axis, even)  14.8 us
    ppermute x9, starting transfers between devices, beside(): lax.ppermute(array[1], axis, odd)  6.81 us
  transfers between devices with their start and end apart: 23, of which 7 were waited for; matrix products, arithmetic and copies ran while one was open for 3% of the time, Pallas kernels for 23%

profile of v5, /device:TPU:0, one launch (start us, length us, event | category | flops | bytes accessed | tf_op | source)
XLA Modules:
  0.0 145.9 jit_solution(6029239013617702763)
XLA Ops:
  3.9 3.1 %own.3 = (f32[2,3,2,32,128]{4,3,2,1,0:T(8,128)}, f32[8,192,128]{2,1,0:T(8,128)}) custom-call(f32[3,3,27]{2,1,0:T(4,128)S(1)} %bitcast.15, bf16[288,864]{1,0:T(8,128)(2,1)S(1)} %matrix.1.packed, f32[2,3,2,32,128]{4,3,2,1,0:T(8,128)S(1)} %slice.15.forcing_ref, f32[2,3,2,32,128]{4,3,2,1,0:T(8,128)S(1)} %collective-permute-done.even_ref, ...), custom_call_target="tpu_custom_call" | custom-call | flops 764411904 | bytes 1586124 | tf_op jit(solution)/shard_map/own/pallas_call | solution.py:434
  7.0 7.0 %all-to-all-start = ((f32[8,192,128]{2,1,0:T(8,128)}), f32[8,192,128]{2,1,0:T(8,128)S(1)}, u32[]{:S(2)}, u32[]{:S(2)}) async-start(f32[8,192,128]{2,1,0:T(8,128)} %get-tuple-element.43), calls=%async_computation | async-start | bytes 1572864 | tf_op jit(solution)/shard_map/all_to_all | solution.py:454
  14.9 4.8 %collective-permute-start.2 = (f32[2,3,2,32,128]{4,3,2,1,0:T(8,128)S(1)}, f32[2,3,2,32,128]{4,3,2,1,0:T(8,128)S(1)}, u32[]{:S(2)}, u32[]{:S(2)}) collective-permute-start(f32[2,3,2,32,128]{4,3,2,1,0:T(8,128)S(1)} %slice.16.forcing_ref), channel_id=1, source_target_pairs={{0,8},{8,0},{16,24},{24,16},{1,9},{9,1},{17,25},{25,17},{2,10},{10... | collective-permute-start | bytes 589832 | tf_op jit(solution)/shard_map/ppermute | solution.py:450
  20.4 2.8 %collective-permute-start.6 = (f32[5,2,32,128]{3,2,1,0:T(8,128)S(1)}, f32[5,2,32,128]{3,2,1,0:T(8,128)S(1)}, u32[]{:S(2)}, u32[]{:S(2)}) collective-permute-start(f32[5,2,32,128]{3,2,1,0:T(8,128)S(1)} %copy-done.8), channel_id=1, source_target_pairs={{0,8},{8,0},{16,24},{24,16},{1,9},{9,1},{17,25},{25,17},{2,10},{10... | collective-permute-start | bytes 491528 | tf_op jit(solution)/shard_map/ppermute | solution.py:450
  27.2 3.0 %own.4 = (f32[2,3,2,32,128]{4,3,2,1,0:T(8,128)}, f32[8,128,128]{2,1,0:T(8,128)}) custom-call(f32[3,3,27]{2,1,0:T(4,128)S(1)} %bitcast.16, bf16[288,864]{1,0:T(8,128)(2,1)S(1)} %matrix.1.packed, f32[2,3,2,32,128]{4,3,2,1,0:T(8,128)S(1)} %slice.16.forcing_ref, f32[2,3,2,32,128]{4,3,2,1,0:T(8,128)S(1)} %collective-permute-done.2.even_ref, ...), custom_call_target="tpu_custom_call" | custom-call | flops 764411904 | bytes 1586124 | tf_op jit(solution)/shard_map/own/pallas_call | solution.py:434
  30.2 2.6 %all-to-all-done.image_ref = f32[8,192,128]{2,1,0:T(8,128)S(1)} async-done(((f32[8,192,128]{2,1,0:T(8,128)}), f32[8,192,128]{2,1,0:T(8,128)S(1)}, u32[]{:S(2)}, u32[]{:S(2)}) %all-to-all-start) | async-done | bytes 786464 | tf_op jit(solution)/shard_map/all_to_all | solution.py:454
  32.9 5.0 %all-to-all-start.1 = ((f32[8,128,128]{2,1,0:T(8,128)}), f32[8,128,128]{2,1,0:T(8,128)}, u32[]{:S(2)}, u32[]{:S(2)}) async-start(f32[8,128,128]{2,1,0:T(8,128)} %get-tuple-element.54), calls=%async_computation.1 | async-start | bytes 1048576 | tf_op jit(solution)/shard_map/all_to_all | solution.py:454
  39.1 1.6 %collective-permute-start.8 = (f32[1,112,128]{2,1,0:T(8,128)}, f32[1,112,128]{2,1,0:T(8,128)S(1)}, u32[]{:S(2)}, u32[]{:S(2)}) collective-permute-start(f32[1,112,128]{2,1,0:T(8,128)} %first.1.own_hbm), channel_id=1, source_target_pairs={{0,8},{8,0},{16,24},{24,16},{1,9},{9,1},{17,25},{25,17},{2,10},{10... | collective-permute-start | bytes 172040 | tf_op jit(solution)/shard_map/ppermute | solution.py:450
  41.4 4.3 %own.5 = (f32[5,3,2,32,128]{4,3,2,1,0:T(8,128)}, f32[8,200,128]{2,1,0:T(8,128)}) custom-call(f32[3,3,27]{2,1,0:T(4,128)S(1)} %bitcast.17, bf16[288,864]{1,0:T(8,128)(2,1)S(1)} %matrix.1.packed, f32[5,3,2,32,128]{4,3,2,1,0:T(8,128)S(1)} %slice.17.forcing_ref, f32[5,3,2,32,128]{4,3,2,1,0:T(8,128)S(1)} %collective-permute-done.4.even_ref, ...), custom_call_target="tpu_custom_call" | custom-call | flops 1911029760 | bytes 2470860 | tf_op jit(solution)/shard_map/own/pallas_call | solution.py:434
  46.4 4.9 %level.3 = (f32[8,24,128]{2,1,0:T(8,128)}, f32[5,88,128]{2,1,0:T(8,128)}) custom-call(s32[144]{0:T(256)} %slot_ref.13, f32[5,126]{1,0:T(8,128)} %bitcast.21, f32[3,3,27]{2,1,0:T(4,128)} %bitcast.10, f32[1,112,128]{2,1,0:T(8,128)} %first.1.own_hbm, f32[1,112,128]{2,1,0:T(8,128)} %copy-done.13, f32[1,112,128]{2,1,0:T(8,128)} %copy-done.14, ...), custom_call_target="tpu_custom_call" | custom-call | flops 637009920 | bytes 1454052 | tf_op jit(solution)/shard_map/level/pallas_call | solution.py:434
  51.3 2.4 %collective-permute-start.10 = (f32[5,88,128]{2,1,0:T(8,128)}, f32[5,88,128]{2,1,0:T(8,128)S(1)}, u32[]{:S(2)}, u32[]{:S(2)}) collective-permute-start(f32[5,88,128]{2,1,0:T(8,128)} %get-tuple-element.51.own_hbm), channel_id=1, source_target_pairs={{0,8},{8,0},{16,24},{24,16},{1,9},{9,1},{17,25},{25,17},{2,10},{10... | collective-permute-start | bytes 675848 | tf_op jit(solution)/shard_map/ppermute | solution.py:450
  55.0 5.9 %all-to-all-start.2 = ((f32[8,200,128]{2,1,0:T(8,128)}), f32[8,200,128]{2,1,0:T(8,128)}, u32[]{:S(2)}, u32[]{:S(2)}) async-start(f32[8,200,128]{2,1,0:T(8,128)} %get-tuple-element.57), calls=%async_computation.2 | async-start | bytes 1638400 | tf_op jit(solution)/shard_map/all_to_all | solution.py:454
  61.5 6.4 %level.4 = (f32[24,24,128]{2,1,0:T(8,128)}, f32[15,64,128]{2,1,0:T(8,128)}) custom-call(s32[144]{0:T(256)} %slot_ref.13, f32[5,126]{1,0:T(8,128)} %bitcast.22, f32[3,3,27]{2,1,0:T(4,128)} %bitcast.11, f32[5,88,128]{2,1,0:T(8,128)} %get-tuple-element.51.own_hbm, f32[5,88,128]{2,1,0:T(8,128)} %copy-done.11, f32[5,88,128]{2,1,0:T(8,128)} %copy-done.12, ...), custom_call_target="tpu_custom_call" | custom-call | flops 42998169600 | bytes 1794020 | tf_op jit(solution)/shard_map/level/pallas_call | solution.py:434
  70.6 12.6 %all-to-all-done.2 = f32[8,200,128]{2,1,0:T(8,128)} async-done(((f32[8,200,128]{2,1,0:T(8,128)}), f32[8,200,128]{2,1,0:T(8,128)}, u32[]{:S(2)}, u32[]{:S(2)}) %all-to-all-start.2) | async-done | bytes 819232 | tf_op jit(solution)/shard_map/all_to_all | solution.py:454
  83.2 8.6 %level.5 = (f32[64,24,128]{2,1,0:T(8,128)}, f32[35,40,128]{2,1,0:T(8,128)}, f32[9,72,128]{2,1,0:T(8,128)}, f32[9,72,128]{2,1,0:T(8,128)}) custom-call(s32[144]{0:T(256)} %slot_ref.13, f32[5,126]{1,0:T(8,128)} %bitcast.23, f32[3,3,27]{2,1,0:T(4,128)} %bitcast.12, f32[15,64,128]{2,1,0:T(8,128)} %get-tuple-element.56.own_hbm, ...), custom_call_target="tpu_custom_call" | custom-call | flops 41803776000 | bytes 3084260 | tf_op jit(solution)/shard_map/level/pallas_call | solution.py:434
  91.7 4.2 %all-to-all-start.3 = ((f32[8,192,128]{2,1,0:T(8,128)}), f32[8,192,128]{2,1,0:T(8,128)}, u32[]{:S(2)}, u32[]{:S(2)}) async-start(f32[8,192,128]{2,1,0:T(8,128)} %bitcast.20), calls=%async_computation.3 | async-start | bytes 1572864 | tf_op jit(solution)/shard_map/all_to_all | solution.py:454
  96.7 2.0 %select_bitcast_fusion = (f32[9,3,32,128]{3,2,1,0:T(8,128)S(1)}, f32[9,3,32,128]{3,2,1,0:T(8,128)}) fusion(pred[]{:T(512)S(6)} %eq.5, f32[18,3,2,32,128]{4,3,2,1,0:T(8,128)} %forcing_ref), kind=kLoop, calls=%fused_computation | loop fusion | flops 221184 | bytes 1769473 | tf_op jit(solution)/shard_map/jit(_where)/select_n | solution.py:507
  99.7 6.9 %level_last.1 = f32[72,24,128]{2,1,0:T(8,128)} custom-call(s32[144]{0:T(256)} %slot_ref.13, f32[5,126]{1,0:T(8,128)} %bitcast.24, f32[3,3,27]{2,1,0:T(4,128)} %bitcast.13, f32[35,40,128]{2,1,0:T(8,128)} %get-tuple-element.63.own_hbm, f32[9,72,128]{2,1,0:T(8,128)} %copy-done.6, f32[9,72,128]{2,1,0:T(8,128)} %copy-done.7, f32[5,2,32,128]{3,2,1,0:T(8,128)} %fields_hbm.3, ...), custom_call_target="tpu_custom_call" | custom-call | flops 557383680 | bytes 1875940 | tf_op jit(solution)/shard_map/level_last/pallas_call | solution.py:434
  106.5 9.9 %all-to-all-done.3.refs_4_ = f32[8,192,128]{2,1,0:T(8,128)} async-done(((f32[8,192,128]{2,1,0:T(8,128)}), f32[8,192,128]{2,1,0:T(8,128)}, u32[]{:S(2)}, u32[]{:S(2)}) %all-to-all-start.3) | async-done | bytes 786464 | tf_op jit(solution)/shard_map/all_to_all | solution.py:454
  116.5 4.2 %all-to-all-start.4 = ((f32[8,216,128]{2,1,0:T(8,128)}), f32[8,216,128]{2,1,0:T(8,128)}, u32[]{:S(2)}, u32[]{:S(2)}) async-start(f32[8,216,128]{2,1,0:T(8,128)} %bitcast.19), calls=%async_computation.4 | async-start | bytes 1769472 | tf_op jit(solution)/shard_map/all_to_all | solution.py:454
  122.8 3.3 %own_last.1.refs_3_ = f32[9,3,2,32,128]{4,3,2,1,0:T(8,128)} custom-call(f32[3,3,27]{2,1,0:T(4,128)S(1)} %bitcast.18, bf16[288,864]{1,0:T(8,128)(2,1)S(1)} %matrix.1.packed, f32[18,3,2,32,128]{4,3,2,1,0:T(8,128)S(1)} %copy-done.1, f32[9,3,32,128]{3,2,1,0:T(8,128)S(1)} %collective-permute-done.16.even_ref, f32[9,3,32,128]{3,2,1,0:T(8,128)S(1)} %collective-permute-done.17.odd_ref), custom_call_target="tpu_custom_call" | custom-call | flops 1146617856 | bytes 3650508 | tf_op jit(solution)/shard_map/own_last/pallas_call | solution.py:434
  126.1 3.1 %assemble.1.partial_ref = f32[18,3,2,32,128]{4,3,2,1,0:T(8,128)} custom-call(s32[144]{0:T(256)} %slot_ref.13, f32[2,3,2,32,128]{4,3,2,1,0:T(8,128)} %get-tuple-element.38.refs_0_, f32[2,3,2,32,128]{4,3,2,1,0:T(8,128)} %get-tuple-element.41.refs_1_, f32[5,3,2,32,128]{4,3,2,1,0:T(8,128)} %get-tuple-element.42.refs_2_, f32[9,3,2,32,128]{4,3,2,1,0:T(8,128)} %own_last.1.refs_3_, ...), custom_call_target="tpu_custom_call" | custom-call | bytes 2556480 | tf_op jit(solution)/shard_map/assemble/pallas_call | solution.py:434
  129.3 13.6 %all-to-all-done.4.links_hbm = f32[8,216,128]{2,1,0:T(8,128)} async-done(((f32[8,216,128]{2,1,0:T(8,128)}), f32[8,216,128]{2,1,0:T(8,128)}, u32[]{:S(2)}, u32[]{:S(2)}) %all-to-all-start.4) | async-done | bytes 884768 | tf_op jit(solution)/shard_map/all_to_all | solution.py:454
  142.9 2.9 %finish.1 = f32[18,3,2,32,128]{4,3,2,1,0:T(8,128)} custom-call(s32[144]{0:T(256)} %slot_ref.13, f32[18,3,2,32,128]{4,3,2,1,0:T(8,128)} %assemble.1.partial_ref, f32[8,216,128]{2,1,0:T(8,128)} %all-to-all-done.4.links_hbm), custom_call_target="tpu_custom_call", output_to_operand_aliasing={{}: (1, {})} | custom-call | tf_op jit(solution)/shard_map/finish/pallas_call | solution.py:597
  (68 shorter events, 20.4 us)
Async XLA Ops:
  0.9 2.9 %collective-permute-start = (f32[2,3,2,32,128]{4,3,2,1,0:T(8,128)S(1)}, f32[2,3,2,32,128]{4,3,2,1,0:T(8,128)S(1)}, u32[]{:S(2)}, u32[]{:S(2)}) collective-permute-start(f32[2,3,2,32,128]{4,3,2,1,0:T(8,128)S(1)} %slice.15.forcing_ref), channel_id=1, source_target_pairs={{0,8},{8,0},{16,24},{24,16},{1,9},{9,1},{17,25},{25,17},{2,10},{10... | collective-permute-start | bytes 589832 | tf_op jit(solution)/shard_map/ppermute | solution.py:450
  1.5 2.4 %collective-permute-start.1 = (f32[2,3,2,32,128]{4,3,2,1,0:T(8,128)S(1)}, f32[2,3,2,32,128]{4,3,2,1,0:T(8,128)S(1)}, u32[]{:S(2)}, u32[]{:S(2)}) collective-permute-start(f32[2,3,2,32,128]{4,3,2,1,0:T(8,128)S(1)} %slice.15.forcing_ref), channel_id=1, source_target_pairs={{8,16},{16,8},{9,17},{17,9},{10,18},{18,10},{11,19},{19,11},{12,20... | collective-permute-start | bytes 589832 | tf_op jit(solution)/shard_map/ppermute | solution.py:450
  7.0 25.9 %all-to-all-start = ((f32[8,192,128]{2,1,0:T(8,128)}), f32[8,192,128]{2,1,0:T(8,128)S(1)}, u32[]{:S(2)}, u32[]{:S(2)}) async-start(f32[8,192,128]{2,1,0:T(8,128)} %get-tuple-element.43), calls=%async_computation | async-start | bytes 1572864 | tf_op jit(solution)/shard_map/all_to_all | solution.py:454
  14.9 11.7 %collective-permute-start.2 = (f32[2,3,2,32,128]{4,3,2,1,0:T(8,128)S(1)}, f32[2,3,2,32,128]{4,3,2,1,0:T(8,128)S(1)}, u32[]{:S(2)}, u32[]{:S(2)}) collective-permute-start(f32[2,3,2,32,128]{4,3,2,1,0:T(8,128)S(1)} %slice.16.forcing_ref), channel_id=1, source_target_pairs={{0,8},{8,0},{16,24},{24,16},{1,9},{9,1},{17,25},{25,17},{2,10},{10... | collective-permute-start | bytes 589832 | tf_op jit(solution)/shard_map/ppermute | solution.py:450
  19.7 7.5 %collective-permute-start.3 = (f32[2,3,2,32,128]{4,3,2,1,0:T(8,128)S(1)}, f32[2,3,2,32,128]{4,3,2,1,0:T(8,128)S(1)}, u32[]{:S(2)}, u32[]{:S(2)}) collective-permute-start(f32[2,3,2,32,128]{4,3,2,1,0:T(8,128)S(1)} %slice.16.forcing_ref), channel_id=1, source_target_pairs={{8,16},{16,8},{9,17},{17,9},{10,18},{18,10},{11,19},{19,11},{12,20... | collective-permute-start | bytes 589832 | tf_op jit(solution)/shard_map/ppermute | solution.py:450
  20.4 9.9 %collective-permute-start.6 = (f32[5,2,32,128]{3,2,1,0:T(8,128)S(1)}, f32[5,2,32,128]{3,2,1,0:T(8,128)S(1)}, u32[]{:S(2)}, u32[]{:S(2)}) collective-permute-start(f32[5,2,32,128]{3,2,1,0:T(8,128)S(1)} %copy-done.8), channel_id=1, source_target_pairs={{0,8},{8,0},{16,24},{24,16},{1,9},{9,1},{17,25},{25,17},{2,10},{10... | collective-permute-start | bytes 491528 | tf_op jit(solution)/shard_map/ppermute | solution.py:450
  23.1 7.1 %collective-permute-start.7 = (f32[5,2,32,128]{3,2,1,0:T(8,128)S(1)}, f32[5,2,32,128]{3,2,1,0:T(8,128)S(1)}, u32[]{:S(2)}, u32[]{:S(2)}) collective-permute-start(f32[5,2,32,128]{3,2,1,0:T(8,128)S(1)} %copy-done.8), channel_id=1, source_target_pairs={{8,16},{16,8},{9,17},{17,9},{10,18},{18,10},{11,19},{19,11},{12,20... | collective-permute-start | bytes 491528 | tf_op jit(solution)/shard_map/ppermute | solution.py:450
  24.9 16.5 %collective-permute-start.4 = (f32[5,3,2,32,128]{4,3,2,1,0:T(8,128)S(1)}, f32[5,3,2,32,128]{4,3,2,1,0:T(8,128)S(1)}, u32[]{:S(2)}, u32[]{:S(2)}) collective-permute-start(f32[5,3,2,32,128]{4,3,2,1,0:T(8,128)S(1)} %slice.17.forcing_ref), channel_id=1, source_target_pairs={{0,8},{8,0},{16,24},{24,16},{1,9},{9,1},{17,25},{25,17},{2,10},{10... | collective-permute-start | bytes 1474568 | tf_op jit(solution)/shard_map/ppermute | solution.py:450
  26.5 14.9 %collective-permute-start.5 = (f32[5,3,2,32,128]{4,3,2,1,0:T(8,128)S(1)}, f32[5,3,2,32,128]{4,3,2,1,0:T(8,128)S(1)}, u32[]{:S(2)}, u32[]{:S(2)}) collective-permute-start(f32[5,3,2,32,128]{4,3,2,1,0:T(8,128)S(1)} %slice.17.forcing_ref), channel_id=1, source_target_pairs={{8,16},{16,8},{9,17},{17,9},{10,18},{18,10},{11,19},{19,11},{12,20... | collective-permute-start | bytes 1474568 | tf_op jit(solution)/shard_map/ppermute | solution.py:450
  32.9 22.1 %all-to-all-start.1 = ((f32[8,128,128]{2,1,0:T(8,128)}), f32[8,128,128]{2,1,0:T(8,128)}, u32[]{:S(2)}, u32[]{:S(2)}) async-start(f32[8,128,128]{2,1,0:T(8,128)} %get-tuple-element.54), calls=%async_computation.1 | async-start | bytes 1048576 | tf_op jit(solution)/shard_map/all_to_all | solution.py:454
  39.1 6.6 %collective-permute-start.8 = (f32[1,112,128]{2,1,0:T(8,128)}, f32[1,112,128]{2,1,0:T(8,128)S(1)}, u32[]{:S(2)}, u32[]{:S(2)}) collective-permute-start(f32[1,112,128]{2,1,0:T(8,128)} %first.1.own_hbm), channel_id=1, source_target_pairs={{0,8},{8,0},{16,24},{24,16},{1,9},{9,1},{17,25},{25,17},{2,10},{10... | collective-permute-start | bytes 172040 | tf_op jit(solution)/shard_map/ppermute | solution.py:450
  40.7 5.0 %collective-permute-start.9 = (f32[1,112,128]{2,1,0:T(8,128)}, f32[1,112,128]{2,1,0:T(8,128)S(1)}, u32[]{:S(2)}, u32[]{:S(2)}) collective-permute-start(f32[1,112,128]{2,1,0:T(8,128)} %first.1.own_hbm), channel_id=1, source_target_pairs={{8,16},{16,8},{9,17},{17,9},{10,18},{18,10},{11,19},{19,11},{12,20... | collective-permute-start | bytes 172040 | tf_op jit(solution)/shard_map/ppermute | solution.py:450
  51.3 3.7 %collective-permute-start.10 = (f32[5,88,128]{2,1,0:T(8,128)}, f32[5,88,128]{2,1,0:T(8,128)S(1)}, u32[]{:S(2)}, u32[]{:S(2)}) collective-permute-start(f32[5,88,128]{2,1,0:T(8,128)} %get-tuple-element.51.own_hbm), channel_id=1, source_target_pairs={{0,8},{8,0},{16,24},{24,16},{1,9},{9,1},{17,25},{25,17},{2,10},{10... | collective-permute-start | bytes 675848 | tf_op jit(solution)/shard_map/ppermute | solution.py:450
  53.6 7.2 %collective-permute-start.11 = (f32[5,88,128]{2,1,0:T(8,128)}, f32[5,88,128]{2,1,0:T(8,128)S(1)}, u32[]{:S(2)}, u32[]{:S(2)}) collective-permute-start(f32[5,88,128]{2,1,0:T(8,128)} %get-tuple-element.51.own_hbm), channel_id=1, source_target_pairs={{8,16},{16,8},{9,17},{17,9},{10,18},{18,10},{11,19},{19,11},{12,20... | collective-permute-start | bytes 675848 | tf_op jit(solution)/shard_map/ppermute | solution.py:450
  55.0 28.2 %all-to-all-start.2 = ((f32[8,200,128]{2,1,0:T(8,128)}), f32[8,200,128]{2,1,0:T(8,128)}, u32[]{:S(2)}, u32[]{:S(2)}) async-start(f32[8,200,128]{2,1,0:T(8,128)} %get-tuple-element.57), calls=%async_computation.2 | async-start | bytes 1638400 | tf_op jit(solution)/shard_map/all_to_all | solution.py:454
  67.9 2.7 %collective-permute-start.12 = (f32[15,64,128]{2,1,0:T(8,128)}, f32[15,64,128]{2,1,0:T(8,128)}, u32[]{:S(2)}, u32[]{:S(2)}) collective-permute-start(f32[15,64,128]{2,1,0:T(8,128)} %get-tuple-element.56.own_hbm), channel_id=1, source_target_pairs={{0,8},{8,0},{16,24},{24,16},{1,9},{9,1},{17,25},{25,17},{2,10},{10... | collective-permute-start | bytes 1474568 | tf_op jit(solution)/shard_map/ppermute | solution.py:450
  68.8 1.8 %collective-permute-start.13 = (f32[15,64,128]{2,1,0:T(8,128)}, f32[15,64,128]{2,1,0:T(8,128)}, u32[]{:S(2)}, u32[]{:S(2)}) collective-permute-start(f32[15,64,128]{2,1,0:T(8,128)} %get-tuple-element.56.own_hbm), channel_id=1, source_target_pairs={{8,16},{16,8},{9,17},{17,9},{10,18},{18,10},{11,19},{19,11},{12,20... | collective-permute-start | bytes 1474568 | tf_op jit(solution)/shard_map/ppermute | solution.py:450
  91.7 24.7 %all-to-all-start.3 = ((f32[8,192,128]{2,1,0:T(8,128)}), f32[8,192,128]{2,1,0:T(8,128)}, u32[]{:S(2)}, u32[]{:S(2)}) async-start(f32[8,192,128]{2,1,0:T(8,128)} %bitcast.20), calls=%async_computation.3 | async-start | bytes 1572864 | tf_op jit(solution)/shard_map/all_to_all | solution.py:454
  96.0 2.8 %collective-permute-start.14 = (f32[9,72,128]{2,1,0:T(8,128)}, f32[9,72,128]{2,1,0:T(8,128)S(1)}, u32[]{:S(2)}, u32[]{:S(2)}) collective-permute-start(f32[9,72,128]{2,1,0:T(8,128)} %get-tuple-element.59), channel_id=1, source_target_pairs={{0,8},{8,0},{16,24},{24,16},{1,9},{9,1},{17,25},{25,17},{2,10},{10... | collective-permute-start | bytes 995336 | tf_op jit(solution)/shard_map/ppermute | solution.py:450
  96.0 2.7 %collective-permute-start.15 = (f32[9,72,128]{2,1,0:T(8,128)}, f32[9,72,128]{2,1,0:T(8,128)S(1)}, u32[]{:S(2)}, u32[]{:S(2)}) collective-permute-start(f32[9,72,128]{2,1,0:T(8,128)} %get-tuple-element.60), channel_id=1, source_target_pairs={{8,16},{16,8},{9,17},{17,9},{10,18},{18,10},{11,19},{19,11},{12,20... | collective-permute-start | bytes 995336 | tf_op jit(solution)/shard_map/ppermute | solution.py:450
  99.7 23.1 %copy-start.4 = (f32[27,3,3]{0,2,1:T(4,128)S(1)}, f32[27,3,3]{0,2,1:T(4,128)}, u32[]{:S(2)}) copy-start(f32[27,3,3]{0,2,1:T(4,128)} %param.6) | copy-start | bytes 2920
  116.5 26.4 %all-to-all-start.4 = ((f32[8,216,128]{2,1,0:T(8,128)}), f32[8,216,128]{2,1,0:T(8,128)}, u32[]{:S(2)}, u32[]{:S(2)}) async-start(f32[8,216,128]{2,1,0:T(8,128)} %bitcast.19), calls=%async_computation.4 | async-start | bytes 1769472 | tf_op jit(solution)/shard_map/all_to_all | solution.py:454
  120.7 2.1 %collective-permute-start.16 = (f32[9,3,32,128]{3,2,1,0:T(8,128)}, f32[9,3,32,128]{3,2,1,0:T(8,128)S(1)}, u32[]{:S(2)}, u32[]{:S(2)}) collective-permute-start(f32[9,3,32,128]{3,2,1,0:T(8,128)} %get-tuple-element.61), channel_id=1, source_target_pairs={{0,8},{8,0},{16,24},{24,16},{1,9},{9,1},{17,25},{25,17},{2,10},{10... | collective-permute-start | bytes 1327112 | tf_op jit(solution)/shard_map/ppermute | solution.py:450
  120.8 2.0 %collective-permute-start.17 = (f32[9,3,32,128]{3,2,1,0:T(8,128)S(1)}, f32[9,3,32,128]{3,2,1,0:T(8,128)S(1)}, u32[]{:S(2)}, u32[]{:S(2)}) collective-permute-start(f32[9,3,32,128]{3,2,1,0:T(8,128)S(1)} %get-tuple-element.62), channel_id=1, source_target_pairs={{8,16},{16,8},{9,17},{17,9},{10,18},{18,10},{11,19},{19,11},{12,20... | collective-permute-start | bytes 1327112 | tf_op jit(solution)/shard_map/ppermute | solution.py:450
  (14 other events, 120.0 us)
